TPU v7x, 256 devices: a whole 4x4x8 slice. The times are simulated.
256 devices in a mesh: ctx: 16 (over z_lo, x), tp: 16 (over z_hi, y, core).
Axes of the slice: x: 4, y: 4, z: 8 (z_hi: 2, z_lo: 4; z = z_hi * 4 + z_lo), core: 2. Of those that a mesh axis runs over, the one named last changes fastest.
Arguments:
- hidden_in: bfloat16 [4096, 4096], P('tp', 'ctx'), may hold values from -24 to 24
- norm_gain: float32 [4096], replicated, may hold values from 0.1 to 1.9
- in_weight: bfloat16 [3, 4096, 4096], P(None, 'tp'), may hold values from -0.125 to 0.125
- filters: float32 [256, 128], P('tp'), may hold values from -0.5 to 0.5
- out_weight: bfloat16 [4096, 4096], P('tp'), may hold values from -0.125 to 0.125
- out_grads: bfloat16 [4096, 4096], P('tp', 'ctx'), may hold values from -6 to 6
Outputs:
- layer_out: bfloat16 [4096, 4096], P('tp', 'ctx')
- hidden_grads: bfloat16 [4096, 4096], P('tp', 'ctx')
- in_weight_grads: float32 [3, 4096, 4096], P(None, 'tp', 'ctx')
- filter_grads: float32 [256, 128], P(('tp', 'ctx'))
- out_weight_grads: float32 [4096, 4096], P('tp', 'ctx')
All inputs are finite; a program needn't handle non-finite values.
Results may differ from a plain program's by a relative error of at most 0.03.
Values may be sent and summed in bfloat16 or wider, within the bound.
No kernel may reach another device: no remote copies, remote signals or barrier semaphores. Data moves between devices by JAX's collectives and lax.ppermute only.
A program may use at most 128 MiB of HBM per device.

v0:
```python
import functools

import jax
import jax.numpy as jnp
from jax import lax
from jax.experimental import pallas as pl
from jax.experimental.pallas import tpu as pltpu
from jax.sharding import Mesh, PartitionSpec as P

GS = 16
EPS = 1e-06
F32 = jnp.float32
BF = jnp.bfloat16
VM = pl.BlockSpec(memory_space=pltpu.VMEM)
SM = pl.BlockSpec(memory_space=pltpu.SMEM)
SWAP = [(0, 1), (1, 0)]


def shape(*dims, dtype=BF):
    return jax.ShapeDtypeStruct(dims, dtype)


def call(body, outs, *args, scratch=(), flops=0, moved=0, smem=True, name=None, limit=10):
    specs = [SM if smem and i == 0 else VM for i in range(len(args))]
    multi = isinstance(outs, (list, tuple))
    return pl.pallas_call(
        body,
        out_shape=list(outs) if multi else outs,
        in_specs=specs,
        out_specs=[VM] * len(outs) if multi else VM,
        scratch_shapes=list(scratch),
        compiler_params=pltpu.CompilerParams(vmem_limit_bytes=limit * 2**20),
        cost_estimate=pl.CostEstimate(flops=flops, bytes_accessed=moved, transcendentals=0),
        name=name,
    )(*args)


def ring(size, step):
    return [(i, (i + step) % size) for i in range(size)]


def after(value, *earlier):
    return lax.optimization_barrier((value, *earlier))[0]


def dot_nt(a, b):
    return lax.dot_general(a, b, (((1,), (1,)), ((), ())), preferred_element_type=F32)


def dot_tn(a, b):
    return lax.dot_general(a, b, (((0,), (0,)), ((), ())), preferred_element_type=F32)


def up(x):
    return x.astype(F32)


def toeplitz_body(filt_ref, fwd_ref, back_ref):
    n = filt_ref.shape[1]
    row = lax.broadcasted_iota(jnp.int32, (n, n), 0)
    col = lax.broadcasted_iota(jnp.int32, (n, n), 1)

    def group(g, _):
        mat = jnp.broadcast_to(filt_ref[pl.ds(g, 1), :], (n, n))
        step = 1
        while step < n:
            mat = jnp.where((row & step) != 0, pltpu.roll(mat, step, 1), mat)
            step *= 2
        same = jnp.where(col >= row, mat, 0.0).astype(BF)
        prev = jnp.where(col < row, mat, 0.0).astype(BF)
        fwd_ref[g, :n, :] = prev
        fwd_ref[g, n:, :] = same
        back_ref[g, :, :n] = same
        back_ref[g, :, n:] = prev
        return 0

    lax.fori_loop(0, filt_ref.shape[0], group, 0, unroll=8)


def piece_slots(ids):
    zh, y, c = ids[0], ids[1], ids[2]
    return [
        [z * 8 + lax.rem(y + 4 - s, 4) * 2 + k for s in range(4)]
        for z, k in ((zh, c), (1 - zh, c), (zh, 1 - c), (1 - zh, 1 - c))
    ]


def send_rows(ids, full_ref, send_refs):
    c, x = ids[2], ids[3]
    for s, send_ref in enumerate(send_refs):
        for k in range(2):
            send_ref[k] = full_ref[(2 * c + k) * 4 + lax.rem(x + s, 4)]


def project_body(
    ids, gain_ref, w_ref, a_ref, b_ref, c_ref, d_ref,
    proj_ref, mixed_in_ref, tail_ref, rms_ref, s0, s1, s2, s3, full_ref,
):
    parts = (a_ref, b_ref, c_ref, d_ref)
    total = jnp.zeros((1, 256), F32)
    for part in parts:
        for s in range(4):
            h = up(part[s])
            total = total + jnp.sum(h * h, axis=0, keepdims=True)
    rms = lax.rsqrt(total * (1.0 / 4096.0) + EPS)
    rms_ref[...] = rms
    gains = jnp.concatenate([gain_ref[...], jnp.zeros((112, 256), F32)], axis=0).T
    lane = lax.broadcasted_iota(jnp.int32, (256, 128), 1)
    for part, slots in zip(parts, piece_slots(ids)):
        for s in range(4):
            gain = jnp.sum(jnp.where(lane == slots[s], gains, 0.0), axis=1, keepdims=True)
            full_ref[slots[s]] = (up(part[s]) * rms * gain).astype(BF)

    normed = full_ref[...].reshape(4096, 256)
    for p in range(3):
        proj_ref[p] = jnp.dot(w_ref[p], normed, preferred_element_type=F32).astype(BF)
    mixed = (up(proj_ref[1]) * up(proj_ref[2])).astype(BF)
    mixed_in_ref[...] = mixed
    tail_ref[...] = mixed[:, 128:]
    send_rows(ids, full_ref, (s0, s1, s2, s3))


def conv_body(x_ref, halo_ref, fwd_ref, proj_ref, conv_ref, mixed_ref):
    def group(g, _):
        rows = pl.ds(pl.multiple_of(g * GS, GS), GS)
        first = jnp.concatenate([halo_ref[rows, :], x_ref[rows, :128]], axis=1)
        both = jnp.concatenate([first, x_ref[rows, :]], axis=0)
        out = jnp.dot(both, fwd_ref[g], preferred_element_type=F32).astype(BF)
        conv = jnp.concatenate([out[:GS], out[GS:]], axis=1)
        conv_ref[rows, :] = conv
        mixed_ref[rows, :] = (up(proj_ref[0, rows, :]) * up(conv)).astype(BF)
        return 0

    lax.fori_loop(0, 16, group, 0, unroll=4)


def conv_back_body(
    g_ref, halo_ref, back_ref, proj_ref, conv_ref, mg_ref, pg_ref, all_ref, part_ref, mig_ref
):
    def group(g, _):
        rows = pl.ds(pl.multiple_of(g * GS, GS), GS)
        second = jnp.concatenate([g_ref[rows, 128:], halo_ref[rows, :]], axis=1)
        both = jnp.concatenate([g_ref[rows, :], second], axis=0)
        out = dot_nt(both, back_ref[g]).astype(BF)
        mig_ref[rows, :] = jnp.concatenate([out[:GS], out[GS:]], axis=1)
        return 0

    lax.fori_loop(0, 16, group, 0, unroll=4)
    mig = up(mig_ref[...])
    key, value = up(proj_ref[1]), up(proj_ref[2])
    qg = (up(mg_ref[...]) * up(conv_ref[...])).astype(BF)
    kg = (mig * value).astype(BF)
    vg = (mig * key).astype(BF)
    pg_ref[0] = qg
    pg_ref[1] = kg
    pg_ref[2] = vg
    for dest in range(4):
        all_ref[dest] = pg_ref[...]
    terms = up(qg) * up(proj_ref[0]) + up(kg) * key + up(vg) * value
    part_ref[...] = jnp.sum(terms, axis=0, keepdims=True)


def filter_grad_body(x_ref, halo_ref, g_ref, out_ref):
    n = 128
    row = lax.broadcasted_iota(jnp.int32, (n, n), 0)
    col = lax.broadcasted_iota(jnp.int32, (n, n), 1)

    def group(g, _):
        rows = pl.ds(pl.multiple_of(g * GS, GS), GS)
        first, second = x_ref[rows, :n], x_ref[rows, n:]
        grads = jnp.concatenate([g_ref[rows, :n], g_ref[rows, n:]], axis=0)
        here = jnp.concatenate([first, second], axis=0)
        before = jnp.concatenate([halo_ref[rows, :], first], axis=0)
        mat = jnp.where(col >= row, dot_tn(here, grads), dot_tn(before, grads))
        step = 1
        while step < n:
            mat = jnp.where((row & step) != 0, pltpu.roll(mat, n - step, 1), mat)
            step *= 2
        out_ref[pl.ds(g, 1), :] = jnp.sum(mat, axis=0, keepdims=True)
        return 0

    lax.fori_loop(0, 16, group, 0, unroll=8)


def rs_first_body(ids, w_ref, g_ref, out_ref):
    zh, y, c = ids[0], ids[1], ids[2]
    grads = [g_ref[p].T for p in range(g_ref.shape[0])]
    for zr, z in enumerate((zh, 1 - zh)):
        for s in range(4):
            slot = z * 8 + lax.rem(y + s, 4) * 2 + (1 - c)
            cols = pl.ds(pl.multiple_of(slot * 256, 256), 256)
            acc = jnp.dot(grads[0], w_ref[0, :, cols], preferred_element_type=F32)
            for p in range(1, len(grads)):
                acc += jnp.dot(grads[p], w_ref[p, :, cols], preferred_element_type=F32)
            out_ref[zr, s] = acc.astype(BF)


def split_sum(value):
    high = up(value.astype(BF))
    row = lax.broadcasted_iota(jnp.int32, (16, value.shape[1]), 0)
    return jnp.where(row == 0, high, jnp.where(row == 1, value - high, 0.0)).astype(BF)


def rs_second_body(ids, w_ref, g_ref, recv_ref, rider_ref, *out_refs):
    zh, y, c = ids[0], ids[1], ids[2]
    grads = [g_ref[p].T for p in range(g_ref.shape[0])]
    for s in (1, 3, 2, 0):
        for zr, z in ((1, 1 - zh), (0, zh)):
            slot = z * 8 + lax.rem(y + s, 4) * 2 + c
            cols = pl.ds(pl.multiple_of(slot * 256, 256), 256)
            acc = up(recv_ref[zr, s])
            for p in range(len(grads)):
                acc += jnp.dot(grads[p], w_ref[p, :, cols], preferred_element_type=F32)
            out_refs[s][zr * 256 : zr * 256 + 256, :] = acc.astype(BF)
        if rider_ref.shape[0] == 1:
            out_refs[s][512:, :] = split_sum(rider_ref[...])
        else:
            out_refs[s][512:, :] = rider_ref[...]


def combine_body(p0, p1, p2, p3, near_ref, far_ref, rider_ref):
    parts = (p0, p1, p2, p3)

    def total(rows):
        return up(p0[rows, :]) + up(p1[rows, :]) + up(p2[rows, :]) + up(p3[rows, :])

    near_ref[...] = total(slice(0, 256)).astype(BF)
    far_ref[:256, :] = total(slice(256, 512)).astype(BF)
    if rider_ref.shape[0] == 1:
        row = jnp.sum(total(slice(512, 528)), axis=0, keepdims=True)
        rider_ref[...] = row
        far_ref[256:, :] = split_sum(row)
    else:
        for s, part in enumerate(parts):
            rider_ref[s] = part[512:, :]


def swap_products(ids, weight, grads, name):
    planes = grads.shape[0]
    first = call(
        rs_first_body, shape(2, 4, 256, 256), ids, weight, grads,
        flops=2 * 2048 * 256 * 256 * planes, moved=planes * 2**20, name=name + "_a",
    )
    return lax.ppermute(first, "core", SWAP)


def reduce_scatter_tp(ids, weight, grads, recv, rider, name):
    planes = grads.shape[0]
    summed = rider.shape[0] == 1
    rows = 528 if summed else 768
    blocks = call(
        rs_second_body, [shape(rows, 256)] * 4, ids, weight, grads, recv, rider,
        flops=2 * 2048 * 256 * 256 * planes, moved=planes * 2**20, name=name + "_b",
    )
    parts = [blocks[0]] + [lax.ppermute(blocks[s], "y", ring(4, s)) for s in (1, 2, 3)]
    near, far, riders = call(
        combine_body,
        [
            shape(256, 256), shape(272 if summed else 256, 256),
            shape(1, 256, dtype=F32) if summed else shape(4, 256, 256),
        ],
        *parts, smem=False, name=name + "_sum",
    )
    return blocks[0], near, lax.ppermute(far, "zh", SWAP), riders


def gather_tp(block):
    near = [block] + [lax.ppermute(block, "y", ring(4, s)) for s in (1, 2, 3)]
    other = lax.ppermute(block, "zh", SWAP)
    far = [other] + [lax.ppermute(other, "y", ring(4, s)) for s in (1, 2, 3)]
    near = jnp.stack(near)
    far = jnp.stack(far)
    return near, far, lax.ppermute(near, "core", SWAP), lax.ppermute(far, "core", SWAP)


def mixed_grad_body(near_ref, far_ref, proj_ref, mg_ref, cg_ref, head_ref):
    grads = (up(near_ref[...]) + up(far_ref[...])).T.astype(BF)
    mg_ref[...] = grads
    cg = (up(grads) * up(proj_ref[0])).astype(BF)
    cg_ref[...] = cg
    head_ref[...] = cg[:, :128]


def hidden_grad_body(near_ref, far_ref, hid_ref, og_ref, gain_ref, rms_ref, mom_ref, out_ref):
    grads = (up(near_ref[...]) + up(far_ref[:256, :])).T
    rms = rms_ref[...]
    total = mom_ref[...] + jnp.sum(up(far_ref[256:, :]), axis=0, keepdims=True)
    moment = total / (rms * 4096.0)
    out = up(og_ref[...]) + rms * (
        gain_ref[...] * grads - up(hid_ref[...]) * (rms * rms * moment)
    )
    out_ref[...] = out.astype(BF)


def out_body(ids, w_ref, hid_ref, og_ref, a_ref, b_ref, c_ref, d_ref, out_ref, send_ref, full_ref):
    for part, slots in zip((a_ref, b_ref, c_ref, d_ref), piece_slots(ids)):
        for s in range(4):
            full_ref[slots[s]] = part[s]
    mixed = full_ref[...].reshape(4096, 256)
    acc = jnp.dot(w_ref[...], mixed, preferred_element_type=F32)
    out_ref[...] = (up(hid_ref[...]) + acc).astype(BF)
    for dest in range(4):
        for k in range(2):
            send_ref[dest, k] = full_ref[(2 * ids[2] + k) * 4 + dest]
        send_ref[dest, 2] = og_ref[...]


def weight_grad_body(relative, first, ids, mine_ref, other_ref, g_ref, out_ref):
    c, x = ids[2], ids[3]
    planes = out_ref.shape[1]
    for core, ref in ((c, mine_ref), (1 - c, other_ref)):
        for k in range(2):
            acc = None
            for s in range(4):
                at = lax.rem(x + 4 - s, 4) if relative else s
                left = g_ref[at, first : first + planes].reshape(planes * 256, 256)
                term = dot_nt(left, ref[s, k])
                acc = term if acc is None else acc + term
            out_ref[2 * core + k] = acc.astype(BF).reshape(planes, 256, 256)


def weight_grads(ids, mine, other, grads, relative, first, planes, name):
    return call(
        functools.partial(weight_grad_body, relative, first), shape(4, planes, 256, 256),
        ids, mine, other, grads,
        flops=2 * 1024 * 1024 * 256 * planes, moved=planes * 2**20, name=name,
    )


def per_device(hidden_in, norm_gain, in_weight, filters, out_weight, out_grads):
    zl, x, zh, y, c = (lax.axis_index(name) for name in ("zl", "x", "zh", "y", "core"))
    ids = jnp.stack([zh, y, c, x, zl]).astype(jnp.int32)
    gain = norm_gain.reshape(16, 256)
    tp = zh * 8 + y * 2 + c
    gain_rows = lax.dynamic_slice_in_dim(norm_gain, tp * 256, 256, 0).reshape(256, 1)

    near = jnp.stack([hidden_in] + [lax.ppermute(hidden_in, "y", ring(4, s)) for s in (1, 2, 3)])
    near_swap = lax.ppermute(near, "core", SWAP)
    other = lax.ppermute(hidden_in, "zh", SWAP)
    fwd, back = call(
        toeplitz_body, [shape(16, 256, 128), shape(16, 128, 256)], after(filters, near), smem=False, name="taps"
    )
    og = out_grads[None]
    swapped = swap_products(ids, out_weight[None], og, "mixed_grads")
    _, *mg_parts, far = reduce_scatter_tp(
        ids, out_weight[None], og, swapped, after(other, near), "mixed_grads"
    )
    gathered = near, far, near_swap, lax.ppermute(far, "core", SWAP)
    proj, mixed_in, tail, rms, *send = call(
        project_body,
        [
            shape(3, 256, 256), shape(256, 256), shape(256, 128), shape(1, 256, dtype=F32),
            *[shape(2, 256, 256)] * 4,
        ],
        after(ids, mg_parts[0]), gain, in_weight, *gathered,
        scratch=[pltpu.VMEM((16, 256, 256), BF)],
        flops=2 * 768 * 4096 * 256, moved=10 * 2**20, name="project",
    )
    halo = lax.ppermute(tail, ("zl", "x"), [(i, i + 1) for i in range(15)])
    mg, cg, head = call(
        mixed_grad_body, [shape(256, 256)] * 2 + [shape(256, 128)], *mg_parts, proj,
        smem=False, name="mixed_grad",
    )
    next_halo = lax.ppermute(head, ("zl", "x"), [(i + 1, i) for i in range(15)])
    conv, mixed = call(
        conv_body, [shape(256, 256)] * 2, mixed_in, after(halo, mg_parts[1]), fwd, proj, smem=False,
        flops=2 * 256 * 256 * 256, name="conv",
    )
    pg, pg_all, part = call(
        conv_back_body,
        [shape(3, 256, 256), shape(4, 3, 256, 256), shape(1, 256, dtype=F32)],
        cg, next_halo, back, proj, conv, mg, smem=False,
        scratch=[pltpu.VMEM((256, 256), BF)], flops=2 * 256 * 256 * 256, name="conv_back",
    )
    mixed_pieces = gather_tp(after(mixed, pg))
    send = [send[0]] + [after(block, pg) for block in send[1:]]
    normed_x = [send[0]] + [lax.ppermute(send[s], "x", ring(4, s)) for s in (1, 2, 3)]
    normed_x = jnp.stack([after(normed_x[0], pg, *mixed_pieces[:2])] + normed_x[1:])
    normed_other = lax.ppermute(normed_x, "core", SWAP)
    pg_x = lax.all_to_all(pg_all, "x", 0, 0, tiled=True)
    swapped = swap_products(ids, in_weight, after(pg, normed_x), "norm_grads")
    part = part + lax.ppermute(part, "core", SWAP)
    ng_block, *ng_parts = reduce_scatter_tp(
        ids, in_weight, pg, swapped, part, "norm_grads"
    )
    in_part = weight_grads(
        ids, normed_x, normed_other, after(pg_x, mixed_pieces[0], ng_block), True, 0, 3, "in_w"
    )
    in_weight_grads = lax.psum_scatter(in_part, "zl", scatter_dimension=0, tiled=False).astype(F32)

    layer_out, m_send = call(
        out_body, [shape(256, 256), shape(4, 3, 256, 256)],
        ids, after(out_weight, in_part), hidden_in, out_grads, *mixed_pieces,
        scratch=[pltpu.VMEM((16, 256, 256), BF)],
        flops=2 * 256 * 4096 * 256, moved=4 * 2**20, name="layer_out",
    )
    taps = call(
        filter_grad_body, shape(16, 128, dtype=F32), mixed_in, halo, after(cg, m_send),
        smem=False, flops=2 * 256 * 256 * 256, name="tap_grads",
    )
    taps = taps.reshape(4, 4, 128)
    pick = lambda s: lax.dynamic_index_in_dim(taps, lax.rem(x + s, 4), 1, False)
    taps = pick(0) + sum(lax.ppermute(pick(s), "x", ring(4, s)) for s in (1, 2, 3))
    mixed_x = lax.all_to_all(m_send, "x", 0, 0, tiled=True)
    mixed_other = lax.ppermute(after(mixed_x, taps, ng_parts[0]), "core", SWAP)
    out_part = weight_grads(ids, mixed_x, mixed_other, mixed_x, False, 2, 1, "out_w")
    out_recv = lax.all_to_all(out_part[:, 0], "zl", 0, 0, tiled=True)
    out_weight_grads = jnp.sum(up(out_recv), axis=0)

    hidden_grads = call(
        hidden_grad_body, shape(256, 256), *ng_parts[:2], hidden_in, out_grads, gain_rows, rms, ng_parts[2],
        smem=False, name="hidden_grads",
    )

    row = lambda s: lax.dynamic_index_in_dim(taps, lax.rem(zl + s, 4), 0, True)
    filter_grads = row(0) + sum(lax.ppermute(row(s), "zl", ring(4, s)) for s in (1, 2, 3))

    return layer_out, hidden_grads, in_weight_grads, filter_grads, out_weight_grads


def solution(mesh):
    fine = Mesh(mesh.devices.reshape(4, 4, 2, 4, 2), ("zl", "x", "zh", "y", "core"))
    tp, ctx = ("zh", "y", "core"), ("zl", "x")
    return jax.shard_map(
        per_device,
        mesh=fine,
        in_specs=(P(tp, ctx), P(), P(None, tp, None), P(tp, None), P(tp, None), P(tp, ctx)),
        out_specs=(P(tp, ctx), P(tp, ctx), P(None, tp, ctx), P(tp + ctx, None), P(tp, ctx)),
        check_vma=False,
    )
```

profile of v0, /device:TPU:1, one launch (start us, length us, event | category | flops | bytes accessed | tf_op | source)
XLA Modules:
  0.0 201.4 jit_solution(1733347217261370304)
XLA Ops:
  7.3 1.6 copy-done.2
  9.8 1.0 mixed_grads_a.1
  10.8 3.3 %collective-permute-start = (bf16[2,4,256,256]{3,2,1,0:T(8,128)(2,1)S(1)}, bf16[2,4,256,256]{3,2,1,0:T(8,128)(2,1)S(1)}, u32[]{:S(2)}, u32[]{:S(2)}) collective-permute-start(bf16[2,4,256,256]{3,2,1,0:T(8,128)(2,1)S(1)} %mixed_grads_a.1), channel_id=1, source_target_pairs={{0,1},{1,0},{2,3},{3,2},{4,5},{5,4},{6,7},{7,6},{8,9},{9,8},{10,11... | collective-permute-start | bytes 3145736 | tf_op jit(solution)/shard_map/ppermute | solution.py:244
  14.1 1.0 collective-permute-start.4
  15.6 1.2 collective-permute-start.3
  16.8 6.9 %collective-permute-start.1 = (bf16[256,256]{1,0:T(8,128)(2,1)S(1)}, bf16[256,256]{1,0:T(8,128)(2,1)S(1)}, u32[]{:S(2)}, u32[]{:S(2)}) collective-permute-start(bf16[256,256]{1,0:T(8,128)(2,1)S(1)} %copy-done.12), channel_id=1, source_target_pairs={{0,8},{8,0},{1,9},{9,1},{2,10},{10,2},{3,11},{11,3},{4,12},{12,4},... | collective-permute-start | bytes 393224 | tf_op jit(solution)/shard_map/ppermute | solution.py:339
  23.9 2.7 %collective-permute-done.1.rider_ref = bf16[256,256]{1,0:T(8,128)(2,1)S(1)} collective-permute-done((bf16[256,256]{1,0:T(8,128)(2,1)S(1)}, bf16[256,256]{1,0:T(8,128)(2,1)S(1)}, u32[]{:S(2)}, u32[]{:S(2)}) %collective-permute-start.1) | collective-permute-done | bytes 131104 | tf_op jit(solution)/shard_map/ppermute | solution.py:339
  26.6 1.0 mixed_grads_b.1
  27.6 1.7 collective-permute-start.5
  30.2 1.6 collective-permute-start.7
  31.8 2.2 %collective-permute-start.8 = (bf16[4,256,256]{2,1,0:T(8,128)(2,1)S(1)}, bf16[4,256,256]{2,1,0:T(8,128)(2,1)S(1)}, u32[]{:S(2)}, u32[]{:S(2)}) collective-permute-start(bf16[4,256,256]{2,1,0:T(8,128)(2,1)S(1)} %pad_maximum_fusion.1.a_ref), channel_id=1, source_target_pairs={{0,1},{1,0},{2,3},{3,2},{4,5},{5,4},{6,7},{7,6},{8,9},{9,8},{10,11... | collective-permute-start | bytes 1572872 | tf_op jit(solution)/shard_map/ppermute | solution.py:338
  34.0 3.9 %collective-permute-done.5.p1 = bf16[768,256]{1,0:T(8,128)(2,1)S(1)} collective-permute-done((bf16[768,256]{1,0:T(8,128)(2,1)S(1)}, bf16[768,256]{1,0:T(8,128)(2,1)S(1)}, u32[]{:S(2)}, u32[]{:S(2)}) %collective-permute-start.5) | collective-permute-done | bytes 393248 | tf_op jit(solution)/shard_map/ppermute | solution.py:255
  37.9 8.6 %collective-permute-done.6.p2 = bf16[768,256]{1,0:T(8,128)(2,1)S(1)} collective-permute-done((bf16[768,256]{1,0:T(8,128)(2,1)S(1)}, bf16[768,256]{1,0:T(8,128)(2,1)S(1)}, u32[]{:S(2)}, u32[]{:S(2)}) %collective-permute-start.6) | collective-permute-done | bytes 393248 | tf_op jit(solution)/shard_map/ppermute | solution.py:255
  46.5 1.4 collective-permute-done.7.p3
  48.1 1.6 collective-permute-start.9
  49.8 5.0 %collective-permute-start.10 = (bf16[256,256]{1,0:T(8,128)(2,1)S(1)}, bf16[256,256]{1,0:T(8,128)(2,1)S(1)}, u32[]{:S(2)}, u32[]{:S(2)}) collective-permute-start(bf16[256,256]{1,0:T(8,128)(2,1)S(1)} %get-tuple-element.62), channel_id=1, source_target_pairs={{0,8},{8,0},{1,9},{9,1},{2,10},{10,2},{3,11},{11,3},{4,12},{12,4},... | collective-permute-start | bytes 393224 | tf_op jit(solution)/shard_map/ppermute | solution.py:264
  54.7 2.8 %copy-done = bf16[3,256,4096]{2,1,0:T(8,128)(2,1)S(1)} copy-done((bf16[3,256,4096]{2,1,0:T(8,128)(2,1)S(1)}, bf16[3,256,4096]{2,1,0:T(8,128)(2,1)}, u32[]{:S(2)}) %copy-start) | copy-done | bytes 6291480
  57.5 3.1 %project.1 = (bf16[3,256,256]{2,1,0:T(8,128)(2,1)S(1)}, bf16[256,256]{1,0:T(8,128)(2,1)S(1)}, bf16[256,128]{1,0:T(8,128)(2,1)S(1)}, f32[1,256]{1,0:T(1,128)S(1)}...) custom-call(s32[5]{0:T(128)S(1)} %stack.83.ids, ...), custom_call_target="tpu_custom_call" | custom-call | flops 1610612736 | bytes 10485760 | tf_op jit(solution)/shard_map/project/pallas_call | solution.py:26
  60.6 3.1 %collective-permute-start.12 = (bf16[256,128]{1,0:T(8,128)(2,1)S(1)}, bf16[256,128]{1,0:T(8,128)(2,1)S(1)}, u32[]{:S(2)}, u32[]{:S(2)}) collective-permute-start(bf16[256,128]{1,0:T(8,128)(2,1)S(1)} %get-tuple-element.69), channel_id=1, source_target_pairs={{0,16},{16,32},{32,48},{48,64},{64,80},{80,96},{96,112},{112,128},... | collective-permute-start | bytes 196616 | tf_op jit(solution)/shard_map/ppermute | solution.py:359
  63.9 1.3 collective-permute-start.11
  65.2 1.1 taps.1
  67.1 1.9 collective-permute-done.11.halo_ref
  68.9 1.2 conv_back.1
  70.9 1.4 collective-permute-start.16
  72.4 1.4 collective-permute-start.13
  73.7 2.1 %collective-permute-start.14 = (bf16[256,256]{1,0:T(8,128)(2,1)S(1)}, bf16[256,256]{1,0:T(8,128)(2,1)S(1)}, u32[]{:S(2)}, u32[]{:S(2)}) collective-permute-start(bf16[256,256]{1,0:T(8,128)(2,1)S(1)} %get-tuple-element.76), channel_id=1, source_target_pairs={{0,4},{2,6},{4,0},{6,2},{1,5},{3,7},{5,1},{7,3},{8,12},{10,14},{12... | collective-permute-start | bytes 393224 | tf_op jit(solution)/shard_map/ppermute | solution.py:268
  76.5 2.2 %collective-permute-done.16 = bf16[256,256]{1,0:T(8,128)(2,1)S(1)} collective-permute-done((bf16[256,256]{1,0:T(8,128)(2,1)S(1)}, bf16[256,256]{1,0:T(8,128)(2,1)S(1)}, u32[]{:S(2)}, u32[]{:S(2)}) %collective-permute-start.16) | collective-permute-done | bytes 131104 | tf_op jit(solution)/shard_map/ppermute | solution.py:269
  78.7 1.4 collective-permute-start.17
  80.0 1.2 collective-permute-start.20
  81.3 4.3 %collective-permute-start.21 = (bf16[2,256,256]{2,1,0:T(8,128)(2,1)}, bf16[2,256,256]{2,1,0:T(8,128)(2,1)}, u32[]{:S(2)}, u32[]{:S(2)}) collective-permute-start(bf16[2,256,256]{2,1,0:T(8,128)(2,1)} %get-tuple-element.81), channel_id=1, source_target_pairs={{0,32},{16,48},{32,0},{48,16},{1,33},{17,49},{33,1},{49,17},{2,34}... | collective-permute-start | bytes 786440 | tf_op jit(solution)/shard_map/ppermute | solution.py:377
  85.5 2.2 %collective-permute-start.18 = (bf16[256,256]{1,0:T(8,128)(2,1)S(1)}, bf16[256,256]{1,0:T(8,128)(2,1)}, u32[]{:S(2)}, u32[]{:S(2)}) collective-permute-start(bf16[256,256]{1,0:T(8,128)(2,1)S(1)} %collective-permute-done.16), channel_id=1, source_target_pairs={{0,4},{2,6},{4,0},{6,2},{1,5},{3,7},{5,1},{7,3},{8,12},{10,14},{12... | collective-permute-start | bytes 393224 | tf_op jit(solution)/shard_map/ppermute | solution.py:270
  88.4 4.5 %all-to-all-start = ((bf16[4,3,256,256]{3,2,1,0:T(8,128)(2,1)}), bf16[4,3,256,256]{3,2,1,0:T(8,128)(2,1)}, u32[]{:S(2)}, u32[]{:S(2)}) async-start(bf16[4,3,256,256]{3,2,1,0:T(8,128)(2,1)} %copy-done.11), calls=%async_computation | async-start | bytes 3145728 | tf_op jit(solution)/shard_map/all_to_all | solution.py:380
  93.0 1.0 pad_maximum_fusion.2.a_ref
  94.0 1.2 pad_maximum_fusion.3.b_ref
  95.3 2.2 %pad_maximum_fusion.mine_ref = bf16[4,2,256,256]{3,2,1,0:T(8,128)(2,1)} fusion(bf16[1,2,256,256]{3,2,1,0:T(8,128)(2,1)} %bitcast.22, bf16[1,2,256,256]{3,2,1,0:T(8,128)(2,1)} %bitcast.21, bf16[1,2,256,256]{3,2,1,0:T(8,128)(2,1)} %bitcast.20, bf16[1,2,256,256]{3,2,1,0:T(8,128)(2,1)S(1)} %bitcast.40), kind=kLoop, calls=%fused_computation | loop fusion | flops 1572864 | bytes 2097152 | tf_op jit(solution)/shard_map/stack | solution.py:378
  97.5 2.8 %copy-done.1 = bf16[3,256,4096]{2,1,0:T(8,128)(2,1)S(1)} copy-done((bf16[3,256,4096]{2,1,0:T(8,128)(2,1)S(1)}, bf16[3,256,4096]{2,1,0:T(8,128)(2,1)}, u32[]{:S(2)}) %copy-start.1) | copy-done | bytes 6291480
  100.3 1.6 norm_grads_a.1
  101.9 4.8 %collective-permute-start.24 = (bf16[2,4,256,256]{3,2,1,0:T(8,128)(2,1)S(1)}, bf16[2,4,256,256]{3,2,1,0:T(8,128)(2,1)S(1)}, u32[]{:S(2)}, u32[]{:S(2)}) collective-permute-start(bf16[2,4,256,256]{3,2,1,0:T(8,128)(2,1)S(1)} %norm_grads_a.1), channel_id=1, source_target_pairs={{0,1},{1,0},{2,3},{3,2},{4,5},{5,4},{6,7},{7,6},{8,9},{9,8},{10,11... | collective-permute-start | bytes 3145736 | tf_op jit(solution)/shard_map/ppermute | solution.py:244
  107.7 1.8 collective-permute-done.25
  109.5 2.3 %norm_grads_b.1 = (bf16[528,256]{1,0:T(8,128)(2,1)S(1)}, bf16[528,256]{1,0:T(8,128)(2,1)}, bf16[528,256]{1,0:T(8,128)(2,1)}, bf16[528,256]{1,0:T(8,128)(2,1)S(1)}) custom-call(s32[5]{0:T(128)S(1)} %stack.83.ids, bf16[3,256,4096]{2,1,0:T(8,128)(2,1)S(1)} %bitcast.34, bf16[3,256,256]{2,1,0:T(8,128)(2,1)S(1)} %copy-done.8, ...), custom_call_target="tpu_custom_call" | custom-call | flops 805306368 | bytes 3145728 | tf_op jit(solution)/shard_map/norm_grads_b/pallas_call | solution.py:26
  113.2 4.0 %in_w.1 = bf16[4,3,256,256]{3,2,1,0:T(8,128)(2,1)S(1)} custom-call(s32[5]{0:T(128)S(1)} %stack.83.ids, bf16[4,2,256,256]{3,2,1,0:T(8,128)(2,1)} %pad_maximum_fusion.mine_ref, bf16[4,2,256,256]{3,2,1,0:T(8,128)(2,1)} %collective-permute-done.23.other_ref, bf16[4,3,256,256]{3,2,1,0:T(8,128)(2,1)} %all-to-all-done.g_ref), custom_call_target="tpu_custom_call" | custom-call | flops 1610612736 | bytes 3145728 | tf_op jit(solution)/shard_map/in_w/pallas_call | solution.py:26
  117.2 1.1 copy-done.9
  118.3 2.7 %layer_out.1 = (bf16[256,256]{1,0:T(8,128)(2,1)}, bf16[4,3,256,256]{3,2,1,0:T(8,128)(2,1)S(1)}) custom-call(s32[5]{0:T(128)S(1)} %stack.83.ids, bf16[256,4096]{1,0:T(8,128)(2,1)S(1)} %copy-done.4, bf16[256,256]{1,0:T(8,128)(2,1)S(1)} %copy-done.12, bf16[256,256]{1,0:T(8,128)(2,1)S(1)} %copy-done.6, bf16[4,256,256]{2,1,0:T(8,128)(2,1)S(1)} %pad_maximum_fusion.2.a_ref, ...), custom_call_target="tpu_custom_call" | custom-call | flops 536870912 | bytes 4194304 | tf_op jit(solution)/shard_map/layer_out/pallas_call | solution.py:26
  121.1 1.1 copy-done.10
  122.2 4.4 %all-to-all-start.1 = ((bf16[4,3,256,256]{3,2,1,0:T(8,128)(2,1)}), bf16[4,3,256,256]{3,2,1,0:T(8,128)(2,1)S(1)}, u32[]{:S(2)}, u32[]{:S(2)}) async-start(bf16[4,3,256,256]{3,2,1,0:T(8,128)(2,1)} %copy-done.10), calls=%async_computation.2 | async-start | bytes 3145728 | tf_op jit(solution)/shard_map/all_to_all | solution.py:404
  127.4 1.0 collective-permute-start.28
  128.4 1.7 collective-permute-start.29
  130.1 2.0 collective-permute-start.30
  132.1 4.5 %tap_grads.1 = f32[16,128]{1,0:T(8,128)S(1)} custom-call(bf16[256,256]{1,0:T(8,128)(2,1)S(1)} %get-tuple-element.68.x_ref, bf16[256,128]{1,0:T(8,128)(2,1)S(1)} %copy-done.18, bf16[256,256]{1,0:T(8,128)(2,1)S(1)} %copy-done.14), custom_call_target="tpu_custom_call" | custom-call | flops 33554432 | tf_op jit(solution)/shard_map/tap_grads/pallas_call | solution.py:26
  136.7 1.5 collective-permute-start.32
  138.1 2.4 %collective-permute-start.33 = (f32[4,128]{1,0:T(4,128)S(1)}, f32[4,128]{1,0:T(4,128)S(1)}, u32[]{:S(2)}, u32[]{:S(2)}) collective-permute-start(f32[4,128]{1,0:T(4,128)S(1)} %bitcast.54), channel_id=1, source_target_pairs={{0,32},{16,48},{32,0},{48,16},{1,33},{17,49},{33,1},{49,17},{2,34}... | collective-permute-start | bytes 6152 | tf_op jit(solution)/shard_map/ppermute | solution.py:403
  140.5 2.0 collective-permute-done.32
  142.5 3.6 %collective-permute-start.34 = (f32[4,128]{1,0:T(4,128)S(1)}, f32[4,128]{1,0:T(4,128)S(1)}, u32[]{:S(2)}, u32[]{:S(2)}) collective-permute-start(f32[4,128]{1,0:T(4,128)S(1)} %bitcast.53), channel_id=1, source_target_pairs={{0,48},{16,0},{32,16},{48,32},{1,49},{17,1},{33,17},{49,33},{2,50}... | collective-permute-start | bytes 6152 | tf_op jit(solution)/shard_map/ppermute | solution.py:403
  147.1 3.4 %collective-permute-start.38 = (bf16[4,3,256,256]{3,2,1,0:T(8,128)(2,1)S(1)}, bf16[4,3,256,256]{3,2,1,0:T(8,128)(2,1)S(1)}, u32[]{:S(2)}, u32[]{:S(2)}) collective-permute-start(bf16[4,3,256,256]{3,2,1,0:T(8,128)(2,1)S(1)} %all-to-all-done.1.mine_ref.g_ref), channel_id=1, source_target_pairs={{0,1},{1,0},{2,3},{3,2},{4,5},{5,4},{6,7},{7,6},{8,9},{9,8},{10,11... | collective-permute-start | bytes 4718600 | tf_op jit(solution)/shard_map/ppermute | solution.py:405
  150.5 3.0 %collective-permute-done.38.other_ref = bf16[4,3,256,256]{3,2,1,0:T(8,128)(2,1)S(1)} collective-permute-done((bf16[4,3,256,256]{3,2,1,0:T(8,128)(2,1)S(1)}, bf16[4,3,256,256]{3,2,1,0:T(8,128)(2,1)S(1)}, u32[]{:S(2)}, u32[]{:S(2)}) %collective-permute-start.38) | collective-permute-done | bytes 1572896 | tf_op jit(solution)/shard_map/ppermute | solution.py:405
  153.6 2.1 %out_w.1 = bf16[4,1,256,256]{3,2,1,0:T(8,128)(2,1)} custom-call(s32[5]{0:T(128)S(1)} %stack.83.ids, bf16[4,3,256,256]{3,2,1,0:T(8,128)(2,1)S(1)} %all-to-all-done.1.mine_ref.g_ref, bf16[4,3,256,256]{3,2,1,0:T(8,128)(2,1)S(1)} %collective-permute-done.38.other_ref, bf16[4,3,256,256]{3,2,1,0:T(8,128)(2,1)S(1)} %all-to-all-done.1.mine_ref.g_ref), custom_call_target="tpu_custom_call" | custom-call | flops 536870912 | bytes 1048576 | tf_op jit(solution)/shard_map/out_w/pallas_call | solution.py:26
  155.6 6.2 %all-to-all-start.2 = ((bf16[4,256,256]{2,1,0:T(8,128)(2,1)}), bf16[4,256,256]{2,1,0:T(8,128)(2,1)S(1)}, u32[]{:S(2)}, u32[]{:S(2)}) async-start(bf16[4,256,256]{2,1,0:T(8,128)(2,1)} %bitcast.30), calls=%async_computation.3 | async-start | bytes 1048576 | tf_op jit(solution)/shard_map/all_to_all | solution.py:407
  161.8 1.5 collective-permute-start.35
  163.3 2.1 %collective-permute-start.36 = (f32[1,128]{1,0:T(1,128)S(1)}, f32[1,128]{1,0:T(1,128)S(1)}, u32[]{:S(2)}, u32[]{:S(2)}) collective-permute-start(f32[1,128]{1,0:T(1,128)S(1)} %get-tuple-element.105), channel_id=1, source_target_pairs={{0,128},{64,192},{128,0},{192,64},{1,129},{65,193},{129,1},{193,65... | collective-permute-start | bytes 1544 | tf_op jit(solution)/shard_map/ppermute | solution.py:416
  165.4 1.2 collective-permute-start.37
  167.5 4.3 %collective-permute-start.31 = (bf16[272,256]{1,0:T(8,128)(2,1)S(1)}, bf16[272,256]{1,0:T(8,128)(2,1)S(1)}, u32[]{:S(2)}, u32[]{:S(2)}) collective-permute-start(bf16[272,256]{1,0:T(8,128)(2,1)S(1)} %get-tuple-element.95), channel_id=1, source_target_pairs={{0,8},{8,0},{1,9},{9,1},{2,10},{10,2},{3,11},{11,3},{4,12},{12,4},... | collective-permute-start | bytes 417800 | tf_op jit(solution)/shard_map/ppermute | solution.py:264
  171.9 11.0 %collective-permute-done.35 = f32[1,128]{1,0:T(1,128)S(1)} collective-permute-done((f32[1,128]{1,0:T(1,128)S(1)}, f32[1,128]{1,0:T(1,128)S(1)}, u32[]{:S(2)}, u32[]{:S(2)}) %collective-permute-start.35) | collective-permute-done | bytes 544 | tf_op jit(solution)/shard_map/ppermute | solution.py:416
  182.9 7.5 %collective-permute-done.36 = f32[1,128]{1,0:T(1,128)S(1)} collective-permute-done((f32[1,128]{1,0:T(1,128)S(1)}, f32[1,128]{1,0:T(1,128)S(1)}, u32[]{:S(2)}, u32[]{:S(2)}) %collective-permute-start.36) | collective-permute-done | bytes 544 | tf_op jit(solution)/shard_map/ppermute | solution.py:416
  191.8 1.9 bitcast_convert_fusion
  (117 shorter events, 12.8 us)
Async XLA Ops:
  9.8 4.3 %copy-start.12 = (bf16[256,256]{1,0:T(8,128)(2,1)S(1)}, bf16[256,256]{1,0:T(8,128)(2,1)}, u32[]{:S(2)}) copy-start(bf16[256,256]{1,0:T(8,128)(2,1)} %hid_ref.3) | copy-start | bytes 393220
  9.8 16.9 %copy-start.3 = (bf16[256,4096]{1,0:T(8,128)(2,1)S(1)}, bf16[256,4096]{1,0:T(8,128)(2,1)}, u32[]{:S(2)}) copy-start(bf16[256,4096]{1,0:T(8,128)(2,1)} %w_ref.6) | copy-start | bytes 6291460
  9.8 16.9 %copy-start.6 = (bf16[256,256]{1,0:T(8,128)(2,1)S(1)}, bf16[256,256]{1,0:T(8,128)(2,1)}, u32[]{:S(2)}) copy-start(bf16[256,256]{1,0:T(8,128)(2,1)} %og_ref.3) | copy-start | bytes 393220
  10.8 15.8 %collective-permute-start = (bf16[2,4,256,256]{3,2,1,0:T(8,128)(2,1)S(1)}, bf16[2,4,256,256]{3,2,1,0:T(8,128)(2,1)S(1)}, u32[]{:S(2)}, u32[]{:S(2)}) collective-permute-start(bf16[2,4,256,256]{3,2,1,0:T(8,128)(2,1)S(1)} %mixed_grads_a.1), channel_id=1, source_target_pairs={{0,1},{1,0},{2,3},{3,2},{4,5},{5,4},{6,7},{7,6},{8,9},{9,8},{10,11... | collective-permute-start | bytes 3145736 | tf_op jit(solution)/shard_map/ppermute | solution.py:244
  14.1 9.6 %collective-permute-start.4 = (bf16[256,256]{1,0:T(8,128)(2,1)S(1)}, bf16[256,256]{1,0:T(8,128)(2,1)S(1)}, u32[]{:S(2)}, u32[]{:S(2)}) collective-permute-start(bf16[256,256]{1,0:T(8,128)(2,1)S(1)} %copy-done.12), channel_id=1, source_target_pairs={{0,6},{2,0},{4,2},{6,4},{1,7},{3,1},{5,3},{7,5},{8,14},{10,8},{12,... | collective-permute-start | bytes 393224 | tf_op jit(solution)/shard_map/ppermute | solution.py:337
  15.1 8.7 %collective-permute-start.2 = (bf16[256,256]{1,0:T(8,128)(2,1)S(1)}, bf16[256,256]{1,0:T(8,128)(2,1)S(1)}, u32[]{:S(2)}, u32[]{:S(2)}) collective-permute-start(bf16[256,256]{1,0:T(8,128)(2,1)S(1)} %copy-done.12), channel_id=1, source_target_pairs={{0,2},{2,4},{4,6},{6,0},{1,3},{3,5},{5,7},{7,1},{8,10},{10,12},{12... | collective-permute-start | bytes 393224 | tf_op jit(solution)/shard_map/ppermute | solution.py:337
  15.6 8.3 %collective-permute-start.3 = (bf16[256,256]{1,0:T(8,128)(2,1)S(1)}, bf16[256,256]{1,0:T(8,128)(2,1)S(1)}, u32[]{:S(2)}, u32[]{:S(2)}) collective-permute-start(bf16[256,256]{1,0:T(8,128)(2,1)S(1)} %copy-done.12), channel_id=1, source_target_pairs={{0,4},{2,6},{4,0},{6,2},{1,5},{3,7},{5,1},{7,3},{8,12},{10,14},{12... | collective-permute-start | bytes 393224 | tf_op jit(solution)/shard_map/ppermute | solution.py:337
  16.8 9.8 %collective-permute-start.1 = (bf16[256,256]{1,0:T(8,128)(2,1)S(1)}, bf16[256,256]{1,0:T(8,128)(2,1)S(1)}, u32[]{:S(2)}, u32[]{:S(2)}) collective-permute-start(bf16[256,256]{1,0:T(8,128)(2,1)S(1)} %copy-done.12), channel_id=1, source_target_pairs={{0,8},{8,0},{1,9},{9,1},{2,10},{10,2},{3,11},{11,3},{4,12},{12,4},... | collective-permute-start | bytes 393224 | tf_op jit(solution)/shard_map/ppermute | solution.py:339
  27.6 22.1 %copy-start.28 = (f32[4096]{0:T(1024)S(1)}, f32[4096]{0:T(1024)}, u32[]{:S(2)}) copy-start(f32[4096]{0:T(1024)} %param.7) | copy-start | bytes 49156
  27.6 10.3 %collective-permute-start.5 = (bf16[768,256]{1,0:T(8,128)(2,1)S(1)}, bf16[768,256]{1,0:T(8,128)(2,1)S(1)}, u32[]{:S(2)}, u32[]{:S(2)}) collective-permute-start(bf16[768,256]{1,0:T(8,128)(2,1)S(1)} %get-tuple-element.55), channel_id=1, source_target_pairs={{0,2},{2,4},{4,6},{6,0},{1,3},{3,5},{5,7},{7,1},{8,10},{10,12},{12... | collective-permute-start | bytes 1179656 | tf_op jit(solution)/shard_map/ppermute | solution.py:255
  29.3 17.2 %collective-permute-start.6 = (bf16[768,256]{1,0:T(8,128)(2,1)S(1)}, bf16[768,256]{1,0:T(8,128)(2,1)S(1)}, u32[]{:S(2)}, u32[]{:S(2)}) collective-permute-start(bf16[768,256]{1,0:T(8,128)(2,1)S(1)} %get-tuple-element.56), channel_id=1, source_target_pairs={{0,4},{2,6},{4,0},{6,2},{1,5},{3,7},{5,1},{7,3},{8,12},{10,14},{12... | collective-permute-start | bytes 1179656 | tf_op jit(solution)/shard_map/ppermute | solution.py:255
  30.2 17.7 %collective-permute-start.7 = (bf16[768,256]{1,0:T(8,128)(2,1)S(1)}, bf16[768,256]{1,0:T(8,128)(2,1)S(1)}, u32[]{:S(2)}, u32[]{:S(2)}) collective-permute-start(bf16[768,256]{1,0:T(8,128)(2,1)S(1)} %get-tuple-element.57), channel_id=1, source_target_pairs={{0,6},{2,0},{4,2},{6,4},{1,7},{3,1},{5,3},{7,5},{8,14},{10,8},{12,... | collective-permute-start | bytes 1179656 | tf_op jit(solution)/shard_map/ppermute | solution.py:255
  31.8 22.9 %collective-permute-start.8 = (bf16[4,256,256]{2,1,0:T(8,128)(2,1)S(1)}, bf16[4,256,256]{2,1,0:T(8,128)(2,1)S(1)}, u32[]{:S(2)}, u32[]{:S(2)}) collective-permute-start(bf16[4,256,256]{2,1,0:T(8,128)(2,1)S(1)} %pad_maximum_fusion.1.a_ref), channel_id=1, source_target_pairs={{0,1},{1,0},{2,3},{3,2},{4,5},{5,4},{6,7},{7,6},{8,9},{9,8},{10,11... | collective-permute-start | bytes 1572872 | tf_op jit(solution)/shard_map/ppermute | solution.py:338
  48.1 6.6 %collective-permute-start.9 = (bf16[4,256,256]{2,1,0:T(8,128)(2,1)S(1)}, bf16[4,256,256]{2,1,0:T(8,128)(2,1)S(1)}, u32[]{:S(2)}, u32[]{:S(2)}) collective-permute-start(bf16[4,256,256]{2,1,0:T(8,128)(2,1)S(1)} %get-tuple-element.60.b_ref), channel_id=1, source_target_pairs={{0,1},{1,0},{2,3},{3,2},{4,5},{5,4},{6,7},{7,6},{8,9},{9,8},{10,11... | collective-permute-start | bytes 1572872 | tf_op jit(solution)/shard_map/ppermute | solution.py:348
  49.8 14.0 %collective-permute-start.10 = (bf16[256,256]{1,0:T(8,128)(2,1)S(1)}, bf16[256,256]{1,0:T(8,128)(2,1)S(1)}, u32[]{:S(2)}, u32[]{:S(2)}) collective-permute-start(bf16[256,256]{1,0:T(8,128)(2,1)S(1)} %get-tuple-element.62), channel_id=1, source_target_pairs={{0,8},{8,0},{1,9},{9,1},{2,10},{10,2},{3,11},{11,3},{4,12},{12,4},... | collective-permute-start | bytes 393224 | tf_op jit(solution)/shard_map/ppermute | solution.py:264
  54.7 2.8 %copy-start = (bf16[3,256,4096]{2,1,0:T(8,128)(2,1)S(1)}, bf16[3,256,4096]{2,1,0:T(8,128)(2,1)}, u32[]{:S(2)}) copy-start(bf16[3,256,4096]{2,1,0:T(8,128)(2,1)} %w_ref.5) | copy-start | bytes 18874372
  57.5 7.7 %copy-start.23 = (f32[16,128]{1,0:T(8,128)S(1)}, f32[16,128]{1,0:T(8,128)}, u32[]{:S(2)}) copy-start(f32[16,128]{1,0:T(8,128)} %filt_ref) | copy-start | bytes 24580
  60.6 9.5 %copy-start.19 = (bf16[2,256,256]{2,1,0:T(8,128)(2,1)}, bf16[2,256,256]{2,1,0:T(8,128)(2,1)S(1)}, u32[]{:S(2)}) copy-start(bf16[2,256,256]{2,1,0:T(8,128)(2,1)S(1)} %get-tuple-element.77) | copy-start | bytes 786436
  60.6 5.7 %collective-permute-start.12 = (bf16[256,128]{1,0:T(8,128)(2,1)S(1)}, bf16[256,128]{1,0:T(8,128)(2,1)S(1)}, u32[]{:S(2)}, u32[]{:S(2)}) collective-permute-start(bf16[256,128]{1,0:T(8,128)(2,1)S(1)} %get-tuple-element.69), channel_id=1, source_target_pairs={{0,16},{16,32},{32,48},{48,64},{64,80},{80,96},{96,112},{112,128},... | collective-permute-start | bytes 196616 | tf_op jit(solution)/shard_map/ppermute | solution.py:359
  63.9 6.3 %copy-start.13 = (bf16[256,256]{1,0:T(8,128)(2,1)}, bf16[256,256]{1,0:T(8,128)(2,1)S(1)}, u32[]{:S(2)}) copy-start(bf16[256,256]{1,0:T(8,128)(2,1)S(1)} %get-tuple-element.99.g_ref) | copy-start | bytes 393220
  63.9 5.0 %collective-permute-start.11 = (bf16[256,128]{1,0:T(8,128)(2,1)S(1)}, bf16[256,128]{1,0:T(8,128)(2,1)S(1)}, u32[]{:S(2)}, u32[]{:S(2)}) collective-permute-start(bf16[256,128]{1,0:T(8,128)(2,1)S(1)} %get-tuple-element.65), channel_id=1, source_target_pairs={{16,0},{32,16},{48,32},{64,48},{80,64},{96,80},{112,96},{128,112},... | collective-permute-start | bytes 196616 | tf_op jit(solution)/shard_map/ppermute | solution.py:364
  67.0 21.3 %copy-start.21 = (bf16[256,256]{1,0:T(8,128)(2,1)}, bf16[256,256]{1,0:T(8,128)(2,1)S(1)}, u32[]{:S(2)}) copy-start(bf16[256,256]{1,0:T(8,128)(2,1)S(1)} %get-tuple-element.76) | copy-start | bytes 393220
  70.9 17.4 %copy-start.11 = (bf16[4,3,256,256]{3,2,1,0:T(8,128)(2,1)}, bf16[4,3,256,256]{3,2,1,0:T(8,128)(2,1)S(1)}, u32[]{:S(2)}) copy-start(bf16[4,3,256,256]{3,2,1,0:T(8,128)(2,1)S(1)} %get-tuple-element.84) | copy-start | bytes 4718596
  70.9 7.7 %collective-permute-start.16 = (bf16[256,256]{1,0:T(8,128)(2,1)S(1)}, bf16[256,256]{1,0:T(8,128)(2,1)S(1)}, u32[]{:S(2)}, u32[]{:S(2)}) collective-permute-start(bf16[256,256]{1,0:T(8,128)(2,1)S(1)} %get-tuple-element.76), channel_id=1, source_target_pairs={{0,8},{8,0},{1,9},{9,1},{2,10},{10,2},{3,11},{11,3},{4,12},{12,4},... | collective-permute-start | bytes 393224 | tf_op jit(solution)/shard_map/ppermute | solution.py:269
  72.4 8.9 %collective-permute-start.13 = (bf16[256,256]{1,0:T(8,128)(2,1)S(1)}, bf16[256,256]{1,0:T(8,128)(2,1)S(1)}, u32[]{:S(2)}, u32[]{:S(2)}) collective-permute-start(bf16[256,256]{1,0:T(8,128)(2,1)S(1)} %get-tuple-element.76), channel_id=1, source_target_pairs={{0,2},{2,4},{4,6},{6,0},{1,3},{3,5},{5,7},{7,1},{8,10},{10,12},{12... | collective-permute-start | bytes 393224 | tf_op jit(solution)/shard_map/ppermute | solution.py:268
  73.7 11.8 %collective-permute-start.14 = (bf16[256,256]{1,0:T(8,128)(2,1)S(1)}, bf16[256,256]{1,0:T(8,128)(2,1)S(1)}, u32[]{:S(2)}, u32[]{:S(2)}) collective-permute-start(bf16[256,256]{1,0:T(8,128)(2,1)S(1)} %get-tuple-element.76), channel_id=1, source_target_pairs={{0,4},{2,6},{4,0},{6,2},{1,5},{3,7},{5,1},{7,3},{8,12},{10,14},{12... | collective-permute-start | bytes 393224 | tf_op jit(solution)/shard_map/ppermute | solution.py:268
  75.9 9.6 %collective-permute-start.15 = (bf16[256,256]{1,0:T(8,128)(2,1)S(1)}, bf16[256,256]{1,0:T(8,128)(2,1)S(1)}, u32[]{:S(2)}, u32[]{:S(2)}) collective-permute-start(bf16[256,256]{1,0:T(8,128)(2,1)S(1)} %get-tuple-element.76), channel_id=1, source_target_pairs={{0,6},{2,0},{4,2},{6,4},{1,7},{3,1},{5,3},{7,5},{8,14},{10,8},{12,... | collective-permute-start | bytes 393224 | tf_op jit(solution)/shard_map/ppermute | solution.py:268
  78.6 9.7 %copy-start.25 = (bf16[256,256]{1,0:T(8,128)(2,1)}, bf16[256,256]{1,0:T(8,128)(2,1)S(1)}, u32[]{:S(2)}) copy-start(bf16[256,256]{1,0:T(8,128)(2,1)S(1)} %collective-permute-done.16) | copy-start | bytes 393220
  78.7 9.1 %collective-permute-start.17 = (bf16[256,256]{1,0:T(8,128)(2,1)S(1)}, bf16[256,256]{1,0:T(8,128)(2,1)S(1)}, u32[]{:S(2)}, u32[]{:S(2)}) collective-permute-start(bf16[256,256]{1,0:T(8,128)(2,1)S(1)} %collective-permute-done.16), channel_id=1, source_target_pairs={{0,2},{2,4},{4,6},{6,0},{1,3},{3,5},{5,7},{7,1},{8,10},{10,12},{12... | collective-permute-start | bytes 393224 | tf_op jit(solution)/shard_map/ppermute | solution.py:270
  80.0 15.2 %collective-permute-start.20 = (bf16[2,256,256]{2,1,0:T(8,128)(2,1)}, bf16[2,256,256]{2,1,0:T(8,128)(2,1)}, u32[]{:S(2)}, u32[]{:S(2)}) collective-permute-start(bf16[2,256,256]{2,1,0:T(8,128)(2,1)} %get-tuple-element.79), channel_id=1, source_target_pairs={{0,16},{16,32},{32,48},{48,0},{1,17},{17,33},{33,49},{49,1},{2,18}... | collective-permute-start | bytes 786440 | tf_op jit(solution)/shard_map/ppermute | solution.py:377
  81.3 14.0 %collective-permute-start.21 = (bf16[2,256,256]{2,1,0:T(8,128)(2,1)}, bf16[2,256,256]{2,1,0:T(8,128)(2,1)}, u32[]{:S(2)}, u32[]{:S(2)}) collective-permute-start(bf16[2,256,256]{2,1,0:T(8,128)(2,1)} %get-tuple-element.81), channel_id=1, source_target_pairs={{0,32},{16,48},{32,0},{48,16},{1,33},{17,49},{33,1},{49,17},{2,34}... | collective-permute-start | bytes 786440 | tf_op jit(solution)/shard_map/ppermute | solution.py:377
  85.5 9.7 %collective-permute-start.22 = (bf16[2,256,256]{2,1,0:T(8,128)(2,1)}, bf16[2,256,256]{2,1,0:T(8,128)(2,1)}, u32[]{:S(2)}, u32[]{:S(2)}) collective-permute-start(bf16[2,256,256]{2,1,0:T(8,128)(2,1)} %get-tuple-element.83), channel_id=1, source_target_pairs={{0,48},{16,0},{32,16},{48,32},{1,49},{17,1},{33,17},{49,33},{2,50}... | collective-permute-start | bytes 786440 | tf_op jit(solution)/shard_map/ppermute | solution.py:377
  85.5 2.9 %copy-start.27 = (bf16[256,256]{1,0:T(8,128)(2,1)}, bf16[256,256]{1,0:T(8,128)(2,1)S(1)}, u32[]{:S(2)}) copy-start(bf16[256,256]{1,0:T(8,128)(2,1)S(1)} %collective-permute-done.15) | copy-start | bytes 393220
  85.5 8.4 %collective-permute-start.18 = (bf16[256,256]{1,0:T(8,128)(2,1)S(1)}, bf16[256,256]{1,0:T(8,128)(2,1)}, u32[]{:S(2)}, u32[]{:S(2)}) collective-permute-start(bf16[256,256]{1,0:T(8,128)(2,1)S(1)} %collective-permute-done.16), channel_id=1, source_target_pairs={{0,4},{2,6},{4,0},{6,2},{1,5},{3,7},{5,1},{7,3},{8,12},{10,14},{12... | collective-permute-start | bytes 393224 | tf_op jit(solution)/shard_map/ppermute | solution.py:270
  87.8 6.2 %collective-permute-start.19 = (bf16[256,256]{1,0:T(8,128)(2,1)S(1)}, bf16[256,256]{1,0:T(8,128)(2,1)}, u32[]{:S(2)}, u32[]{:S(2)}) collective-permute-start(bf16[256,256]{1,0:T(8,128)(2,1)S(1)} %collective-permute-done.16), channel_id=1, source_target_pairs={{0,6},{2,0},{4,2},{6,4},{1,7},{3,1},{5,3},{7,5},{8,14},{10,8},{12,... | collective-permute-start | bytes 393224 | tf_op jit(solution)/shard_map/ppermute | solution.py:270
  88.4 4.6 %copy-start.22 = (bf16[256,256]{1,0:T(8,128)(2,1)S(1)}, bf16[256,256]{1,0:T(8,128)(2,1)}, u32[]{:S(2)}) copy-start(bf16[256,256]{1,0:T(8,128)(2,1)} %copy-done.21) | copy-start | bytes 393220
  88.4 21.1 %slice-start = ((s8[6291456]{0:T(1024)(128)(4,1)}), s8[2097152]{0:T(1024)(128)(4,1)S(1)}, s32[]{:S(2)}) async-start(s8[6291456]{0:T(1024)(128)(4,1)} %bitcast.33), calls=%async_computation.5 | async-start | bytes 4194304
  88.4 24.7 %all-to-all-start = ((bf16[4,3,256,256]{3,2,1,0:T(8,128)(2,1)}), bf16[4,3,256,256]{3,2,1,0:T(8,128)(2,1)}, u32[]{:S(2)}, u32[]{:S(2)}) async-start(bf16[4,3,256,256]{3,2,1,0:T(8,128)(2,1)} %copy-done.11), calls=%async_computation | async-start | bytes 3145728 | tf_op jit(solution)/shard_map/all_to_all | solution.py:380
  94.0 3.5 %copy-start.8 = (bf16[3,256,256]{2,1,0:T(8,128)(2,1)S(1)}, bf16[3,256,256]{2,1,0:T(8,128)(2,1)}, u32[]{:S(2)}) copy-start(bf16[3,256,256]{2,1,0:T(8,128)(2,1)} %copy-done.7) | copy-start | bytes 1179652
  97.5 2.8 %copy-start.1 = (bf16[3,256,4096]{2,1,0:T(8,128)(2,1)S(1)}, bf16[3,256,4096]{2,1,0:T(8,128)(2,1)}, u32[]{:S(2)}) copy-start(bf16[3,256,4096]{2,1,0:T(8,128)(2,1)} %w_ref.5) | copy-start | bytes 18874372
  100.3 9.2 %slice-start.1 = ((s8[6291456]{0:T(1024)(128)(4,1)}), s8[4194304]{0:T(1024)(128)(4,1)S(1)}, s32[]{:S(2)}) async-start(s8[6291456]{0:T(1024)(128)(4,1)} %bitcast.33), calls=%async_computation.6 | async-start | bytes 8388608
  101.9 7.6 %collective-permute-start.24 = (bf16[2,4,256,256]{3,2,1,0:T(8,128)(2,1)S(1)}, bf16[2,4,256,256]{3,2,1,0:T(8,128)(2,1)S(1)}, u32[]{:S(2)}, u32[]{:S(2)}) collective-permute-start(bf16[2,4,256,256]{3,2,1,0:T(8,128)(2,1)S(1)} %norm_grads_a.1), channel_id=1, source_target_pairs={{0,1},{1,0},{2,3},{3,2},{4,5},{5,4},{6,7},{7,6},{8,9},{9,8},{10,11... | collective-permute-start | bytes 3145736 | tf_op jit(solution)/shard_map/ppermute | solution.py:244
  106.7 6.5 %collective-permute-start.23 = (bf16[4,2,256,256]{3,2,1,0:T(8,128)(2,1)}, bf16[4,2,256,256]{3,2,1,0:T(8,128)(2,1)}, u32[]{:S(2)}, u32[]{:S(2)}) collective-permute-start(bf16[4,2,256,256]{3,2,1,0:T(8,128)(2,1)} %pad_maximum_fusion.mine_ref), channel_id=1, source_target_pairs={{0,1},{1,0},{2,3},{3,2},{4,5},{5,4},{6,7},{7,6},{8,9},{9,8},{10,11... | collective-permute-start | bytes 3145736 | tf_op jit(solution)/shard_map/ppermute | solution.py:379
  106.8 11.6 %collective-permute-start.26 = (bf16[4,256,256]{2,1,0:T(8,128)(2,1)S(1)}, bf16[4,256,256]{2,1,0:T(8,128)(2,1)}, u32[]{:S(2)}, u32[]{:S(2)}) collective-permute-start(bf16[4,256,256]{2,1,0:T(8,128)(2,1)S(1)} %pad_maximum_fusion.2.a_ref), channel_id=1, source_target_pairs={{0,1},{1,0},{2,3},{3,2},{4,5},{5,4},{6,7},{7,6},{8,9},{9,8},{10,11... | collective-permute-start | bytes 1572872 | tf_op jit(solution)/shard_map/ppermute | solution.py:273
  107.2 11.2 %collective-permute-start.27 = (bf16[4,256,256]{2,1,0:T(8,128)(2,1)S(1)}, bf16[4,256,256]{2,1,0:T(8,128)(2,1)}, u32[]{:S(2)}, u32[]{:S(2)}) collective-permute-start(bf16[4,256,256]{2,1,0:T(8,128)(2,1)S(1)} %pad_maximum_fusion.3.b_ref), channel_id=1, source_target_pairs={{0,1},{1,0},{2,3},{3,2},{4,5},{5,4},{6,7},{7,6},{8,9},{9,8},{10,11... | collective-permute-start | bytes 1572872 | tf_op jit(solution)/shard_map/ppermute | solution.py:273
  107.3 2.2 %collective-permute-start.25 = (f32[1,256]{1,0:T(1,128)S(1)}, f32[1,256]{1,0:T(1,128)S(1)}, u32[]{:S(2)}, u32[]{:S(2)}) collective-permute-start(f32[1,256]{1,0:T(1,128)S(1)} %get-tuple-element.86), channel_id=1, source_target_pairs={{0,1},{1,0},{2,3},{3,2},{4,5},{5,4},{6,7},{7,6},{8,9},{9,8},{10,11... | collective-permute-start | bytes 3080 | tf_op jit(solution)/shard_map/ppermute | solution.py:382
  113.2 5.2 %copy-start.4 = (bf16[256,4096]{1,0:T(8,128)(2,1)S(1)}, bf16[256,4096]{1,0:T(8,128)(2,1)}, u32[]{:S(2)}) copy-start(bf16[256,4096]{1,0:T(8,128)(2,1)} %w_ref.6) | copy-start | bytes 6291460
  122.2 24.8 %all-to-all-start.1 = ((bf16[4,3,256,256]{3,2,1,0:T(8,128)(2,1)}), bf16[4,3,256,256]{3,2,1,0:T(8,128)(2,1)S(1)}, u32[]{:S(2)}, u32[]{:S(2)}) async-start(bf16[4,3,256,256]{3,2,1,0:T(8,128)(2,1)} %copy-done.10), calls=%async_computation.2 | async-start | bytes 3145728 | tf_op jit(solution)/shard_map/all_to_all | solution.py:404
  126.6 5.5 %copy-start.14 = (bf16[256,256]{1,0:T(8,128)(2,1)S(1)}, bf16[256,256]{1,0:T(8,128)(2,1)}, u32[]{:S(2)}) copy-start(bf16[256,256]{1,0:T(8,128)(2,1)} %copy-done.13) | copy-start | bytes 393220
  126.6 5.5 %copy-start.18 = (bf16[256,128]{1,0:T(8,128)(2,1)S(1)}, bf16[256,128]{1,0:T(8,128)(2,1)}, u32[]{:S(2)}) copy-start(bf16[256,128]{1,0:T(8,128)(2,1)} %copy-done.17) | copy-start | bytes 196612
  126.6 20.3 %copy-start.16 = (bf16[528,256]{1,0:T(8,128)(2,1)S(1)}, bf16[528,256]{1,0:T(8,128)(2,1)}, u32[]{:S(2)}) copy-start(bf16[528,256]{1,0:T(8,128)(2,1)} %copy-done.15) | copy-start | bytes 811012
  126.6 65.2 %reduce-scatter.2.cloned.1.call-start = ((), (), s32[]{:S(2)}) async-start(), calls=%async_computation.4 | async-start | bytes 1966080 | tf_op jit(solution)/shard_map/reduce_scatter | solution.py:389
  127.4 19.5 %collective-permute-start.28 = (bf16[528,256]{1,0:T(8,128)(2,1)}, bf16[528,256]{1,0:T(8,128)(2,1)S(1)}, u32[]{:S(2)}, u32[]{:S(2)}) collective-permute-start(bf16[528,256]{1,0:T(8,128)(2,1)} %get-tuple-element.91), channel_id=1, source_target_pairs={{0,2},{2,4},{4,6},{6,0},{1,3},{3,5},{5,7},{7,1},{8,10},{10,12},{12... | collective-permute-start | bytes 811016 | tf_op jit(solution)/shard_map/ppermute | solution.py:255
  128.4 18.5 %collective-permute-start.29 = (bf16[528,256]{1,0:T(8,128)(2,1)}, bf16[528,256]{1,0:T(8,128)(2,1)S(1)}, u32[]{:S(2)}, u32[]{:S(2)}) collective-permute-start(bf16[528,256]{1,0:T(8,128)(2,1)} %get-tuple-element.92), channel_id=1, source_target_pairs={{0,4},{2,6},{4,0},{6,2},{1,5},{3,7},{5,1},{7,3},{8,12},{10,14},{12... | collective-permute-start | bytes 811016 | tf_op jit(solution)/shard_map/ppermute | solution.py:255
  130.1 16.8 %collective-permute-start.30 = (bf16[528,256]{1,0:T(8,128)(2,1)}, bf16[528,256]{1,0:T(8,128)(2,1)S(1)}, u32[]{:S(2)}, u32[]{:S(2)}) collective-permute-start(bf16[528,256]{1,0:T(8,128)(2,1)} %copy-done.24), channel_id=1, source_target_pairs={{0,6},{2,0},{4,2},{6,4},{1,7},{3,1},{5,3},{7,5},{8,14},{10,8},{12,... | collective-permute-start | bytes 811016 | tf_op jit(solution)/shard_map/ppermute | solution.py:255
  136.7 5.9 %collective-permute-start.32 = (f32[4,128]{1,0:T(4,128)S(1)}, f32[4,128]{1,0:T(4,128)S(1)}, u32[]{:S(2)}, u32[]{:S(2)}) collective-permute-start(f32[4,128]{1,0:T(4,128)S(1)} %bitcast.55), channel_id=1, source_target_pairs={{0,16},{16,32},{32,48},{48,0},{1,17},{17,33},{33,49},{49,1},{2,18}... | collective-permute-start | bytes 6152 | tf_op jit(solution)/shard_map/ppermute | solution.py:403
  138.1 8.0 %collective-permute-start.33 = (f32[4,128]{1,0:T(4,128)S(1)}, f32[4,128]{1,0:T(4,128)S(1)}, u32[]{:S(2)}, u32[]{:S(2)}) collective-permute-start(f32[4,128]{1,0:T(4,128)S(1)} %bitcast.54), channel_id=1, source_target_pairs={{0,32},{16,48},{32,0},{48,16},{1,33},{17,49},{33,1},{49,17},{2,34}... | collective-permute-start | bytes 6152 | tf_op jit(solution)/shard_map/ppermute | solution.py:403
  142.5 4.3 %collective-permute-start.34 = (f32[4,128]{1,0:T(4,128)S(1)}, f32[4,128]{1,0:T(4,128)S(1)}, u32[]{:S(2)}, u32[]{:S(2)}) collective-permute-start(f32[4,128]{1,0:T(4,128)S(1)} %bitcast.53), channel_id=1, source_target_pairs={{0,48},{16,0},{32,16},{48,32},{1,49},{17,1},{33,17},{49,33},{2,50}... | collective-permute-start | bytes 6152 | tf_op jit(solution)/shard_map/ppermute | solution.py:403
  147.1 6.5 %collective-permute-start.38 = (bf16[4,3,256,256]{3,2,1,0:T(8,128)(2,1)S(1)}, bf16[4,3,256,256]{3,2,1,0:T(8,128)(2,1)S(1)}, u32[]{:S(2)}, u32[]{:S(2)}) collective-permute-start(bf16[4,3,256,256]{3,2,1,0:T(8,128)(2,1)S(1)} %all-to-all-done.1.mine_ref.g_ref), channel_id=1, source_target_pairs={{0,1},{1,0},{2,3},{3,2},{4,5},{5,4},{6,7},{7,6},{8,9},{9,8},{10,11... | collective-permute-start | bytes 4718600 | tf_op jit(solution)/shard_map/ppermute | solution.py:405
  155.6 38.1 %all-to-all-start.2 = ((bf16[4,256,256]{2,1,0:T(8,128)(2,1)}), bf16[4,256,256]{2,1,0:T(8,128)(2,1)S(1)}, u32[]{:S(2)}, u32[]{:S(2)}) async-start(bf16[4,256,256]{2,1,0:T(8,128)(2,1)} %bitcast.30), calls=%async_computation.3 | async-start | bytes 1048576 | tf_op jit(solution)/shard_map/all_to_all | solution.py:407
  161.8 21.1 %collective-permute-start.35 = (f32[1,128]{1,0:T(1,128)S(1)}, f32[1,128]{1,0:T(1,128)S(1)}, u32[]{:S(2)}, u32[]{:S(2)}) collective-permute-start(f32[1,128]{1,0:T(1,128)S(1)} %get-tuple-element.107), channel_id=1, source_target_pairs={{0,64},{64,128},{128,192},{192,0},{1,65},{65,129},{129,193},{193,1... | collective-permute-start | bytes 1544 | tf_op jit(solution)/shard_map/ppermute | solution.py:416
  163.3 27.1 %collective-permute-start.36 = (f32[1,128]{1,0:T(1,128)S(1)}, f32[1,128]{1,0:T(1,128)S(1)}, u32[]{:S(2)}, u32[]{:S(2)}) collective-permute-start(f32[1,128]{1,0:T(1,128)S(1)} %get-tuple-element.105), channel_id=1, source_target_pairs={{0,128},{64,192},{128,0},{192,64},{1,129},{65,193},{129,1},{193,65... | collective-permute-start | bytes 1544 | tf_op jit(solution)/shard_map/ppermute | solution.py:416
  165.4 25.0 %collective-permute-start.37 = (f32[1,128]{1,0:T(1,128)S(1)}, f32[1,128]{1,0:T(1,128)S(1)}, u32[]{:S(2)}, u32[]{:S(2)}) collective-permute-start(f32[1,128]{1,0:T(1,128)S(1)} %get-tuple-element.106), channel_id=1, source_target_pairs={{0,192},{64,0},{128,64},{192,128},{1,193},{65,1},{129,65},{193,129... | collective-permute-start | bytes 1544 | tf_op jit(solution)/shard_map/ppermute | solution.py:416
  167.5 23.4 %collective-permute-start.31 = (bf16[272,256]{1,0:T(8,128)(2,1)S(1)}, bf16[272,256]{1,0:T(8,128)(2,1)S(1)}, u32[]{:S(2)}, u32[]{:S(2)}) collective-permute-start(bf16[272,256]{1,0:T(8,128)(2,1)S(1)} %get-tuple-element.95), channel_id=1, source_target_pairs={{0,8},{8,0},{1,9},{9,1},{2,10},{10,2},{3,11},{11,3},{4,12},{12,4},... | collective-permute-start | bytes 417800 | tf_op jit(solution)/shard_map/ppermute | solution.py:264
  (10 other events, 12.5 us)
Sparse Core Ops, SparseCore 0:
  130.0 49.8 reduce-scatter.1
where the time goes:
time: 202 us; the launch traced here: 201 us
  starting transfers between devices  91.2 us (45%)
  waiting for transfers between devices  47.7 us (24%)
  Pallas kernels  26.5 us (13%)
  between operations  14.5 us (7%)
  local copies, waits for them, and re-layouts  13.6 us (7%)
  other arithmetic  7.76 us (4%)
    pallas_call x16, Pallas kernels, call(): pl.pallas_call(body, out_shape=list(outs) if multi else outs, in_specs=sp...  26.5 us
    ppermute x3, waiting for transfers between devices, per_device(): lax.ppermute(row(s), 'zl', ring(4, s))  18.6 us
    ppermute x6, waiting for transfers between devices, reduce_scatter_tp(): lax.ppermute(blocks[s], 'y', ring(4, s))  14 us
    unnamed x62, local copies, waits for them, and re-layouts  12.6 us
    ppermute x2, starting transfers between devices, reduce_scatter_tp(): return (blocks[0], near, lax.ppermute(far, 'zh', SWAP), riders)  9.32 us
    ppermute x6, starting transfers between devices, reduce_scatter_tp(): lax.ppermute(blocks[s], 'y', ring(4, s))  8.89 us
    ppermute x2, starting transfers between devices, swap_products(): return lax.ppermute(first, 'core', SWAP)  8.13 us
    ppermute x3, starting transfers between devices, per_device(): lax.ppermute(pick(s), 'x', ring(4, s))  7.48 us
  transfers between devices with their start and end apart: 43, of which 13 were waited for; matrix products, arithmetic and copies ran while one was open for 4% of the time, Pallas kernels for 10%

commit v1 on v0

--- a/solution.py
+++ b/solution.py
@@ -402,7 +402,7 @@
     pick = lambda s: lax.dynamic_index_in_dim(taps, lax.rem(x + s, 4), 1, False)
     taps = pick(0) + sum(lax.ppermute(pick(s), "x", ring(4, s)) for s in (1, 2, 3))
     mixed_x = lax.all_to_all(m_send, "x", 0, 0, tiled=True)
-    mixed_other = lax.ppermute(after(mixed_x, taps, ng_parts[0]), "core", SWAP)
+    mixed_other = lax.ppermute(after(mixed_x, taps, ng_parts[1]), "core", SWAP)
     out_part = weight_grads(ids, mixed_x, mixed_other, mixed_x, False, 2, 1, "out_w")
     out_recv = lax.all_to_all(out_part[:, 0], "zl", 0, 0, tiled=True)
     out_weight_grads = jnp.sum(up(out_recv), axis=0)

time: 202 us -> 201 us (level)
  waiting for transfers between devices: 47.7 us -> 40.9 us
  starting transfers between devices: 91.2 us -> 97.3 us
    ppermute x3, waiting for transfers between devices: 18.6 us -> 8.39 us  [per_device(): lax.ppermute(row(s), 'zl', ring(4, s))]
    ppermute x1, starting transfers between devices: 3.44 us -> 8.73 us  [per_device(): mixed_other = lax.ppermute(after(mixed_x, taps, ng_parts[1]), 'core', SWAP)]
    ppermute x2, waiting for transfers between devices: 0.01 us -> 4.81 us  [reduce_scatter_tp(): return (blocks[0], near, lax.ppermute(far, 'zh', SWAP), riders)]
    all_to_all x1, starting transfers between devices: 6.17 us -> 11 us  [per_device(): out_recv = lax.all_to_all(out_part[:, 0], 'zl', 0, 0, tiled=True)]
    ppermute x3, starting transfers between devices: 7.48 us -> 5.05 us  [per_device(): lax.ppermute(pick(s), 'x', ring(4, s))]
    ppermute x3, waiting for transfers between devices: 2.73 us -> 0.37 us  [per_device(): lax.ppermute(pick(s), 'x', ring(4, s))]
  transfers between devices with their start and end apart: 43 -> 43, of which waited for: 13 -> 14; matrix products, arithmetic and copies ran while one was open for 4% -> 4% of each run, Pallas kernels for 10% -> 10%
where the time goes in v1:
time: 201 us
  starting transfers between devices  97.3 us (48%)
  waiting for transfers between devices  40.9 us (20%)
  Pallas kernels  26.5 us (13%)
  between operations  14.5 us (7%)
  local copies, waits for them, and re-layouts  13.6 us (7%)
  other arithmetic  7.75 us (4%)
    pallas_call x16, Pallas kernels, call(): pl.pallas_call(body, out_shape=list(outs) if multi else outs, in_specs=sp...  26.5 us
    ppermute x6, waiting for transfers between devices, reduce_scatter_tp(): lax.ppermute(blocks[s], 'y', ring(4, s))  14.8 us
    unnamed x62, local copies, waits for them, and re-layouts  12.6 us
    all_to_all x1, starting transfers between devices, per_device(): out_recv = lax.all_to_all(out_part[:, 0], 'zl', 0, 0, tiled=True)  11 us
    ppermute x6, starting transfers between devices, reduce_scatter_tp(): lax.ppermute(blocks[s], 'y', ring(4, s))  8.89 us
    ppermute x1, starting transfers between devices, per_device(): mixed_other = lax.ppermute(after(mixed_x, taps, ng_parts[1]), 'core', SWAP)  8.73 us
    ppermute x3, waiting for transfers between devices, per_device(): lax.ppermute(row(s), 'zl', ring(4, s))  8.39 us
    ppermute x2, starting transfers between devices, swap_products(): return lax.ppermute(first, 'core', SWAP)  8.13 us
  transfers between devices with their start and end apart: 43, of which 14 were waited for; matrix products, arithmetic and copies ran while one was open for 4% of the time, Pallas kernels for 10%

profile of v1, /device:TPU:1, one launch (start us, length us, event | category | flops | bytes accessed | tf_op | source)
XLA Modules:
  0.0 200.6 jit_solution(2843770554821606105)
XLA Ops:
  7.3 1.6 copy-done.2
  9.8 1.0 mixed_grads_a.1
  10.8 3.3 %collective-permute-start = (bf16[2,4,256,256]{3,2,1,0:T(8,128)(2,1)S(1)}, bf16[2,4,256,256]{3,2,1,0:T(8,128)(2,1)S(1)}, u32[]{:S(2)}, u32[]{:S(2)}) collective-permute-start(bf16[2,4,256,256]{3,2,1,0:T(8,128)(2,1)S(1)} %mixed_grads_a.1), channel_id=1, source_target_pairs={{0,1},{1,0},{2,3},{3,2},{4,5},{5,4},{6,7},{7,6},{8,9},{9,8},{10,11... | collective-permute-start | bytes 3145736 | tf_op jit(solution)/shard_map/ppermute | solution.py:244
  14.1 1.0 collective-permute-start.4
  15.6 1.2 collective-permute-start.3
  16.8 6.9 %collective-permute-start.1 = (bf16[256,256]{1,0:T(8,128)(2,1)S(1)}, bf16[256,256]{1,0:T(8,128)(2,1)S(1)}, u32[]{:S(2)}, u32[]{:S(2)}) collective-permute-start(bf16[256,256]{1,0:T(8,128)(2,1)S(1)} %copy-done.12), channel_id=1, source_target_pairs={{0,8},{8,0},{1,9},{9,1},{2,10},{10,2},{3,11},{11,3},{4,12},{12,4},... | collective-permute-start | bytes 393224 | tf_op jit(solution)/shard_map/ppermute | solution.py:339
  23.9 2.7 %collective-permute-done.1.rider_ref = bf16[256,256]{1,0:T(8,128)(2,1)S(1)} collective-permute-done((bf16[256,256]{1,0:T(8,128)(2,1)S(1)}, bf16[256,256]{1,0:T(8,128)(2,1)S(1)}, u32[]{:S(2)}, u32[]{:S(2)}) %collective-permute-start.1) | collective-permute-done | bytes 131104 | tf_op jit(solution)/shard_map/ppermute | solution.py:339
  26.6 1.0 mixed_grads_b.1
  27.6 1.7 collective-permute-start.5
  30.2 1.6 collective-permute-start.7
  31.8 2.2 %collective-permute-start.8 = (bf16[4,256,256]{2,1,0:T(8,128)(2,1)S(1)}, bf16[4,256,256]{2,1,0:T(8,128)(2,1)S(1)}, u32[]{:S(2)}, u32[]{:S(2)}) collective-permute-start(bf16[4,256,256]{2,1,0:T(8,128)(2,1)S(1)} %pad_maximum_fusion.1.a_ref), channel_id=1, source_target_pairs={{0,1},{1,0},{2,3},{3,2},{4,5},{5,4},{6,7},{7,6},{8,9},{9,8},{10,11... | collective-permute-start | bytes 1572872 | tf_op jit(solution)/shard_map/ppermute | solution.py:338
  34.0 3.9 %collective-permute-done.5.p1 = bf16[768,256]{1,0:T(8,128)(2,1)S(1)} collective-permute-done((bf16[768,256]{1,0:T(8,128)(2,1)S(1)}, bf16[768,256]{1,0:T(8,128)(2,1)S(1)}, u32[]{:S(2)}, u32[]{:S(2)}) %collective-permute-start.5) | collective-permute-done | bytes 393248 | tf_op jit(solution)/shard_map/ppermute | solution.py:255
  37.9 8.6 %collective-permute-done.6.p2 = bf16[768,256]{1,0:T(8,128)(2,1)S(1)} collective-permute-done((bf16[768,256]{1,0:T(8,128)(2,1)S(1)}, bf16[768,256]{1,0:T(8,128)(2,1)S(1)}, u32[]{:S(2)}, u32[]{:S(2)}) %collective-permute-start.6) | collective-permute-done | bytes 393248 | tf_op jit(solution)/shard_map/ppermute | solution.py:255
  46.5 1.4 collective-permute-done.7.p3
  48.1 1.6 collective-permute-start.9
  49.8 5.0 %collective-permute-start.10 = (bf16[256,256]{1,0:T(8,128)(2,1)S(1)}, bf16[256,256]{1,0:T(8,128)(2,1)S(1)}, u32[]{:S(2)}, u32[]{:S(2)}) collective-permute-start(bf16[256,256]{1,0:T(8,128)(2,1)S(1)} %get-tuple-element.62), channel_id=1, source_target_pairs={{0,8},{8,0},{1,9},{9,1},{2,10},{10,2},{3,11},{11,3},{4,12},{12,4},... | collective-permute-start | bytes 393224 | tf_op jit(solution)/shard_map/ppermute | solution.py:264
  54.7 2.8 %copy-done = bf16[3,256,4096]{2,1,0:T(8,128)(2,1)S(1)} copy-done((bf16[3,256,4096]{2,1,0:T(8,128)(2,1)S(1)}, bf16[3,256,4096]{2,1,0:T(8,128)(2,1)}, u32[]{:S(2)}) %copy-start) | copy-done | bytes 6291480
  57.5 3.1 %project.1 = (bf16[3,256,256]{2,1,0:T(8,128)(2,1)S(1)}, bf16[256,256]{1,0:T(8,128)(2,1)S(1)}, bf16[256,128]{1,0:T(8,128)(2,1)S(1)}, f32[1,256]{1,0:T(1,128)S(1)}...) custom-call(s32[5]{0:T(128)S(1)} %stack.83.ids, ...), custom_call_target="tpu_custom_call" | custom-call | flops 1610612736 | bytes 10485760 | tf_op jit(solution)/shard_map/project/pallas_call | solution.py:26
  60.6 3.1 %collective-permute-start.12 = (bf16[256,128]{1,0:T(8,128)(2,1)S(1)}, bf16[256,128]{1,0:T(8,128)(2,1)S(1)}, u32[]{:S(2)}, u32[]{:S(2)}) collective-permute-start(bf16[256,128]{1,0:T(8,128)(2,1)S(1)} %get-tuple-element.69), channel_id=1, source_target_pairs={{0,16},{16,32},{32,48},{48,64},{64,80},{80,96},{96,112},{112,128},... | collective-permute-start | bytes 196616 | tf_op jit(solution)/shard_map/ppermute | solution.py:359
  63.9 1.3 collective-permute-start.11
  65.2 1.1 taps.1
  67.1 1.9 collective-permute-done.11.halo_ref
  68.9 1.2 conv_back.1
  70.9 1.4 collective-permute-start.16
  72.4 1.4 collective-permute-start.13
  73.7 2.1 %collective-permute-start.14 = (bf16[256,256]{1,0:T(8,128)(2,1)S(1)}, bf16[256,256]{1,0:T(8,128)(2,1)S(1)}, u32[]{:S(2)}, u32[]{:S(2)}) collective-permute-start(bf16[256,256]{1,0:T(8,128)(2,1)S(1)} %get-tuple-element.76), channel_id=1, source_target_pairs={{0,4},{2,6},{4,0},{6,2},{1,5},{3,7},{5,1},{7,3},{8,12},{10,14},{12... | collective-permute-start | bytes 393224 | tf_op jit(solution)/shard_map/ppermute | solution.py:268
  76.5 2.2 %collective-permute-done.16 = bf16[256,256]{1,0:T(8,128)(2,1)S(1)} collective-permute-done((bf16[256,256]{1,0:T(8,128)(2,1)S(1)}, bf16[256,256]{1,0:T(8,128)(2,1)S(1)}, u32[]{:S(2)}, u32[]{:S(2)}) %collective-permute-start.16) | collective-permute-done | bytes 131104 | tf_op jit(solution)/shard_map/ppermute | solution.py:269
  78.7 1.4 collective-permute-start.17
  80.0 1.2 collective-permute-start.20
  81.3 4.3 %collective-permute-start.21 = (bf16[2,256,256]{2,1,0:T(8,128)(2,1)}, bf16[2,256,256]{2,1,0:T(8,128)(2,1)}, u32[]{:S(2)}, u32[]{:S(2)}) collective-permute-start(bf16[2,256,256]{2,1,0:T(8,128)(2,1)} %get-tuple-element.81), channel_id=1, source_target_pairs={{0,32},{16,48},{32,0},{48,16},{1,33},{17,49},{33,1},{49,17},{2,34}... | collective-permute-start | bytes 786440 | tf_op jit(solution)/shard_map/ppermute | solution.py:377
  85.5 2.2 %collective-permute-start.18 = (bf16[256,256]{1,0:T(8,128)(2,1)S(1)}, bf16[256,256]{1,0:T(8,128)(2,1)}, u32[]{:S(2)}, u32[]{:S(2)}) collective-permute-start(bf16[256,256]{1,0:T(8,128)(2,1)S(1)} %collective-permute-done.16), channel_id=1, source_target_pairs={{0,4},{2,6},{4,0},{6,2},{1,5},{3,7},{5,1},{7,3},{8,12},{10,14},{12... | collective-permute-start | bytes 393224 | tf_op jit(solution)/shard_map/ppermute | solution.py:270
  88.4 4.5 %all-to-all-start = ((bf16[4,3,256,256]{3,2,1,0:T(8,128)(2,1)}), bf16[4,3,256,256]{3,2,1,0:T(8,128)(2,1)}, u32[]{:S(2)}, u32[]{:S(2)}) async-start(bf16[4,3,256,256]{3,2,1,0:T(8,128)(2,1)} %copy-done.11), calls=%async_computation | async-start | bytes 3145728 | tf_op jit(solution)/shard_map/all_to_all | solution.py:380
  93.0 1.0 pad_maximum_fusion.2.a_ref
  94.0 1.2 pad_maximum_fusion.3.b_ref
  95.3 2.2 %pad_maximum_fusion.mine_ref = bf16[4,2,256,256]{3,2,1,0:T(8,128)(2,1)} fusion(bf16[1,2,256,256]{3,2,1,0:T(8,128)(2,1)} %bitcast.22, bf16[1,2,256,256]{3,2,1,0:T(8,128)(2,1)} %bitcast.21, bf16[1,2,256,256]{3,2,1,0:T(8,128)(2,1)} %bitcast.20, bf16[1,2,256,256]{3,2,1,0:T(8,128)(2,1)S(1)} %bitcast.40), kind=kLoop, calls=%fused_computation | loop fusion | flops 1572864 | bytes 2097152 | tf_op jit(solution)/shard_map/stack | solution.py:378
  97.5 2.8 %copy-done.1 = bf16[3,256,4096]{2,1,0:T(8,128)(2,1)S(1)} copy-done((bf16[3,256,4096]{2,1,0:T(8,128)(2,1)S(1)}, bf16[3,256,4096]{2,1,0:T(8,128)(2,1)}, u32[]{:S(2)}) %copy-start.1) | copy-done | bytes 6291480
  100.3 1.6 norm_grads_a.1
  101.9 4.8 %collective-permute-start.24 = (bf16[2,4,256,256]{3,2,1,0:T(8,128)(2,1)S(1)}, bf16[2,4,256,256]{3,2,1,0:T(8,128)(2,1)S(1)}, u32[]{:S(2)}, u32[]{:S(2)}) collective-permute-start(bf16[2,4,256,256]{3,2,1,0:T(8,128)(2,1)S(1)} %norm_grads_a.1), channel_id=1, source_target_pairs={{0,1},{1,0},{2,3},{3,2},{4,5},{5,4},{6,7},{7,6},{8,9},{9,8},{10,11... | collective-permute-start | bytes 3145736 | tf_op jit(solution)/shard_map/ppermute | solution.py:244
  107.7 1.8 collective-permute-done.25
  109.5 2.3 %norm_grads_b.1 = (bf16[528,256]{1,0:T(8,128)(2,1)S(1)}, bf16[528,256]{1,0:T(8,128)(2,1)}, bf16[528,256]{1,0:T(8,128)(2,1)}, bf16[528,256]{1,0:T(8,128)(2,1)S(1)}) custom-call(s32[5]{0:T(128)S(1)} %stack.83.ids, bf16[3,256,4096]{2,1,0:T(8,128)(2,1)S(1)} %bitcast.34, bf16[3,256,256]{2,1,0:T(8,128)(2,1)S(1)} %copy-done.8, ...), custom_call_target="tpu_custom_call" | custom-call | flops 805306368 | bytes 3145728 | tf_op jit(solution)/shard_map/norm_grads_b/pallas_call | solution.py:26
  113.2 4.0 %in_w.1 = bf16[4,3,256,256]{3,2,1,0:T(8,128)(2,1)S(1)} custom-call(s32[5]{0:T(128)S(1)} %stack.83.ids, bf16[4,2,256,256]{3,2,1,0:T(8,128)(2,1)} %pad_maximum_fusion.mine_ref, bf16[4,2,256,256]{3,2,1,0:T(8,128)(2,1)} %collective-permute-done.23.other_ref, bf16[4,3,256,256]{3,2,1,0:T(8,128)(2,1)} %all-to-all-done.g_ref), custom_call_target="tpu_custom_call" | custom-call | flops 1610612736 | bytes 3145728 | tf_op jit(solution)/shard_map/in_w/pallas_call | solution.py:26
  117.2 1.1 copy-done.9
  118.3 2.7 %layer_out.1 = (bf16[256,256]{1,0:T(8,128)(2,1)}, bf16[4,3,256,256]{3,2,1,0:T(8,128)(2,1)S(1)}) custom-call(s32[5]{0:T(128)S(1)} %stack.83.ids, bf16[256,4096]{1,0:T(8,128)(2,1)S(1)} %copy-done.4, bf16[256,256]{1,0:T(8,128)(2,1)S(1)} %copy-done.12, bf16[256,256]{1,0:T(8,128)(2,1)S(1)} %copy-done.6, bf16[4,256,256]{2,1,0:T(8,128)(2,1)S(1)} %pad_maximum_fusion.2.a_ref, ...), custom_call_target="tpu_custom_call" | custom-call | flops 536870912 | bytes 4194304 | tf_op jit(solution)/shard_map/layer_out/pallas_call | solution.py:26
  121.1 1.1 copy-done.10
  122.2 4.4 %all-to-all-start.1 = ((bf16[4,3,256,256]{3,2,1,0:T(8,128)(2,1)}), bf16[4,3,256,256]{3,2,1,0:T(8,128)(2,1)S(1)}, u32[]{:S(2)}, u32[]{:S(2)}) async-start(bf16[4,3,256,256]{3,2,1,0:T(8,128)(2,1)} %copy-done.10), calls=%async_computation.2 | async-start | bytes 3145728 | tf_op jit(solution)/shard_map/all_to_all | solution.py:404
  127.4 1.0 collective-permute-start.28
  128.4 1.7 collective-permute-start.29
  130.1 2.0 collective-permute-start.30
  132.1 4.5 %tap_grads.1 = f32[16,128]{1,0:T(8,128)S(1)} custom-call(bf16[256,256]{1,0:T(8,128)(2,1)S(1)} %get-tuple-element.68.x_ref, bf16[256,128]{1,0:T(8,128)(2,1)S(1)} %copy-done.18, bf16[256,256]{1,0:T(8,128)(2,1)S(1)} %copy-done.14), custom_call_target="tpu_custom_call" | custom-call | flops 33554432 | tf_op jit(solution)/shard_map/tap_grads/pallas_call | solution.py:26
  136.6 1.5 collective-permute-start.32
  138.1 2.4 %collective-permute-start.33 = (f32[4,128]{1,0:T(4,128)S(1)}, f32[4,128]{1,0:T(4,128)S(1)}, u32[]{:S(2)}, u32[]{:S(2)}) collective-permute-start(f32[4,128]{1,0:T(4,128)S(1)} %bitcast.54), channel_id=1, source_target_pairs={{0,32},{16,48},{32,0},{48,16},{1,33},{17,49},{33,1},{49,17},{2,34}... | collective-permute-start | bytes 6152 | tf_op jit(solution)/shard_map/ppermute | solution.py:403
  140.5 1.2 collective-permute-start.34
  142.7 2.8 %collective-permute-start.31 = (bf16[272,256]{1,0:T(8,128)(2,1)S(1)}, bf16[272,256]{1,0:T(8,128)(2,1)S(1)}, u32[]{:S(2)}, u32[]{:S(2)}) collective-permute-start(bf16[272,256]{1,0:T(8,128)(2,1)S(1)} %get-tuple-element.95), channel_id=1, source_target_pairs={{0,8},{8,0},{1,9},{9,1},{2,10},{10,2},{3,11},{11,3},{4,12},{12,4},... | collective-permute-start | bytes 417800 | tf_op jit(solution)/shard_map/ppermute | solution.py:264
  145.9 4.8 %collective-permute-done.31.far_ref = bf16[272,256]{1,0:T(8,128)(2,1)S(1)} collective-permute-done((bf16[272,256]{1,0:T(8,128)(2,1)S(1)}, bf16[272,256]{1,0:T(8,128)(2,1)S(1)}, u32[]{:S(2)}, u32[]{:S(2)}) %collective-permute-start.31) | collective-permute-done | bytes 139296 | tf_op jit(solution)/shard_map/ppermute | solution.py:264
  150.7 8.7 %collective-permute-start.38 = (bf16[4,3,256,256]{3,2,1,0:T(8,128)(2,1)S(1)}, bf16[4,3,256,256]{3,2,1,0:T(8,128)(2,1)S(1)}, u32[]{:S(2)}, u32[]{:S(2)}) collective-permute-start(bf16[4,3,256,256]{3,2,1,0:T(8,128)(2,1)S(1)} %all-to-all-done.1.mine_ref.g_ref), channel_id=1, source_target_pairs={{0,1},{1,0},{2,3},{3,2},{4,5},{5,4},{6,7},{7,6},{8,9},{9,8},{10,11... | collective-permute-start | bytes 4718600 | tf_op jit(solution)/shard_map/ppermute | solution.py:405
  159.4 3.0 %collective-permute-done.38.other_ref = bf16[4,3,256,256]{3,2,1,0:T(8,128)(2,1)S(1)} collective-permute-done((bf16[4,3,256,256]{3,2,1,0:T(8,128)(2,1)S(1)}, bf16[4,3,256,256]{3,2,1,0:T(8,128)(2,1)S(1)}, u32[]{:S(2)}, u32[]{:S(2)}) %collective-permute-start.38) | collective-permute-done | bytes 1572896 | tf_op jit(solution)/shard_map/ppermute | solution.py:405
  162.5 2.1 %out_w.1 = bf16[4,1,256,256]{3,2,1,0:T(8,128)(2,1)} custom-call(s32[5]{0:T(128)S(1)} %stack.83.ids, bf16[4,3,256,256]{3,2,1,0:T(8,128)(2,1)S(1)} %all-to-all-done.1.mine_ref.g_ref, bf16[4,3,256,256]{3,2,1,0:T(8,128)(2,1)S(1)} %collective-permute-done.38.other_ref, bf16[4,3,256,256]{3,2,1,0:T(8,128)(2,1)S(1)} %all-to-all-done.1.mine_ref.g_ref), custom_call_target="tpu_custom_call" | custom-call | flops 536870912 | bytes 1048576 | tf_op jit(solution)/shard_map/out_w/pallas_call | solution.py:26
  164.6 11.0 %all-to-all-start.2 = ((bf16[4,256,256]{2,1,0:T(8,128)(2,1)}), bf16[4,256,256]{2,1,0:T(8,128)(2,1)S(1)}, u32[]{:S(2)}, u32[]{:S(2)}) async-start(bf16[4,256,256]{2,1,0:T(8,128)(2,1)} %bitcast.30), calls=%async_computation.3 | async-start | bytes 1048576 | tf_op jit(solution)/shard_map/all_to_all | solution.py:407
  175.5 2.3 %collective-permute-start.35 = (f32[1,128]{1,0:T(1,128)S(1)}, f32[1,128]{1,0:T(1,128)S(1)}, u32[]{:S(2)}, u32[]{:S(2)}) collective-permute-start(f32[1,128]{1,0:T(1,128)S(1)} %get-tuple-element.107), channel_id=1, source_target_pairs={{0,64},{64,128},{128,192},{192,0},{1,65},{65,129},{129,193},{193,1... | collective-permute-start | bytes 1544 | tf_op jit(solution)/shard_map/ppermute | solution.py:416
  177.8 1.3 collective-permute-start.36
  179.1 1.2 collective-permute-start.37
  181.2 6.2 %collective-permute-done.35 = f32[1,128]{1,0:T(1,128)S(1)} collective-permute-done((f32[1,128]{1,0:T(1,128)S(1)}, f32[1,128]{1,0:T(1,128)S(1)}, u32[]{:S(2)}, u32[]{:S(2)}) %collective-permute-start.35) | collective-permute-done | bytes 544 | tf_op jit(solution)/shard_map/ppermute | solution.py:416
  187.4 2.2 %collective-permute-done.36 = f32[1,128]{1,0:T(1,128)S(1)} collective-permute-done((f32[1,128]{1,0:T(1,128)S(1)}, f32[1,128]{1,0:T(1,128)S(1)}, u32[]{:S(2)}, u32[]{:S(2)}) %collective-permute-start.36) | collective-permute-done | bytes 544 | tf_op jit(solution)/shard_map/ppermute | solution.py:416
  191.0 1.9 bitcast_convert_fusion
  (117 shorter events, 13.3 us)
Async XLA Ops:
  9.8 4.3 %copy-start.12 = (bf16[256,256]{1,0:T(8,128)(2,1)S(1)}, bf16[256,256]{1,0:T(8,128)(2,1)}, u32[]{:S(2)}) copy-start(bf16[256,256]{1,0:T(8,128)(2,1)} %hid_ref.3) | copy-start | bytes 393220
  9.8 16.9 %copy-start.3 = (bf16[256,4096]{1,0:T(8,128)(2,1)S(1)}, bf16[256,4096]{1,0:T(8,128)(2,1)}, u32[]{:S(2)}) copy-start(bf16[256,4096]{1,0:T(8,128)(2,1)} %w_ref.6) | copy-start | bytes 6291460
  9.8 16.9 %copy-start.6 = (bf16[256,256]{1,0:T(8,128)(2,1)S(1)}, bf16[256,256]{1,0:T(8,128)(2,1)}, u32[]{:S(2)}) copy-start(bf16[256,256]{1,0:T(8,128)(2,1)} %og_ref.3) | copy-start | bytes 393220
  10.8 15.8 %collective-permute-start = (bf16[2,4,256,256]{3,2,1,0:T(8,128)(2,1)S(1)}, bf16[2,4,256,256]{3,2,1,0:T(8,128)(2,1)S(1)}, u32[]{:S(2)}, u32[]{:S(2)}) collective-permute-start(bf16[2,4,256,256]{3,2,1,0:T(8,128)(2,1)S(1)} %mixed_grads_a.1), channel_id=1, source_target_pairs={{0,1},{1,0},{2,3},{3,2},{4,5},{5,4},{6,7},{7,6},{8,9},{9,8},{10,11... | collective-permute-start | bytes 3145736 | tf_op jit(solution)/shard_map/ppermute | solution.py:244
  14.1 9.6 %collective-permute-start.4 = (bf16[256,256]{1,0:T(8,128)(2,1)S(1)}, bf16[256,256]{1,0:T(8,128)(2,1)S(1)}, u32[]{:S(2)}, u32[]{:S(2)}) collective-permute-start(bf16[256,256]{1,0:T(8,128)(2,1)S(1)} %copy-done.12), channel_id=1, source_target_pairs={{0,6},{2,0},{4,2},{6,4},{1,7},{3,1},{5,3},{7,5},{8,14},{10,8},{12,... | collective-permute-start | bytes 393224 | tf_op jit(solution)/shard_map/ppermute | solution.py:337
  15.1 8.7 %collective-permute-start.2 = (bf16[256,256]{1,0:T(8,128)(2,1)S(1)}, bf16[256,256]{1,0:T(8,128)(2,1)S(1)}, u32[]{:S(2)}, u32[]{:S(2)}) collective-permute-start(bf16[256,256]{1,0:T(8,128)(2,1)S(1)} %copy-done.12), channel_id=1, source_target_pairs={{0,2},{2,4},{4,6},{6,0},{1,3},{3,5},{5,7},{7,1},{8,10},{10,12},{12... | collective-permute-start | bytes 393224 | tf_op jit(solution)/shard_map/ppermute | solution.py:337
  15.6 8.3 %collective-permute-start.3 = (bf16[256,256]{1,0:T(8,128)(2,1)S(1)}, bf16[256,256]{1,0:T(8,128)(2,1)S(1)}, u32[]{:S(2)}, u32[]{:S(2)}) collective-permute-start(bf16[256,256]{1,0:T(8,128)(2,1)S(1)} %copy-done.12), channel_id=1, source_target_pairs={{0,4},{2,6},{4,0},{6,2},{1,5},{3,7},{5,1},{7,3},{8,12},{10,14},{12... | collective-permute-start | bytes 393224 | tf_op jit(solution)/shard_map/ppermute | solution.py:337
  16.8 9.8 %collective-permute-start.1 = (bf16[256,256]{1,0:T(8,128)(2,1)S(1)}, bf16[256,256]{1,0:T(8,128)(2,1)S(1)}, u32[]{:S(2)}, u32[]{:S(2)}) collective-permute-start(bf16[256,256]{1,0:T(8,128)(2,1)S(1)} %copy-done.12), channel_id=1, source_target_pairs={{0,8},{8,0},{1,9},{9,1},{2,10},{10,2},{3,11},{11,3},{4,12},{12,4},... | collective-permute-start | bytes 393224 | tf_op jit(solution)/shard_map/ppermute | solution.py:339
  27.6 22.1 %copy-start.28 = (f32[4096]{0:T(1024)S(1)}, f32[4096]{0:T(1024)}, u32[]{:S(2)}) copy-start(f32[4096]{0:T(1024)} %param.7) | copy-start | bytes 49156
  27.6 10.3 %collective-permute-start.5 = (bf16[768,256]{1,0:T(8,128)(2,1)S(1)}, bf16[768,256]{1,0:T(8,128)(2,1)S(1)}, u32[]{:S(2)}, u32[]{:S(2)}) collective-permute-start(bf16[768,256]{1,0:T(8,128)(2,1)S(1)} %get-tuple-element.55), channel_id=1, source_target_pairs={{0,2},{2,4},{4,6},{6,0},{1,3},{3,5},{5,7},{7,1},{8,10},{10,12},{12... | collective-permute-start | bytes 1179656 | tf_op jit(solution)/shard_map/ppermute | solution.py:255
  29.3 17.2 %collective-permute-start.6 = (bf16[768,256]{1,0:T(8,128)(2,1)S(1)}, bf16[768,256]{1,0:T(8,128)(2,1)S(1)}, u32[]{:S(2)}, u32[]{:S(2)}) collective-permute-start(bf16[768,256]{1,0:T(8,128)(2,1)S(1)} %get-tuple-element.56), channel_id=1, source_target_pairs={{0,4},{2,6},{4,0},{6,2},{1,5},{3,7},{5,1},{7,3},{8,12},{10,14},{12... | collective-permute-start | bytes 1179656 | tf_op jit(solution)/shard_map/ppermute | solution.py:255
  30.2 17.7 %collective-permute-start.7 = (bf16[768,256]{1,0:T(8,128)(2,1)S(1)}, bf16[768,256]{1,0:T(8,128)(2,1)S(1)}, u32[]{:S(2)}, u32[]{:S(2)}) collective-permute-start(bf16[768,256]{1,0:T(8,128)(2,1)S(1)} %get-tuple-element.57), channel_id=1, source_target_pairs={{0,6},{2,0},{4,2},{6,4},{1,7},{3,1},{5,3},{7,5},{8,14},{10,8},{12,... | collective-permute-start | bytes 1179656 | tf_op jit(solution)/shard_map/ppermute | solution.py:255
  31.8 22.9 %collective-permute-start.8 = (bf16[4,256,256]{2,1,0:T(8,128)(2,1)S(1)}, bf16[4,256,256]{2,1,0:T(8,128)(2,1)S(1)}, u32[]{:S(2)}, u32[]{:S(2)}) collective-permute-start(bf16[4,256,256]{2,1,0:T(8,128)(2,1)S(1)} %pad_maximum_fusion.1.a_ref), channel_id=1, source_target_pairs={{0,1},{1,0},{2,3},{3,2},{4,5},{5,4},{6,7},{7,6},{8,9},{9,8},{10,11... | collective-permute-start | bytes 1572872 | tf_op jit(solution)/shard_map/ppermute | solution.py:338
  48.1 6.6 %collective-permute-start.9 = (bf16[4,256,256]{2,1,0:T(8,128)(2,1)S(1)}, bf16[4,256,256]{2,1,0:T(8,128)(2,1)S(1)}, u32[]{:S(2)}, u32[]{:S(2)}) collective-permute-start(bf16[4,256,256]{2,1,0:T(8,128)(2,1)S(1)} %get-tuple-element.60.b_ref), channel_id=1, source_target_pairs={{0,1},{1,0},{2,3},{3,2},{4,5},{5,4},{6,7},{7,6},{8,9},{9,8},{10,11... | collective-permute-start | bytes 1572872 | tf_op jit(solution)/shard_map/ppermute | solution.py:348
  49.8 14.0 %collective-permute-start.10 = (bf16[256,256]{1,0:T(8,128)(2,1)S(1)}, bf16[256,256]{1,0:T(8,128)(2,1)S(1)}, u32[]{:S(2)}, u32[]{:S(2)}) collective-permute-start(bf16[256,256]{1,0:T(8,128)(2,1)S(1)} %get-tuple-element.62), channel_id=1, source_target_pairs={{0,8},{8,0},{1,9},{9,1},{2,10},{10,2},{3,11},{11,3},{4,12},{12,4},... | collective-permute-start | bytes 393224 | tf_op jit(solution)/shard_map/ppermute | solution.py:264
  54.7 2.8 %copy-start = (bf16[3,256,4096]{2,1,0:T(8,128)(2,1)S(1)}, bf16[3,256,4096]{2,1,0:T(8,128)(2,1)}, u32[]{:S(2)}) copy-start(bf16[3,256,4096]{2,1,0:T(8,128)(2,1)} %w_ref.5) | copy-start | bytes 18874372
  57.5 7.7 %copy-start.23 = (f32[16,128]{1,0:T(8,128)S(1)}, f32[16,128]{1,0:T(8,128)}, u32[]{:S(2)}) copy-start(f32[16,128]{1,0:T(8,128)} %filt_ref) | copy-start | bytes 24580
  60.6 9.5 %copy-start.19 = (bf16[2,256,256]{2,1,0:T(8,128)(2,1)}, bf16[2,256,256]{2,1,0:T(8,128)(2,1)S(1)}, u32[]{:S(2)}) copy-start(bf16[2,256,256]{2,1,0:T(8,128)(2,1)S(1)} %get-tuple-element.77) | copy-start | bytes 786436
  60.6 5.7 %collective-permute-start.12 = (bf16[256,128]{1,0:T(8,128)(2,1)S(1)}, bf16[256,128]{1,0:T(8,128)(2,1)S(1)}, u32[]{:S(2)}, u32[]{:S(2)}) collective-permute-start(bf16[256,128]{1,0:T(8,128)(2,1)S(1)} %get-tuple-element.69), channel_id=1, source_target_pairs={{0,16},{16,32},{32,48},{48,64},{64,80},{80,96},{96,112},{112,128},... | collective-permute-start | bytes 196616 | tf_op jit(solution)/shard_map/ppermute | solution.py:359
  63.9 6.3 %copy-start.13 = (bf16[256,256]{1,0:T(8,128)(2,1)}, bf16[256,256]{1,0:T(8,128)(2,1)S(1)}, u32[]{:S(2)}) copy-start(bf16[256,256]{1,0:T(8,128)(2,1)S(1)} %get-tuple-element.99.g_ref) | copy-start | bytes 393220
  63.9 5.0 %collective-permute-start.11 = (bf16[256,128]{1,0:T(8,128)(2,1)S(1)}, bf16[256,128]{1,0:T(8,128)(2,1)S(1)}, u32[]{:S(2)}, u32[]{:S(2)}) collective-permute-start(bf16[256,128]{1,0:T(8,128)(2,1)S(1)} %get-tuple-element.65), channel_id=1, source_target_pairs={{16,0},{32,16},{48,32},{64,48},{80,64},{96,80},{112,96},{128,112},... | collective-permute-start | bytes 196616 | tf_op jit(solution)/shard_map/ppermute | solution.py:364
  67.0 21.3 %copy-start.21 = (bf16[256,256]{1,0:T(8,128)(2,1)}, bf16[256,256]{1,0:T(8,128)(2,1)S(1)}, u32[]{:S(2)}) copy-start(bf16[256,256]{1,0:T(8,128)(2,1)S(1)} %get-tuple-element.76) | copy-start | bytes 393220
  70.9 17.4 %copy-start.11 = (bf16[4,3,256,256]{3,2,1,0:T(8,128)(2,1)}, bf16[4,3,256,256]{3,2,1,0:T(8,128)(2,1)S(1)}, u32[]{:S(2)}) copy-start(bf16[4,3,256,256]{3,2,1,0:T(8,128)(2,1)S(1)} %get-tuple-element.84) | copy-start | bytes 4718596
  70.9 7.7 %collective-permute-start.16 = (bf16[256,256]{1,0:T(8,128)(2,1)S(1)}, bf16[256,256]{1,0:T(8,128)(2,1)S(1)}, u32[]{:S(2)}, u32[]{:S(2)}) collective-permute-start(bf16[256,256]{1,0:T(8,128)(2,1)S(1)} %get-tuple-element.76), channel_id=1, source_target_pairs={{0,8},{8,0},{1,9},{9,1},{2,10},{10,2},{3,11},{11,3},{4,12},{12,4},... | collective-permute-start | bytes 393224 | tf_op jit(solution)/shard_map/ppermute | solution.py:269
  72.4 8.9 %collective-permute-start.13 = (bf16[256,256]{1,0:T(8,128)(2,1)S(1)}, bf16[256,256]{1,0:T(8,128)(2,1)S(1)}, u32[]{:S(2)}, u32[]{:S(2)}) collective-permute-start(bf16[256,256]{1,0:T(8,128)(2,1)S(1)} %get-tuple-element.76), channel_id=1, source_target_pairs={{0,2},{2,4},{4,6},{6,0},{1,3},{3,5},{5,7},{7,1},{8,10},{10,12},{12... | collective-permute-start | bytes 393224 | tf_op jit(solution)/shard_map/ppermute | solution.py:268
  73.7 11.8 %collective-permute-start.14 = (bf16[256,256]{1,0:T(8,128)(2,1)S(1)}, bf16[256,256]{1,0:T(8,128)(2,1)S(1)}, u32[]{:S(2)}, u32[]{:S(2)}) collective-permute-start(bf16[256,256]{1,0:T(8,128)(2,1)S(1)} %get-tuple-element.76), channel_id=1, source_target_pairs={{0,4},{2,6},{4,0},{6,2},{1,5},{3,7},{5,1},{7,3},{8,12},{10,14},{12... | collective-permute-start | bytes 393224 | tf_op jit(solution)/shard_map/ppermute | solution.py:268
  75.9 9.6 %collective-permute-start.15 = (bf16[256,256]{1,0:T(8,128)(2,1)S(1)}, bf16[256,256]{1,0:T(8,128)(2,1)S(1)}, u32[]{:S(2)}, u32[]{:S(2)}) collective-permute-start(bf16[256,256]{1,0:T(8,128)(2,1)S(1)} %get-tuple-element.76), channel_id=1, source_target_pairs={{0,6},{2,0},{4,2},{6,4},{1,7},{3,1},{5,3},{7,5},{8,14},{10,8},{12,... | collective-permute-start | bytes 393224 | tf_op jit(solution)/shard_map/ppermute | solution.py:268
  78.6 9.7 %copy-start.25 = (bf16[256,256]{1,0:T(8,128)(2,1)}, bf16[256,256]{1,0:T(8,128)(2,1)S(1)}, u32[]{:S(2)}) copy-start(bf16[256,256]{1,0:T(8,128)(2,1)S(1)} %collective-permute-done.16) | copy-start | bytes 393220
  78.7 9.1 %collective-permute-start.17 = (bf16[256,256]{1,0:T(8,128)(2,1)S(1)}, bf16[256,256]{1,0:T(8,128)(2,1)S(1)}, u32[]{:S(2)}, u32[]{:S(2)}) collective-permute-start(bf16[256,256]{1,0:T(8,128)(2,1)S(1)} %collective-permute-done.16), channel_id=1, source_target_pairs={{0,2},{2,4},{4,6},{6,0},{1,3},{3,5},{5,7},{7,1},{8,10},{10,12},{12... | collective-permute-start | bytes 393224 | tf_op jit(solution)/shard_map/ppermute | solution.py:270
  80.0 15.2 %collective-permute-start.20 = (bf16[2,256,256]{2,1,0:T(8,128)(2,1)}, bf16[2,256,256]{2,1,0:T(8,128)(2,1)}, u32[]{:S(2)}, u32[]{:S(2)}) collective-permute-start(bf16[2,256,256]{2,1,0:T(8,128)(2,1)} %get-tuple-element.79), channel_id=1, source_target_pairs={{0,16},{16,32},{32,48},{48,0},{1,17},{17,33},{33,49},{49,1},{2,18}... | collective-permute-start | bytes 786440 | tf_op jit(solution)/shard_map/ppermute | solution.py:377
  81.3 14.0 %collective-permute-start.21 = (bf16[2,256,256]{2,1,0:T(8,128)(2,1)}, bf16[2,256,256]{2,1,0:T(8,128)(2,1)}, u32[]{:S(2)}, u32[]{:S(2)}) collective-permute-start(bf16[2,256,256]{2,1,0:T(8,128)(2,1)} %get-tuple-element.81), channel_id=1, source_target_pairs={{0,32},{16,48},{32,0},{48,16},{1,33},{17,49},{33,1},{49,17},{2,34}... | collective-permute-start | bytes 786440 | tf_op jit(solution)/shard_map/ppermute | solution.py:377
  85.5 9.7 %collective-permute-start.22 = (bf16[2,256,256]{2,1,0:T(8,128)(2,1)}, bf16[2,256,256]{2,1,0:T(8,128)(2,1)}, u32[]{:S(2)}, u32[]{:S(2)}) collective-permute-start(bf16[2,256,256]{2,1,0:T(8,128)(2,1)} %get-tuple-element.83), channel_id=1, source_target_pairs={{0,48},{16,0},{32,16},{48,32},{1,49},{17,1},{33,17},{49,33},{2,50}... | collective-permute-start | bytes 786440 | tf_op jit(solution)/shard_map/ppermute | solution.py:377
  85.5 2.9 %copy-start.27 = (bf16[256,256]{1,0:T(8,128)(2,1)}, bf16[256,256]{1,0:T(8,128)(2,1)S(1)}, u32[]{:S(2)}) copy-start(bf16[256,256]{1,0:T(8,128)(2,1)S(1)} %collective-permute-done.15) | copy-start | bytes 393220
  85.5 8.4 %collective-permute-start.18 = (bf16[256,256]{1,0:T(8,128)(2,1)S(1)}, bf16[256,256]{1,0:T(8,128)(2,1)}, u32[]{:S(2)}, u32[]{:S(2)}) collective-permute-start(bf16[256,256]{1,0:T(8,128)(2,1)S(1)} %collective-permute-done.16), channel_id=1, source_target_pairs={{0,4},{2,6},{4,0},{6,2},{1,5},{3,7},{5,1},{7,3},{8,12},{10,14},{12... | collective-permute-start | bytes 393224 | tf_op jit(solution)/shard_map/ppermute | solution.py:270
  87.8 6.2 %collective-permute-start.19 = (bf16[256,256]{1,0:T(8,128)(2,1)S(1)}, bf16[256,256]{1,0:T(8,128)(2,1)}, u32[]{:S(2)}, u32[]{:S(2)}) collective-permute-start(bf16[256,256]{1,0:T(8,128)(2,1)S(1)} %collective-permute-done.16), channel_id=1, source_target_pairs={{0,6},{2,0},{4,2},{6,4},{1,7},{3,1},{5,3},{7,5},{8,14},{10,8},{12,... | collective-permute-start | bytes 393224 | tf_op jit(solution)/shard_map/ppermute | solution.py:270
  88.4 4.6 %copy-start.22 = (bf16[256,256]{1,0:T(8,128)(2,1)S(1)}, bf16[256,256]{1,0:T(8,128)(2,1)}, u32[]{:S(2)}) copy-start(bf16[256,256]{1,0:T(8,128)(2,1)} %copy-done.21) | copy-start | bytes 393220
  88.4 21.1 %slice-start = ((s8[6291456]{0:T(1024)(128)(4,1)}), s8[2097152]{0:T(1024)(128)(4,1)S(1)}, s32[]{:S(2)}) async-start(s8[6291456]{0:T(1024)(128)(4,1)} %bitcast.33), calls=%async_computation.5 | async-start | bytes 4194304
  88.4 24.7 %all-to-all-start = ((bf16[4,3,256,256]{3,2,1,0:T(8,128)(2,1)}), bf16[4,3,256,256]{3,2,1,0:T(8,128)(2,1)}, u32[]{:S(2)}, u32[]{:S(2)}) async-start(bf16[4,3,256,256]{3,2,1,0:T(8,128)(2,1)} %copy-done.11), calls=%async_computation | async-start | bytes 3145728 | tf_op jit(solution)/shard_map/all_to_all | solution.py:380
  94.0 3.5 %copy-start.8 = (bf16[3,256,256]{2,1,0:T(8,128)(2,1)S(1)}, bf16[3,256,256]{2,1,0:T(8,128)(2,1)}, u32[]{:S(2)}) copy-start(bf16[3,256,256]{2,1,0:T(8,128)(2,1)} %copy-done.7) | copy-start | bytes 1179652
  97.5 2.8 %copy-start.1 = (bf16[3,256,4096]{2,1,0:T(8,128)(2,1)S(1)}, bf16[3,256,4096]{2,1,0:T(8,128)(2,1)}, u32[]{:S(2)}) copy-start(bf16[3,256,4096]{2,1,0:T(8,128)(2,1)} %w_ref.5) | copy-start | bytes 18874372
  100.3 9.2 %slice-start.1 = ((s8[6291456]{0:T(1024)(128)(4,1)}), s8[4194304]{0:T(1024)(128)(4,1)S(1)}, s32[]{:S(2)}) async-start(s8[6291456]{0:T(1024)(128)(4,1)} %bitcast.33), calls=%async_computation.6 | async-start | bytes 8388608
  101.9 7.6 %collective-permute-start.24 = (bf16[2,4,256,256]{3,2,1,0:T(8,128)(2,1)S(1)}, bf16[2,4,256,256]{3,2,1,0:T(8,128)(2,1)S(1)}, u32[]{:S(2)}, u32[]{:S(2)}) collective-permute-start(bf16[2,4,256,256]{3,2,1,0:T(8,128)(2,1)S(1)} %norm_grads_a.1), channel_id=1, source_target_pairs={{0,1},{1,0},{2,3},{3,2},{4,5},{5,4},{6,7},{7,6},{8,9},{9,8},{10,11... | collective-permute-start | bytes 3145736 | tf_op jit(solution)/shard_map/ppermute | solution.py:244
  106.7 6.5 %collective-permute-start.23 = (bf16[4,2,256,256]{3,2,1,0:T(8,128)(2,1)}, bf16[4,2,256,256]{3,2,1,0:T(8,128)(2,1)}, u32[]{:S(2)}, u32[]{:S(2)}) collective-permute-start(bf16[4,2,256,256]{3,2,1,0:T(8,128)(2,1)} %pad_maximum_fusion.mine_ref), channel_id=1, source_target_pairs={{0,1},{1,0},{2,3},{3,2},{4,5},{5,4},{6,7},{7,6},{8,9},{9,8},{10,11... | collective-permute-start | bytes 3145736 | tf_op jit(solution)/shard_map/ppermute | solution.py:379
  106.8 11.6 %collective-permute-start.26 = (bf16[4,256,256]{2,1,0:T(8,128)(2,1)S(1)}, bf16[4,256,256]{2,1,0:T(8,128)(2,1)}, u32[]{:S(2)}, u32[]{:S(2)}) collective-permute-start(bf16[4,256,256]{2,1,0:T(8,128)(2,1)S(1)} %pad_maximum_fusion.2.a_ref), channel_id=1, source_target_pairs={{0,1},{1,0},{2,3},{3,2},{4,5},{5,4},{6,7},{7,6},{8,9},{9,8},{10,11... | collective-permute-start | bytes 1572872 | tf_op jit(solution)/shard_map/ppermute | solution.py:273
  107.2 11.2 %collective-permute-start.27 = (bf16[4,256,256]{2,1,0:T(8,128)(2,1)S(1)}, bf16[4,256,256]{2,1,0:T(8,128)(2,1)}, u32[]{:S(2)}, u32[]{:S(2)}) collective-permute-start(bf16[4,256,256]{2,1,0:T(8,128)(2,1)S(1)} %pad_maximum_fusion.3.b_ref), channel_id=1, source_target_pairs={{0,1},{1,0},{2,3},{3,2},{4,5},{5,4},{6,7},{7,6},{8,9},{9,8},{10,11... | collective-permute-start | bytes 1572872 | tf_op jit(solution)/shard_map/ppermute | solution.py:273
  107.3 2.2 %collective-permute-start.25 = (f32[1,256]{1,0:T(1,128)S(1)}, f32[1,256]{1,0:T(1,128)S(1)}, u32[]{:S(2)}, u32[]{:S(2)}) collective-permute-start(f32[1,256]{1,0:T(1,128)S(1)} %get-tuple-element.86), channel_id=1, source_target_pairs={{0,1},{1,0},{2,3},{3,2},{4,5},{5,4},{6,7},{7,6},{8,9},{9,8},{10,11... | collective-permute-start | bytes 3080 | tf_op jit(solution)/shard_map/ppermute | solution.py:382
  113.2 5.2 %copy-start.4 = (bf16[256,4096]{1,0:T(8,128)(2,1)S(1)}, bf16[256,4096]{1,0:T(8,128)(2,1)}, u32[]{:S(2)}) copy-start(bf16[256,4096]{1,0:T(8,128)(2,1)} %w_ref.6) | copy-start | bytes 6291460
  122.2 28.5 %all-to-all-start.1 = ((bf16[4,3,256,256]{3,2,1,0:T(8,128)(2,1)}), bf16[4,3,256,256]{3,2,1,0:T(8,128)(2,1)S(1)}, u32[]{:S(2)}, u32[]{:S(2)}) async-start(bf16[4,3,256,256]{3,2,1,0:T(8,128)(2,1)} %copy-done.10), calls=%async_computation.2 | async-start | bytes 3145728 | tf_op jit(solution)/shard_map/all_to_all | solution.py:404
  126.6 5.5 %copy-start.14 = (bf16[256,256]{1,0:T(8,128)(2,1)S(1)}, bf16[256,256]{1,0:T(8,128)(2,1)}, u32[]{:S(2)}) copy-start(bf16[256,256]{1,0:T(8,128)(2,1)} %copy-done.13) | copy-start | bytes 393220
  126.6 5.5 %copy-start.18 = (bf16[256,128]{1,0:T(8,128)(2,1)S(1)}, bf16[256,128]{1,0:T(8,128)(2,1)}, u32[]{:S(2)}) copy-start(bf16[256,128]{1,0:T(8,128)(2,1)} %copy-done.17) | copy-start | bytes 196612
  126.6 15.9 %copy-start.16 = (bf16[528,256]{1,0:T(8,128)(2,1)S(1)}, bf16[528,256]{1,0:T(8,128)(2,1)}, u32[]{:S(2)}) copy-start(bf16[528,256]{1,0:T(8,128)(2,1)} %copy-done.15) | copy-start | bytes 811012
  126.6 64.4 %reduce-scatter.2.cloned.1.call-start = ((), (), s32[]{:S(2)}) async-start(), calls=%async_computation.4 | async-start | bytes 1966080 | tf_op jit(solution)/shard_map/reduce_scatter | solution.py:389
  127.4 13.1 %collective-permute-start.28 = (bf16[528,256]{1,0:T(8,128)(2,1)}, bf16[528,256]{1,0:T(8,128)(2,1)S(1)}, u32[]{:S(2)}, u32[]{:S(2)}) collective-permute-start(bf16[528,256]{1,0:T(8,128)(2,1)} %get-tuple-element.91), channel_id=1, source_target_pairs={{0,2},{2,4},{4,6},{6,0},{1,3},{3,5},{5,7},{7,1},{8,10},{10,12},{12... | collective-permute-start | bytes 811016 | tf_op jit(solution)/shard_map/ppermute | solution.py:255
  128.4 13.3 %collective-permute-start.29 = (bf16[528,256]{1,0:T(8,128)(2,1)}, bf16[528,256]{1,0:T(8,128)(2,1)S(1)}, u32[]{:S(2)}, u32[]{:S(2)}) collective-permute-start(bf16[528,256]{1,0:T(8,128)(2,1)} %get-tuple-element.92), channel_id=1, source_target_pairs={{0,4},{2,6},{4,0},{6,2},{1,5},{3,7},{5,1},{7,3},{8,12},{10,14},{12... | collective-permute-start | bytes 811016 | tf_op jit(solution)/shard_map/ppermute | solution.py:255
  130.1 12.5 %collective-permute-start.30 = (bf16[528,256]{1,0:T(8,128)(2,1)}, bf16[528,256]{1,0:T(8,128)(2,1)S(1)}, u32[]{:S(2)}, u32[]{:S(2)}) collective-permute-start(bf16[528,256]{1,0:T(8,128)(2,1)} %copy-done.24), channel_id=1, source_target_pairs={{0,6},{2,0},{4,2},{6,4},{1,7},{3,1},{5,3},{7,5},{8,14},{10,8},{12,... | collective-permute-start | bytes 811016 | tf_op jit(solution)/shard_map/ppermute | solution.py:255
  136.6 8.9 %collective-permute-start.32 = (f32[4,128]{1,0:T(4,128)S(1)}, f32[4,128]{1,0:T(4,128)S(1)}, u32[]{:S(2)}, u32[]{:S(2)}) collective-permute-start(f32[4,128]{1,0:T(4,128)S(1)} %bitcast.55), channel_id=1, source_target_pairs={{0,16},{16,32},{32,48},{48,0},{1,17},{17,33},{33,49},{49,1},{2,18}... | collective-permute-start | bytes 6152 | tf_op jit(solution)/shard_map/ppermute | solution.py:403
  138.1 7.8 %collective-permute-start.33 = (f32[4,128]{1,0:T(4,128)S(1)}, f32[4,128]{1,0:T(4,128)S(1)}, u32[]{:S(2)}, u32[]{:S(2)}) collective-permute-start(f32[4,128]{1,0:T(4,128)S(1)} %bitcast.54), channel_id=1, source_target_pairs={{0,32},{16,48},{32,0},{48,16},{1,33},{17,49},{33,1},{49,17},{2,34}... | collective-permute-start | bytes 6152 | tf_op jit(solution)/shard_map/ppermute | solution.py:403
  140.5 5.4 %collective-permute-start.34 = (f32[4,128]{1,0:T(4,128)S(1)}, f32[4,128]{1,0:T(4,128)S(1)}, u32[]{:S(2)}, u32[]{:S(2)}) collective-permute-start(f32[4,128]{1,0:T(4,128)S(1)} %bitcast.53), channel_id=1, source_target_pairs={{0,48},{16,0},{32,16},{48,32},{1,49},{17,1},{33,17},{49,33},{2,50}... | collective-permute-start | bytes 6152 | tf_op jit(solution)/shard_map/ppermute | solution.py:403
  142.7 8.0 %collective-permute-start.31 = (bf16[272,256]{1,0:T(8,128)(2,1)S(1)}, bf16[272,256]{1,0:T(8,128)(2,1)S(1)}, u32[]{:S(2)}, u32[]{:S(2)}) collective-permute-start(bf16[272,256]{1,0:T(8,128)(2,1)S(1)} %get-tuple-element.95), channel_id=1, source_target_pairs={{0,8},{8,0},{1,9},{9,1},{2,10},{10,2},{3,11},{11,3},{4,12},{12,4},... | collective-permute-start | bytes 417800 | tf_op jit(solution)/shard_map/ppermute | solution.py:264
  150.7 11.8 %collective-permute-start.38 = (bf16[4,3,256,256]{3,2,1,0:T(8,128)(2,1)S(1)}, bf16[4,3,256,256]{3,2,1,0:T(8,128)(2,1)S(1)}, u32[]{:S(2)}, u32[]{:S(2)}) collective-permute-start(bf16[4,3,256,256]{3,2,1,0:T(8,128)(2,1)S(1)} %all-to-all-done.1.mine_ref.g_ref), channel_id=1, source_target_pairs={{0,1},{1,0},{2,3},{3,2},{4,5},{5,4},{6,7},{7,6},{8,9},{9,8},{10,11... | collective-permute-start | bytes 4718600 | tf_op jit(solution)/shard_map/ppermute | solution.py:405
  164.6 28.4 %all-to-all-start.2 = ((bf16[4,256,256]{2,1,0:T(8,128)(2,1)}), bf16[4,256,256]{2,1,0:T(8,128)(2,1)S(1)}, u32[]{:S(2)}, u32[]{:S(2)}) async-start(bf16[4,256,256]{2,1,0:T(8,128)(2,1)} %bitcast.30), calls=%async_computation.3 | async-start | bytes 1048576 | tf_op jit(solution)/shard_map/all_to_all | solution.py:407
  175.5 11.9 %collective-permute-start.35 = (f32[1,128]{1,0:T(1,128)S(1)}, f32[1,128]{1,0:T(1,128)S(1)}, u32[]{:S(2)}, u32[]{:S(2)}) collective-permute-start(f32[1,128]{1,0:T(1,128)S(1)} %get-tuple-element.107), channel_id=1, source_target_pairs={{0,64},{64,128},{128,192},{192,0},{1,65},{65,129},{129,193},{193,1... | collective-permute-start | bytes 1544 | tf_op jit(solution)/shard_map/ppermute | solution.py:416
  177.8 11.8 %collective-permute-start.36 = (f32[1,128]{1,0:T(1,128)S(1)}, f32[1,128]{1,0:T(1,128)S(1)}, u32[]{:S(2)}, u32[]{:S(2)}) collective-permute-start(f32[1,128]{1,0:T(1,128)S(1)} %get-tuple-element.105), channel_id=1, source_target_pairs={{0,128},{64,192},{128,0},{192,64},{1,129},{65,193},{129,1},{193,65... | collective-permute-start | bytes 1544 | tf_op jit(solution)/shard_map/ppermute | solution.py:416
  179.1 10.5 %collective-permute-start.37 = (f32[1,128]{1,0:T(1,128)S(1)}, f32[1,128]{1,0:T(1,128)S(1)}, u32[]{:S(2)}, u32[]{:S(2)}) collective-permute-start(f32[1,128]{1,0:T(1,128)S(1)} %get-tuple-element.106), channel_id=1, source_target_pairs={{0,192},{64,0},{128,64},{192,128},{1,193},{65,1},{129,65},{193,129... | collective-permute-start | bytes 1544 | tf_op jit(solution)/shard_map/ppermute | solution.py:416
  (10 other events, 12.5 us)
Sparse Core Ops, SparseCore 0:
  130.0 49.8 reduce-scatter.1

commit v2 on v0

--- a/solution.py
+++ b/solution.py
@@ -383,25 +383,25 @@
     ng_block, *ng_parts = reduce_scatter_tp(
         ids, in_weight, pg, swapped, part, "norm_grads"
     )
-    in_part = weight_grads(
-        ids, normed_x, normed_other, after(pg_x, mixed_pieces[0], ng_block), True, 0, 3, "in_w"
-    )
-    in_weight_grads = lax.psum_scatter(in_part, "zl", scatter_dimension=0, tiled=False).astype(F32)
-
     layer_out, m_send = call(
         out_body, [shape(256, 256), shape(4, 3, 256, 256)],
-        ids, after(out_weight, in_part), hidden_in, out_grads, *mixed_pieces,
+        ids, out_weight, hidden_in, out_grads, *mixed_pieces,
         scratch=[pltpu.VMEM((16, 256, 256), BF)],
         flops=2 * 256 * 4096 * 256, moved=4 * 2**20, name="layer_out",
     )
+    in_part = weight_grads(
+        ids, normed_x, normed_other, after(pg_x, m_send, ng_block), True, 0, 3, "in_w"
+    )
+    in_weight_grads = lax.psum_scatter(in_part, "zl", scatter_dimension=0, tiled=False).astype(F32)
+
     taps = call(
-        filter_grad_body, shape(16, 128, dtype=F32), mixed_in, halo, after(cg, m_send),
+        filter_grad_body, shape(16, 128, dtype=F32), mixed_in, halo, after(cg, in_part),
         smem=False, flops=2 * 256 * 256 * 256, name="tap_grads",
     )
     taps = taps.reshape(4, 4, 128)
     pick = lambda s: lax.dynamic_index_in_dim(taps, lax.rem(x + s, 4), 1, False)
     taps = pick(0) + sum(lax.ppermute(pick(s), "x", ring(4, s)) for s in (1, 2, 3))
-    mixed_x = lax.all_to_all(m_send, "x", 0, 0, tiled=True)
+    mixed_x = lax.all_to_all(after(m_send, pg_x), "x", 0, 0, tiled=True)
     mixed_other = lax.ppermute(after(mixed_x, taps, ng_parts[0]), "core", SWAP)
     out_part = weight_grads(ids, mixed_x, mixed_other, mixed_x, False, 2, 1, "out_w")
     out_recv = lax.all_to_all(out_part[:, 0], "zl", 0, 0, tiled=True)

time: 202 us -> 204 us (level)
  starting transfers between devices: 91.2 us -> 82.3 us
  waiting for transfers between devices: 47.7 us -> 52.4 us
  Pallas kernels: 26.5 us -> 30.1 us
  local copies, waits for them, and re-layouts: 13.6 us -> 16.2 us
    ppermute x2, starting transfers between devices: 8.13 us -> 11.8 us  [swap_products(): return lax.ppermute(first, 'core', SWAP)]
    pallas_call x16, Pallas kernels: 26.5 us -> 30.1 us  [call(): pl.pallas_call(body, out_shape=list(outs) if multi else outs, in_specs=sp...]
    unnamed x62 -> x50, local copies, waits for them, and re-layouts: 12.6 us -> 15.2 us
    ppermute x1, waiting for transfers between devices: 1.76 us -> 4.27 us  [per_device(): part = part + lax.ppermute(part, 'core', SWAP)]
    ppermute x3, starting transfers between devices: 7.48 us -> 5.05 us  [per_device(): lax.ppermute(pick(s), 'x', ring(4, s))]
  transfers between devices with their start and end apart: 43 -> 43, of which waited for: 13 -> 17; matrix products, arithmetic and copies ran while one was open for 4% -> 4% of each run, Pallas kernels for 10% -> 13%
where the time goes in v2:
time: 204 us; the launch traced here: 203 us
  starting transfers between devices  82.3 us (40%)
  waiting for transfers between devices  52.4 us (26%)
  Pallas kernels  30.1 us (15%)
  local copies, waits for them, and re-layouts  16.2 us (8%)
  between operations  14.4 us (7%)
  other arithmetic  7.82 us (4%)
    pallas_call x16, Pallas kernels, call(): pl.pallas_call(body, out_shape=list(outs) if multi else outs, in_specs=sp...  30.1 us
    ppermute x3, waiting for transfers between devices, per_device(): lax.ppermute(row(s), 'zl', ring(4, s))  19.5 us
    unnamed x50, local copies, waits for them, and re-layouts  15.2 us
    ppermute x6, waiting for transfers between devices, reduce_scatter_tp(): lax.ppermute(blocks[s], 'y', ring(4, s))  13.8 us
    ppermute x2, starting transfers between devices, swap_products(): return lax.ppermute(first, 'core', SWAP)  11.8 us
    ppermute x2, starting transfers between devices, reduce_scatter_tp(): return (blocks[0], near, lax.ppermute(far, 'zh', SWAP), riders)  7.59 us
    ppermute x6, starting transfers between devices, reduce_scatter_tp(): lax.ppermute(blocks[s], 'y', ring(4, s))  7.04 us
    ppermute x1, starting transfers between devices, per_device(): other = lax.ppermute(hidden_in, 'zh', SWAP)  6.91 us
  transfers between devices with their start and end apart: 43, of which 17 were waited for; matrix products, arithmetic and copies ran while one was open for 4% of the time, Pallas kernels for 13%

profile of v2, /device:TPU:1, one launch (start us, length us, event | category | flops | bytes accessed | tf_op | source)
XLA Modules:
  0.0 203.2 jit_solution(942520859387794820)
XLA Ops:
  7.3 1.6 copy-done.3
  8.9 0.9 copy-done.5
  9.8 1.0 mixed_grads_a.1
  10.8 3.3 %collective-permute-start = (bf16[2,4,256,256]{3,2,1,0:T(8,128)(2,1)S(1)}, bf16[2,4,256,256]{3,2,1,0:T(8,128)(2,1)S(1)}, u32[]{:S(2)}, u32[]{:S(2)}) collective-permute-start(bf16[2,4,256,256]{3,2,1,0:T(8,128)(2,1)S(1)} %mixed_grads_a.1), channel_id=1, source_target_pairs={{0,1},{1,0},{2,3},{3,2},{4,5},{5,4},{6,7},{7,6},{8,9},{9,8},{10,11... | collective-permute-start | bytes 3145736 | tf_op jit(solution)/shard_map/ppermute | solution.py:244
  14.1 1.0 collective-permute-start.4
  16.2 6.9 %collective-permute-start.1 = (bf16[256,256]{1,0:T(8,128)(2,1)S(1)}, bf16[256,256]{1,0:T(8,128)(2,1)S(1)}, u32[]{:S(2)}, u32[]{:S(2)}) collective-permute-start(bf16[256,256]{1,0:T(8,128)(2,1)S(1)} %copy-done.9), channel_id=1, source_target_pairs={{0,8},{8,0},{1,9},{9,1},{2,10},{10,2},{3,11},{11,3},{4,12},{12,4},... | collective-permute-start | bytes 393224 | tf_op jit(solution)/shard_map/ppermute | solution.py:339
  23.1 1.8 collective-permute-done.2
  24.9 1.1 collective-permute-done.1.rider_ref
  26.0 1.0 mixed_grads_b.1
  27.1 1.7 collective-permute-start.5
  28.7 1.6 collective-permute-start.6
  30.3 1.1 collective-permute-start.7
  31.4 2.2 %collective-permute-start.8 = (bf16[4,256,256]{2,1,0:T(8,128)(2,1)S(1)}, bf16[4,256,256]{2,1,0:T(8,128)(2,1)S(1)}, u32[]{:S(2)}, u32[]{:S(2)}) collective-permute-start(bf16[4,256,256]{2,1,0:T(8,128)(2,1)S(1)} %pad_maximum_fusion.1.a_ref), channel_id=1, source_target_pairs={{0,1},{1,0},{2,3},{3,2},{4,5},{5,4},{6,7},{7,6},{8,9},{9,8},{10,11... | collective-permute-start | bytes 1572872 | tf_op jit(solution)/shard_map/ppermute | solution.py:338
  33.6 3.7 %collective-permute-done.5.p1 = bf16[768,256]{1,0:T(8,128)(2,1)S(1)} collective-permute-done((bf16[768,256]{1,0:T(8,128)(2,1)S(1)}, bf16[768,256]{1,0:T(8,128)(2,1)S(1)}, u32[]{:S(2)}, u32[]{:S(2)}) %collective-permute-start.5) | collective-permute-done | bytes 393248 | tf_op jit(solution)/shard_map/ppermute | solution.py:255
  37.3 8.9 %collective-permute-done.6.p2 = bf16[768,256]{1,0:T(8,128)(2,1)S(1)} collective-permute-done((bf16[768,256]{1,0:T(8,128)(2,1)S(1)}, bf16[768,256]{1,0:T(8,128)(2,1)S(1)}, u32[]{:S(2)}, u32[]{:S(2)}) %collective-permute-start.6) | collective-permute-done | bytes 393248 | tf_op jit(solution)/shard_map/ppermute | solution.py:255
  46.2 1.1 collective-permute-done.7.p3
  47.4 0.9 mixed_grads_sum.1
  48.9 1.6 collective-permute-start.9
  50.5 5.9 %collective-permute-start.11 = (bf16[256,256]{1,0:T(8,128)(2,1)}, bf16[256,256]{1,0:T(8,128)(2,1)S(1)}, u32[]{:S(2)}, u32[]{:S(2)}) collective-permute-start(bf16[256,256]{1,0:T(8,128)(2,1)} %get-tuple-element.63), channel_id=1, source_target_pairs={{0,8},{8,0},{1,9},{9,1},{2,10},{10,2},{3,11},{11,3},{4,12},{12,4},... | collective-permute-start | bytes 393224 | tf_op jit(solution)/shard_map/ppermute | solution.py:264
  56.5 2.8 %copy-done = bf16[3,256,4096]{2,1,0:T(8,128)(2,1)S(1)} copy-done((bf16[3,256,4096]{2,1,0:T(8,128)(2,1)S(1)}, bf16[3,256,4096]{2,1,0:T(8,128)(2,1)}, u32[]{:S(2)}) %copy-start) | copy-done | bytes 6291480
  59.9 3.7 %project.1 = (bf16[3,256,256]{2,1,0:T(8,128)(2,1)S(1)}, bf16[256,256]{1,0:T(8,128)(2,1)S(1)}, bf16[256,128]{1,0:T(8,128)(2,1)S(1)}, f32[1,256]{1,0:T(1,128)S(1)}...) custom-call(s32[5]{0:T(128)S(1)} %copy-done.15, ...), custom_call_target="tpu_custom_call" | custom-call | flops 1610612736 | bytes 10485760 | tf_op jit(solution)/shard_map/project/pallas_call | solution.py:26
  63.6 3.1 %collective-permute-start.10 = (bf16[256,128]{1,0:T(8,128)(2,1)S(1)}, bf16[256,128]{1,0:T(8,128)(2,1)S(1)}, u32[]{:S(2)}, u32[]{:S(2)}) collective-permute-start(bf16[256,128]{1,0:T(8,128)(2,1)S(1)} %get-tuple-element.62), channel_id=1, source_target_pairs={{0,16},{16,32},{32,48},{48,64},{64,80},{80,96},{96,112},{112,128},... | collective-permute-start | bytes 196616 | tf_op jit(solution)/shard_map/ppermute | solution.py:359
  66.9 1.3 collective-permute-start.12
  68.2 1.1 taps.1
  70.0 1.9 collective-permute-done.12.halo_ref
  71.9 1.2 conv_back.1
  73.2 1.1 copy-done.8
  74.3 1.8 collective-permute-start.16
  76.1 2.3 %collective-permute-start.15 = (bf16[256,256]{1,0:T(8,128)(2,1)S(1)}, bf16[256,256]{1,0:T(8,128)(2,1)S(1)}, u32[]{:S(2)}, u32[]{:S(2)}) collective-permute-start(bf16[256,256]{1,0:T(8,128)(2,1)S(1)} %get-tuple-element.75), channel_id=1, source_target_pairs={{0,6},{2,0},{4,2},{6,4},{1,7},{3,1},{5,3},{7,5},{8,14},{10,8},{12,... | collective-permute-start | bytes 393224 | tf_op jit(solution)/shard_map/ppermute | solution.py:268
  79.0 3.1 %collective-permute-done.16 = bf16[256,256]{1,0:T(8,128)(2,1)} collective-permute-done((bf16[256,256]{1,0:T(8,128)(2,1)S(1)}, bf16[256,256]{1,0:T(8,128)(2,1)}, u32[]{:S(2)}, u32[]{:S(2)}) %collective-permute-start.16) | collective-permute-done | bytes 131104 | tf_op jit(solution)/shard_map/ppermute | solution.py:269
  82.2 2.3 %collective-permute-start.19 = (bf16[256,256]{1,0:T(8,128)(2,1)}, bf16[256,256]{1,0:T(8,128)(2,1)}, u32[]{:S(2)}, u32[]{:S(2)}) collective-permute-start(bf16[256,256]{1,0:T(8,128)(2,1)} %collective-permute-done.16), channel_id=1, source_target_pairs={{0,6},{2,0},{4,2},{6,4},{1,7},{3,1},{5,3},{7,5},{8,14},{10,8},{12,... | collective-permute-start | bytes 393224 | tf_op jit(solution)/shard_map/ppermute | solution.py:270
  84.5 4.1 %collective-permute-start.24 = (bf16[2,256,256]{2,1,0:T(8,128)(2,1)}, bf16[2,256,256]{2,1,0:T(8,128)(2,1)}, u32[]{:S(2)}, u32[]{:S(2)}) collective-permute-start(bf16[2,256,256]{2,1,0:T(8,128)(2,1)} %get-tuple-element.84), channel_id=1, source_target_pairs={{0,48},{16,0},{32,16},{48,32},{1,49},{17,1},{33,17},{49,33},{2,50}... | collective-permute-start | bytes 786440 | tf_op jit(solution)/shard_map/ppermute | solution.py:377
  90.7 4.4 %all-to-all-start = ((bf16[4,3,256,256]{3,2,1,0:T(8,128)(2,1)}), bf16[4,3,256,256]{3,2,1,0:T(8,128)(2,1)}, u32[]{:S(2)}, u32[]{:S(2)}) async-start(bf16[4,3,256,256]{3,2,1,0:T(8,128)(2,1)} %copy-done.8), calls=%async_computation | async-start | bytes 3145728 | tf_op jit(solution)/shard_map/all_to_all | solution.py:380
  95.1 1.1 pad_maximum_fusion.2.a_ref
  97.0 1.2 pad_maximum_fusion.3.b_ref
  98.6 2.2 %pad_maximum_fusion.mine_ref = bf16[4,2,256,256]{3,2,1,0:T(8,128)(2,1)} fusion(bf16[1,2,256,256]{3,2,1,0:T(8,128)(2,1)} %bitcast.22, bf16[1,2,256,256]{3,2,1,0:T(8,128)(2,1)} %bitcast.21, bf16[1,2,256,256]{3,2,1,0:T(8,128)(2,1)} %bitcast.20, bf16[1,2,256,256]{3,2,1,0:T(8,128)(2,1)S(1)} %bitcast.38), kind=kLoop, calls=%fused_computation | loop fusion | flops 1572864 | bytes 2097152 | tf_op jit(solution)/shard_map/stack | solution.py:378
  100.8 2.8 %copy-done.1 = bf16[3,256,4096]{2,1,0:T(8,128)(2,1)S(1)} copy-done((bf16[3,256,4096]{2,1,0:T(8,128)(2,1)S(1)}, bf16[3,256,4096]{2,1,0:T(8,128)(2,1)}, u32[]{:S(2)}) %copy-start.1) | copy-done | bytes 6291480
  103.6 2.5 %norm_grads_a.1 = bf16[2,4,256,256]{3,2,1,0:T(8,128)(2,1)} custom-call(s32[5]{0:T(128)S(1)} %copy-done.16, bf16[3,256,4096]{2,1,0:T(8,128)(2,1)S(1)} %copy-done.1, bf16[3,256,256]{2,1,0:T(8,128)(2,1)S(1)} %get-tuple-element.85.g_ref), custom_call_target="tpu_custom_call" | custom-call | flops 805306368 | bytes 3145728 | tf_op jit(solution)/shard_map/norm_grads_a/pallas_call | solution.py:26
  106.1 8.5 %collective-permute-start.25 = (bf16[2,4,256,256]{3,2,1,0:T(8,128)(2,1)}, bf16[2,4,256,256]{3,2,1,0:T(8,128)(2,1)}, u32[]{:S(2)}, u32[]{:S(2)}) collective-permute-start(bf16[2,4,256,256]{3,2,1,0:T(8,128)(2,1)} %norm_grads_a.1), channel_id=1, source_target_pairs={{0,1},{1,0},{2,3},{3,2},{4,5},{5,4},{6,7},{7,6},{8,9},{9,8},{10,11... | collective-permute-start | bytes 3145736 | tf_op jit(solution)/shard_map/ppermute | solution.py:244
  115.6 4.3 %collective-permute-done.26 = f32[1,256]{1,0:T(1,128)S(1)} collective-permute-done((f32[1,256]{1,0:T(1,128)S(1)}, f32[1,256]{1,0:T(1,128)S(1)}, u32[]{:S(2)}, u32[]{:S(2)}) %collective-permute-start.26) | collective-permute-done | bytes 1056 | tf_op jit(solution)/shard_map/ppermute | solution.py:382
  119.9 2.1 %layer_out.1 = (bf16[256,256]{1,0:T(8,128)(2,1)}, bf16[4,3,256,256]{3,2,1,0:T(8,128)(2,1)S(1)}) custom-call(s32[5]{0:T(128)S(1)} %copy-done.16, bf16[256,4096]{1,0:T(8,128)(2,1)S(1)} %copy-done.4, bf16[256,256]{1,0:T(8,128)(2,1)S(1)} %copy-done.9, bf16[256,256]{1,0:T(8,128)(2,1)S(1)} %copy-done.6, bf16[4,256,256]{2,1,0:T(8,128)(2,1)S(1)} %pad_maximum_fusion.2.a_ref, ...), custom_call_target="tpu_custom_call" | custom-call | flops 536870912 | bytes 4194304 | tf_op jit(solution)/shard_map/layer_out/pallas_call | solution.py:26
  122.0 1.2 copy-done.7
  123.2 4.2 %all-to-all-start.1 = ((bf16[4,3,256,256]{3,2,1,0:T(8,128)(2,1)}), bf16[4,3,256,256]{3,2,1,0:T(8,128)(2,1)S(1)}, u32[]{:S(2)}, u32[]{:S(2)}) async-start(bf16[4,3,256,256]{3,2,1,0:T(8,128)(2,1)} %copy-done.7), calls=%async_computation.2 | async-start | bytes 3145728 | tf_op jit(solution)/shard_map/all_to_all | solution.py:404
  127.4 2.8 %copy-done.2 = bf16[3,256,4096]{2,1,0:T(8,128)(2,1)S(1)} copy-done((bf16[3,256,4096]{2,1,0:T(8,128)(2,1)S(1)}, bf16[3,256,4096]{2,1,0:T(8,128)(2,1)}, u32[]{:S(2)}) %copy-start.2) | copy-done | bytes 6291480
  130.1 2.9 %norm_grads_b.1 = (bf16[528,256]{1,0:T(8,128)(2,1)S(1)}, bf16[528,256]{1,0:T(8,128)(2,1)}, bf16[528,256]{1,0:T(8,128)(2,1)}, bf16[528,256]{1,0:T(8,128)(2,1)S(1)}) custom-call(s32[5]{0:T(128)S(1)} %copy-done.16, bf16[3,256,4096]{2,1,0:T(8,128)(2,1)S(1)} %copy-done.2, bf16[3,256,256]{2,1,0:T(8,128)(2,1)S(1)} %get-tuple-element.85.g_ref, ...), custom_call_target="tpu_custom_call" | custom-call | flops 805306368 | bytes 3145728 | tf_op jit(solution)/shard_map/norm_grads_b/pallas_call | solution.py:26
  133.1 5.1 %in_w.1 = bf16[4,3,256,256]{3,2,1,0:T(8,128)(2,1)} custom-call(s32[5]{0:T(128)S(1)} %copy-done.16, bf16[4,2,256,256]{3,2,1,0:T(8,128)(2,1)} %pad_maximum_fusion.mine_ref, bf16[4,2,256,256]{3,2,1,0:T(8,128)(2,1)} %collective-permute-done.31.other_ref, bf16[4,3,256,256]{3,2,1,0:T(8,128)(2,1)} %all-to-all-done.g_ref), custom_call_target="tpu_custom_call" | custom-call | flops 1610612736 | bytes 3145728 | tf_op jit(solution)/shard_map/in_w/pallas_call | solution.py:26
  138.3 0.8 collective-permute-start.28
  139.2 1.8 collective-permute-start.29
  141.0 4.5 %tap_grads.1 = f32[16,128]{1,0:T(8,128)S(1)} custom-call(bf16[256,256]{1,0:T(8,128)(2,1)S(1)} %get-tuple-element.61.x_ref, bf16[256,128]{1,0:T(8,128)(2,1)S(1)} %collective-permute-done.10.halo_ref, bf16[256,256]{1,0:T(8,128)(2,1)S(1)} %get-tuple-element.98.g_ref), custom_call_target="tpu_custom_call" | custom-call | flops 33554432 | tf_op jit(solution)/shard_map/tap_grads/pallas_call | solution.py:26
  145.5 2.8 %collective-permute-start.34 = (f32[4,128]{1,0:T(4,128)S(1)}, f32[4,128]{1,0:T(4,128)S(1)}, u32[]{:S(2)}, u32[]{:S(2)}) collective-permute-start(f32[4,128]{1,0:T(4,128)S(1)} %bitcast.51), channel_id=1, source_target_pairs={{0,48},{16,0},{32,16},{48,32},{1,49},{17,1},{33,17},{49,33},{2,50}... | collective-permute-start | bytes 6152 | tf_op jit(solution)/shard_map/ppermute | solution.py:403
  149.0 2.3 %collective-permute-start.33 = (f32[4,128]{1,0:T(4,128)S(1)}, f32[4,128]{1,0:T(4,128)S(1)}, u32[]{:S(2)}, u32[]{:S(2)}) collective-permute-start(f32[4,128]{1,0:T(4,128)S(1)} %bitcast.49), channel_id=1, source_target_pairs={{0,32},{16,48},{32,0},{48,16},{1,33},{17,49},{33,1},{49,17},{2,34}... | collective-permute-start | bytes 6152 | tf_op jit(solution)/shard_map/ppermute | solution.py:403
  151.3 0.9 collective-permute-done.32
  152.2 1.1 collective-permute-done.33
  153.5 3.2 %collective-permute-start.38 = (bf16[4,3,256,256]{3,2,1,0:T(8,128)(2,1)S(1)}, bf16[4,3,256,256]{3,2,1,0:T(8,128)(2,1)S(1)}, u32[]{:S(2)}, u32[]{:S(2)}) collective-permute-start(bf16[4,3,256,256]{3,2,1,0:T(8,128)(2,1)S(1)} %all-to-all-done.1.mine_ref.g_ref), channel_id=1, source_target_pairs={{0,1},{1,0},{2,3},{3,2},{4,5},{5,4},{6,7},{7,6},{8,9},{9,8},{10,11... | collective-permute-start | bytes 4718600 | tf_op jit(solution)/shard_map/ppermute | solution.py:405
  156.7 3.0 %collective-permute-done.38.other_ref = bf16[4,3,256,256]{3,2,1,0:T(8,128)(2,1)S(1)} collective-permute-done((bf16[4,3,256,256]{3,2,1,0:T(8,128)(2,1)S(1)}, bf16[4,3,256,256]{3,2,1,0:T(8,128)(2,1)S(1)}, u32[]{:S(2)}, u32[]{:S(2)}) %collective-permute-start.38) | collective-permute-done | bytes 1572896 | tf_op jit(solution)/shard_map/ppermute | solution.py:405
  159.8 2.1 %out_w.1 = bf16[4,1,256,256]{3,2,1,0:T(8,128)(2,1)} custom-call(s32[5]{0:T(128)S(1)} %copy-done.16, bf16[4,3,256,256]{3,2,1,0:T(8,128)(2,1)S(1)} %all-to-all-done.1.mine_ref.g_ref, bf16[4,3,256,256]{3,2,1,0:T(8,128)(2,1)S(1)} %collective-permute-done.38.other_ref, bf16[4,3,256,256]{3,2,1,0:T(8,128)(2,1)S(1)} %all-to-all-done.1.mine_ref.g_ref), custom_call_target="tpu_custom_call" | custom-call | flops 536870912 | bytes 1048576 | tf_op jit(solution)/shard_map/out_w/pallas_call | solution.py:26
  161.9 4.4 %all-to-all-start.2 = ((bf16[4,256,256]{2,1,0:T(8,128)(2,1)}), bf16[4,256,256]{2,1,0:T(8,128)(2,1)S(1)}, u32[]{:S(2)}, u32[]{:S(2)}) async-start(bf16[4,256,256]{2,1,0:T(8,128)(2,1)} %bitcast.30), calls=%async_computation.3 | async-start | bytes 1048576 | tf_op jit(solution)/shard_map/all_to_all | solution.py:407
  166.2 3.3 %collective-permute-start.37 = (f32[1,128]{1,0:T(1,128)S(1)}, f32[1,128]{1,0:T(1,128)S(1)}, u32[]{:S(2)}, u32[]{:S(2)}) collective-permute-start(f32[1,128]{1,0:T(1,128)S(1)} %get-tuple-element.106), channel_id=1, source_target_pairs={{0,192},{64,0},{128,64},{192,128},{1,193},{65,1},{129,65},{193,129... | collective-permute-start | bytes 1544 | tf_op jit(solution)/shard_map/ppermute | solution.py:416
  171.1 1.6 collective-permute-start.30
  172.7 8.0 %collective-permute-done.37 = f32[1,128]{1,0:T(1,128)S(1)} collective-permute-done((f32[1,128]{1,0:T(1,128)S(1)}, f32[1,128]{1,0:T(1,128)S(1)}, u32[]{:S(2)}, u32[]{:S(2)}) %collective-permute-start.37) | collective-permute-done | bytes 544 | tf_op jit(solution)/shard_map/ppermute | solution.py:416
  180.7 4.0 %collective-permute-done.35 = f32[1,128]{1,0:T(1,128)S(1)} collective-permute-done((f32[1,128]{1,0:T(1,128)S(1)}, f32[1,128]{1,0:T(1,128)S(1)}, u32[]{:S(2)}, u32[]{:S(2)}) %collective-permute-start.35) | collective-permute-done | bytes 544 | tf_op jit(solution)/shard_map/ppermute | solution.py:416
  184.6 7.6 %collective-permute-done.36 = f32[1,128]{1,0:T(1,128)S(1)} collective-permute-done((f32[1,128]{1,0:T(1,128)S(1)}, f32[1,128]{1,0:T(1,128)S(1)}, u32[]{:S(2)}, u32[]{:S(2)}) %collective-permute-start.36) | collective-permute-done | bytes 544 | tf_op jit(solution)/shard_map/ppermute | solution.py:416
  192.7 0.9 hidden_grads.1
  193.6 1.9 bitcast_convert_fusion
  (104 shorter events, 12.1 us)
Async XLA Ops:
  7.3 18.8 %copy-start.14 = (s32[5]{0:T(128)}, s32[5]{0:T(128)S(1)}, u32[]{:S(2)}) copy-start(s32[5]{0:T(128)S(1)} %stack.83.ids) | copy-start | bytes 64
  7.3 1.6 copy-start.3
  9.8 4.3 %copy-start.9 = (bf16[256,256]{1,0:T(8,128)(2,1)S(1)}, bf16[256,256]{1,0:T(8,128)(2,1)}, u32[]{:S(2)}) copy-start(bf16[256,256]{1,0:T(8,128)(2,1)} %hid_ref.3) | copy-start | bytes 393220
  9.8 16.3 %copy-start.4 = (bf16[256,4096]{1,0:T(8,128)(2,1)S(1)}, bf16[256,4096]{1,0:T(8,128)(2,1)}, u32[]{:S(2)}) copy-start(bf16[256,4096]{1,0:T(8,128)(2,1)} %w_ref.5) | copy-start | bytes 6291460
  9.8 16.3 %copy-start.6 = (bf16[256,256]{1,0:T(8,128)(2,1)S(1)}, bf16[256,256]{1,0:T(8,128)(2,1)}, u32[]{:S(2)}) copy-start(bf16[256,256]{1,0:T(8,128)(2,1)} %og_ref.3) | copy-start | bytes 393220
  10.8 15.2 %collective-permute-start = (bf16[2,4,256,256]{3,2,1,0:T(8,128)(2,1)S(1)}, bf16[2,4,256,256]{3,2,1,0:T(8,128)(2,1)S(1)}, u32[]{:S(2)}, u32[]{:S(2)}) collective-permute-start(bf16[2,4,256,256]{3,2,1,0:T(8,128)(2,1)S(1)} %mixed_grads_a.1), channel_id=1, source_target_pairs={{0,1},{1,0},{2,3},{3,2},{4,5},{5,4},{6,7},{7,6},{8,9},{9,8},{10,11... | collective-permute-start | bytes 3145736 | tf_op jit(solution)/shard_map/ppermute | solution.py:244
  14.1 9.0 %collective-permute-start.4 = (bf16[256,256]{1,0:T(8,128)(2,1)S(1)}, bf16[256,256]{1,0:T(8,128)(2,1)S(1)}, u32[]{:S(2)}, u32[]{:S(2)}) collective-permute-start(bf16[256,256]{1,0:T(8,128)(2,1)S(1)} %copy-done.9), channel_id=1, source_target_pairs={{0,6},{2,0},{4,2},{6,4},{1,7},{3,1},{5,3},{7,5},{8,14},{10,8},{12,... | collective-permute-start | bytes 393224 | tf_op jit(solution)/shard_map/ppermute | solution.py:337
  15.1 8.0 %collective-permute-start.3 = (bf16[256,256]{1,0:T(8,128)(2,1)S(1)}, bf16[256,256]{1,0:T(8,128)(2,1)S(1)}, u32[]{:S(2)}, u32[]{:S(2)}) collective-permute-start(bf16[256,256]{1,0:T(8,128)(2,1)S(1)} %copy-done.9), channel_id=1, source_target_pairs={{0,4},{2,6},{4,0},{6,2},{1,5},{3,7},{5,1},{7,3},{8,12},{10,14},{12... | collective-permute-start | bytes 393224 | tf_op jit(solution)/shard_map/ppermute | solution.py:337
  15.5 9.4 %collective-permute-start.2 = (bf16[256,256]{1,0:T(8,128)(2,1)S(1)}, bf16[256,256]{1,0:T(8,128)(2,1)S(1)}, u32[]{:S(2)}, u32[]{:S(2)}) collective-permute-start(bf16[256,256]{1,0:T(8,128)(2,1)S(1)} %copy-done.9), channel_id=1, source_target_pairs={{0,2},{2,4},{4,6},{6,0},{1,3},{3,5},{5,7},{7,1},{8,10},{10,12},{12... | collective-permute-start | bytes 393224 | tf_op jit(solution)/shard_map/ppermute | solution.py:337
  16.2 9.8 %collective-permute-start.1 = (bf16[256,256]{1,0:T(8,128)(2,1)S(1)}, bf16[256,256]{1,0:T(8,128)(2,1)S(1)}, u32[]{:S(2)}, u32[]{:S(2)}) collective-permute-start(bf16[256,256]{1,0:T(8,128)(2,1)S(1)} %copy-done.9), channel_id=1, source_target_pairs={{0,8},{8,0},{1,9},{9,1},{2,10},{10,2},{3,11},{11,3},{4,12},{12,4},... | collective-permute-start | bytes 393224 | tf_op jit(solution)/shard_map/ppermute | solution.py:339
  27.0 23.5 %copy-start.24 = (f32[4096]{0:T(1024)S(1)}, f32[4096]{0:T(1024)}, u32[]{:S(2)}) copy-start(f32[4096]{0:T(1024)} %param.7) | copy-start | bytes 49156
  27.1 10.3 %collective-permute-start.5 = (bf16[768,256]{1,0:T(8,128)(2,1)S(1)}, bf16[768,256]{1,0:T(8,128)(2,1)S(1)}, u32[]{:S(2)}, u32[]{:S(2)}) collective-permute-start(bf16[768,256]{1,0:T(8,128)(2,1)S(1)} %get-tuple-element.55), channel_id=1, source_target_pairs={{0,2},{2,4},{4,6},{6,0},{1,3},{3,5},{5,7},{7,1},{8,10},{10,12},{12... | collective-permute-start | bytes 1179656 | tf_op jit(solution)/shard_map/ppermute | solution.py:255
  28.7 17.5 %collective-permute-start.6 = (bf16[768,256]{1,0:T(8,128)(2,1)S(1)}, bf16[768,256]{1,0:T(8,128)(2,1)S(1)}, u32[]{:S(2)}, u32[]{:S(2)}) collective-permute-start(bf16[768,256]{1,0:T(8,128)(2,1)S(1)} %get-tuple-element.56), channel_id=1, source_target_pairs={{0,4},{2,6},{4,0},{6,2},{1,5},{3,7},{5,1},{7,3},{8,12},{10,14},{12... | collective-permute-start | bytes 1179656 | tf_op jit(solution)/shard_map/ppermute | solution.py:255
  30.3 17.1 %collective-permute-start.7 = (bf16[768,256]{1,0:T(8,128)(2,1)S(1)}, bf16[768,256]{1,0:T(8,128)(2,1)S(1)}, u32[]{:S(2)}, u32[]{:S(2)}) collective-permute-start(bf16[768,256]{1,0:T(8,128)(2,1)S(1)} %get-tuple-element.57), channel_id=1, source_target_pairs={{0,6},{2,0},{4,2},{6,4},{1,7},{3,1},{5,3},{7,5},{8,14},{10,8},{12,... | collective-permute-start | bytes 1179656 | tf_op jit(solution)/shard_map/ppermute | solution.py:255
  31.4 25.1 %collective-permute-start.8 = (bf16[4,256,256]{2,1,0:T(8,128)(2,1)S(1)}, bf16[4,256,256]{2,1,0:T(8,128)(2,1)S(1)}, u32[]{:S(2)}, u32[]{:S(2)}) collective-permute-start(bf16[4,256,256]{2,1,0:T(8,128)(2,1)S(1)} %pad_maximum_fusion.1.a_ref), channel_id=1, source_target_pairs={{0,1},{1,0},{2,3},{3,2},{4,5},{5,4},{6,7},{7,6},{8,9},{9,8},{10,11... | collective-permute-start | bytes 1572872 | tf_op jit(solution)/shard_map/ppermute | solution.py:338
  48.9 7.5 %collective-permute-start.9 = (bf16[4,256,256]{2,1,0:T(8,128)(2,1)}, bf16[4,256,256]{2,1,0:T(8,128)(2,1)}, u32[]{:S(2)}, u32[]{:S(2)}) collective-permute-start(bf16[4,256,256]{2,1,0:T(8,128)(2,1)} %get-tuple-element.60.b_ref), channel_id=1, source_target_pairs={{0,1},{1,0},{2,3},{3,2},{4,5},{5,4},{6,7},{7,6},{8,9},{9,8},{10,11... | collective-permute-start | bytes 1572872 | tf_op jit(solution)/shard_map/ppermute | solution.py:348
  50.5 16.3 %collective-permute-start.11 = (bf16[256,256]{1,0:T(8,128)(2,1)}, bf16[256,256]{1,0:T(8,128)(2,1)S(1)}, u32[]{:S(2)}, u32[]{:S(2)}) collective-permute-start(bf16[256,256]{1,0:T(8,128)(2,1)} %get-tuple-element.63), channel_id=1, source_target_pairs={{0,8},{8,0},{1,9},{9,1},{2,10},{10,2},{3,11},{11,3},{4,12},{12,4},... | collective-permute-start | bytes 393224 | tf_op jit(solution)/shard_map/ppermute | solution.py:264
  56.5 2.8 %copy-start = (bf16[3,256,4096]{2,1,0:T(8,128)(2,1)S(1)}, bf16[3,256,4096]{2,1,0:T(8,128)(2,1)}, u32[]{:S(2)}) copy-start(bf16[3,256,4096]{2,1,0:T(8,128)(2,1)} %w_ref.7) | copy-start | bytes 18874372
  59.9 6.9 %copy-start.13 = (bf16[256,256]{1,0:T(8,128)(2,1)S(1)}, bf16[256,256]{1,0:T(8,128)(2,1)}, u32[]{:S(2)}) copy-start(bf16[256,256]{1,0:T(8,128)(2,1)} %copy-done.12) | copy-start | bytes 393220
  59.9 8.3 %copy-start.17 = (f32[16,128]{1,0:T(8,128)S(1)}, f32[16,128]{1,0:T(8,128)}, u32[]{:S(2)}) copy-start(f32[16,128]{1,0:T(8,128)} %filt_ref) | copy-start | bytes 24580
  63.6 9.5 %copy-start.10 = (bf16[2,256,256]{2,1,0:T(8,128)(2,1)}, bf16[2,256,256]{2,1,0:T(8,128)(2,1)S(1)}, u32[]{:S(2)}) copy-start(bf16[2,256,256]{2,1,0:T(8,128)(2,1)S(1)} %get-tuple-element.78) | copy-start | bytes 786436
  63.6 9.5 %copy-start.18 = (f32[1,256]{1,0:T(1,128)}, f32[1,256]{1,0:T(1,128)S(1)}, u32[]{:S(2)}) copy-start(f32[1,256]{1,0:T(1,128)S(1)} %get-tuple-element.93.rms_ref) | copy-start | bytes 3076
  63.6 5.7 %collective-permute-start.10 = (bf16[256,128]{1,0:T(8,128)(2,1)S(1)}, bf16[256,128]{1,0:T(8,128)(2,1)S(1)}, u32[]{:S(2)}, u32[]{:S(2)}) collective-permute-start(bf16[256,128]{1,0:T(8,128)(2,1)S(1)} %get-tuple-element.62), channel_id=1, source_target_pairs={{0,16},{16,32},{32,48},{48,64},{64,80},{80,96},{96,112},{112,128},... | collective-permute-start | bytes 196616 | tf_op jit(solution)/shard_map/ppermute | solution.py:359
  66.9 5.0 %collective-permute-start.12 = (bf16[256,128]{1,0:T(8,128)(2,1)S(1)}, bf16[256,128]{1,0:T(8,128)(2,1)S(1)}, u32[]{:S(2)}, u32[]{:S(2)}) collective-permute-start(bf16[256,128]{1,0:T(8,128)(2,1)S(1)} %get-tuple-element.70), channel_id=1, source_target_pairs={{16,0},{32,16},{48,32},{64,48},{80,64},{96,80},{112,96},{128,112},... | collective-permute-start | bytes 196616 | tf_op jit(solution)/shard_map/ppermute | solution.py:364
  73.2 1.2 copy-start.8
  74.3 7.8 %collective-permute-start.16 = (bf16[256,256]{1,0:T(8,128)(2,1)S(1)}, bf16[256,256]{1,0:T(8,128)(2,1)}, u32[]{:S(2)}, u32[]{:S(2)}) collective-permute-start(bf16[256,256]{1,0:T(8,128)(2,1)S(1)} %get-tuple-element.75), channel_id=1, source_target_pairs={{0,8},{8,0},{1,9},{9,1},{2,10},{10,2},{3,11},{11,3},{4,12},{12,4},... | collective-permute-start | bytes 393224 | tf_op jit(solution)/shard_map/ppermute | solution.py:269
  76.1 12.5 %collective-permute-start.15 = (bf16[256,256]{1,0:T(8,128)(2,1)S(1)}, bf16[256,256]{1,0:T(8,128)(2,1)S(1)}, u32[]{:S(2)}, u32[]{:S(2)}) collective-permute-start(bf16[256,256]{1,0:T(8,128)(2,1)S(1)} %get-tuple-element.75), channel_id=1, source_target_pairs={{0,6},{2,0},{4,2},{6,4},{1,7},{3,1},{5,3},{7,5},{8,14},{10,8},{12,... | collective-permute-start | bytes 393224 | tf_op jit(solution)/shard_map/ppermute | solution.py:268
  78.4 10.2 %collective-permute-start.14 = (bf16[256,256]{1,0:T(8,128)(2,1)S(1)}, bf16[256,256]{1,0:T(8,128)(2,1)S(1)}, u32[]{:S(2)}, u32[]{:S(2)}) collective-permute-start(bf16[256,256]{1,0:T(8,128)(2,1)S(1)} %get-tuple-element.75), channel_id=1, source_target_pairs={{0,4},{2,6},{4,0},{6,2},{1,5},{3,7},{5,1},{7,3},{8,12},{10,14},{12... | collective-permute-start | bytes 393224 | tf_op jit(solution)/shard_map/ppermute | solution.py:268
  78.7 10.6 %collective-permute-start.13 = (bf16[256,256]{1,0:T(8,128)(2,1)S(1)}, bf16[256,256]{1,0:T(8,128)(2,1)S(1)}, u32[]{:S(2)}, u32[]{:S(2)}) collective-permute-start(bf16[256,256]{1,0:T(8,128)(2,1)S(1)} %get-tuple-element.75), channel_id=1, source_target_pairs={{0,2},{2,4},{4,6},{6,0},{1,3},{3,5},{5,7},{7,1},{8,10},{10,12},{12... | collective-permute-start | bytes 393224 | tf_op jit(solution)/shard_map/ppermute | solution.py:268
  82.2 8.1 %collective-permute-start.19 = (bf16[256,256]{1,0:T(8,128)(2,1)}, bf16[256,256]{1,0:T(8,128)(2,1)}, u32[]{:S(2)}, u32[]{:S(2)}) collective-permute-start(bf16[256,256]{1,0:T(8,128)(2,1)} %collective-permute-done.16), channel_id=1, source_target_pairs={{0,6},{2,0},{4,2},{6,4},{1,7},{3,1},{5,3},{7,5},{8,14},{10,8},{12,... | collective-permute-start | bytes 393224 | tf_op jit(solution)/shard_map/ppermute | solution.py:270
  84.5 13.6 %collective-permute-start.24 = (bf16[2,256,256]{2,1,0:T(8,128)(2,1)}, bf16[2,256,256]{2,1,0:T(8,128)(2,1)}, u32[]{:S(2)}, u32[]{:S(2)}) collective-permute-start(bf16[2,256,256]{2,1,0:T(8,128)(2,1)} %get-tuple-element.84), channel_id=1, source_target_pairs={{0,48},{16,0},{32,16},{48,32},{1,49},{17,1},{33,17},{49,33},{2,50}... | collective-permute-start | bytes 786440 | tf_op jit(solution)/shard_map/ppermute | solution.py:377
  88.6 2.1 %copy-start.21 = (bf16[256,256]{1,0:T(8,128)(2,1)}, bf16[256,256]{1,0:T(8,128)(2,1)S(1)}, u32[]{:S(2)}) copy-start(bf16[256,256]{1,0:T(8,128)(2,1)S(1)} %collective-permute-done.15) | copy-start | bytes 393220
  88.6 9.5 %collective-permute-start.23 = (bf16[2,256,256]{2,1,0:T(8,128)(2,1)}, bf16[2,256,256]{2,1,0:T(8,128)(2,1)}, u32[]{:S(2)}, u32[]{:S(2)}) collective-permute-start(bf16[2,256,256]{2,1,0:T(8,128)(2,1)} %get-tuple-element.82), channel_id=1, source_target_pairs={{0,32},{16,48},{32,0},{48,16},{1,33},{17,49},{33,1},{49,17},{2,34}... | collective-permute-start | bytes 786440 | tf_op jit(solution)/shard_map/ppermute | solution.py:377
  88.6 2.1 %copy-start.22 = (bf16[256,256]{1,0:T(8,128)(2,1)}, bf16[256,256]{1,0:T(8,128)(2,1)S(1)}, u32[]{:S(2)}) copy-start(bf16[256,256]{1,0:T(8,128)(2,1)S(1)} %collective-permute-done.14) | copy-start | bytes 393220
  88.6 10.0 %collective-permute-start.22 = (bf16[2,256,256]{2,1,0:T(8,128)(2,1)}, bf16[2,256,256]{2,1,0:T(8,128)(2,1)}, u32[]{:S(2)}, u32[]{:S(2)}) collective-permute-start(bf16[2,256,256]{2,1,0:T(8,128)(2,1)} %get-tuple-element.80), channel_id=1, source_target_pairs={{0,16},{16,32},{32,48},{48,0},{1,17},{17,33},{33,49},{49,1},{2,18}... | collective-permute-start | bytes 786440 | tf_op jit(solution)/shard_map/ppermute | solution.py:377
  89.9 6.3 %collective-permute-start.18 = (bf16[256,256]{1,0:T(8,128)(2,1)}, bf16[256,256]{1,0:T(8,128)(2,1)}, u32[]{:S(2)}, u32[]{:S(2)}) collective-permute-start(bf16[256,256]{1,0:T(8,128)(2,1)} %collective-permute-done.16), channel_id=1, source_target_pairs={{0,4},{2,6},{4,0},{6,2},{1,5},{3,7},{5,1},{7,3},{8,12},{10,14},{12... | collective-permute-start | bytes 393224 | tf_op jit(solution)/shard_map/ppermute | solution.py:270
  90.2 6.7 %collective-permute-start.17 = (bf16[256,256]{1,0:T(8,128)(2,1)}, bf16[256,256]{1,0:T(8,128)(2,1)}, u32[]{:S(2)}, u32[]{:S(2)}) collective-permute-start(bf16[256,256]{1,0:T(8,128)(2,1)} %collective-permute-done.16), channel_id=1, source_target_pairs={{0,2},{2,4},{4,6},{6,0},{1,3},{3,5},{5,7},{7,1},{8,10},{10,12},{12... | collective-permute-start | bytes 393224 | tf_op jit(solution)/shard_map/ppermute | solution.py:270
  90.7 32.4 %all-to-all-start = ((bf16[4,3,256,256]{3,2,1,0:T(8,128)(2,1)}), bf16[4,3,256,256]{3,2,1,0:T(8,128)(2,1)}, u32[]{:S(2)}, u32[]{:S(2)}) async-start(bf16[4,3,256,256]{3,2,1,0:T(8,128)(2,1)} %copy-done.8), calls=%async_computation | async-start | bytes 3145728 | tf_op jit(solution)/shard_map/all_to_all | solution.py:380
  95.1 3.5 %copy-start.11 = (bf16[2,256,256]{2,1,0:T(8,128)(2,1)S(1)}, bf16[2,256,256]{2,1,0:T(8,128)(2,1)}, u32[]{:S(2)}) copy-start(bf16[2,256,256]{2,1,0:T(8,128)(2,1)} %copy-done.10) | copy-start | bytes 786436
  97.0 3.8 %copy-start.16 = (s32[5]{0:T(128)S(1)}, s32[5]{0:T(128)}, u32[]{:S(2)}) copy-start(s32[5]{0:T(128)} %copy-done.14) | copy-start | bytes 64
  100.8 2.8 %copy-start.1 = (bf16[3,256,4096]{2,1,0:T(8,128)(2,1)S(1)}, bf16[3,256,4096]{2,1,0:T(8,128)(2,1)}, u32[]{:S(2)}) copy-start(bf16[3,256,4096]{2,1,0:T(8,128)(2,1)} %w_ref.7) | copy-start | bytes 18874372
  106.1 21.2 %collective-permute-start.25 = (bf16[2,4,256,256]{3,2,1,0:T(8,128)(2,1)}, bf16[2,4,256,256]{3,2,1,0:T(8,128)(2,1)}, u32[]{:S(2)}, u32[]{:S(2)}) collective-permute-start(bf16[2,4,256,256]{3,2,1,0:T(8,128)(2,1)} %norm_grads_a.1), channel_id=1, source_target_pairs={{0,1},{1,0},{2,3},{3,2},{4,5},{5,4},{6,7},{7,6},{8,9},{9,8},{10,11... | collective-permute-start | bytes 3145736 | tf_op jit(solution)/shard_map/ppermute | solution.py:244
  114.6 18.5 %collective-permute-start.31 = (bf16[4,2,256,256]{3,2,1,0:T(8,128)(2,1)}, bf16[4,2,256,256]{3,2,1,0:T(8,128)(2,1)}, u32[]{:S(2)}, u32[]{:S(2)}) collective-permute-start(bf16[4,2,256,256]{3,2,1,0:T(8,128)(2,1)} %pad_maximum_fusion.mine_ref), channel_id=1, source_target_pairs={{0,1},{1,0},{2,3},{3,2},{4,5},{5,4},{6,7},{7,6},{8,9},{9,8},{10,11... | collective-permute-start | bytes 3145736 | tf_op jit(solution)/shard_map/ppermute | solution.py:379
  114.6 5.3 %collective-permute-start.20 = (bf16[4,256,256]{2,1,0:T(8,128)(2,1)S(1)}, bf16[4,256,256]{2,1,0:T(8,128)(2,1)S(1)}, u32[]{:S(2)}, u32[]{:S(2)}) collective-permute-start(bf16[4,256,256]{2,1,0:T(8,128)(2,1)S(1)} %pad_maximum_fusion.2.a_ref), channel_id=1, source_target_pairs={{0,1},{1,0},{2,3},{3,2},{4,5},{5,4},{6,7},{7,6},{8,9},{9,8},{10,11... | collective-permute-start | bytes 1572872 | tf_op jit(solution)/shard_map/ppermute | solution.py:273
  115.1 4.8 %collective-permute-start.21 = (bf16[4,256,256]{2,1,0:T(8,128)(2,1)S(1)}, bf16[4,256,256]{2,1,0:T(8,128)(2,1)S(1)}, u32[]{:S(2)}, u32[]{:S(2)}) collective-permute-start(bf16[4,256,256]{2,1,0:T(8,128)(2,1)S(1)} %pad_maximum_fusion.3.b_ref), channel_id=1, source_target_pairs={{0,1},{1,0},{2,3},{3,2},{4,5},{5,4},{6,7},{7,6},{8,9},{9,8},{10,11... | collective-permute-start | bytes 1572872 | tf_op jit(solution)/shard_map/ppermute | solution.py:273
  115.1 4.8 %collective-permute-start.26 = (f32[1,256]{1,0:T(1,128)S(1)}, f32[1,256]{1,0:T(1,128)S(1)}, u32[]{:S(2)}, u32[]{:S(2)}) collective-permute-start(f32[1,256]{1,0:T(1,128)S(1)} %get-tuple-element.86), channel_id=1, source_target_pairs={{0,1},{1,0},{2,3},{3,2},{4,5},{5,4},{6,7},{7,6},{8,9},{9,8},{10,11... | collective-permute-start | bytes 3080 | tf_op jit(solution)/shard_map/ppermute | solution.py:382
  122.0 1.2 copy-start.7
  123.2 30.4 %all-to-all-start.1 = ((bf16[4,3,256,256]{3,2,1,0:T(8,128)(2,1)}), bf16[4,3,256,256]{3,2,1,0:T(8,128)(2,1)S(1)}, u32[]{:S(2)}, u32[]{:S(2)}) async-start(bf16[4,3,256,256]{3,2,1,0:T(8,128)(2,1)} %copy-done.7), calls=%async_computation.2 | async-start | bytes 3145728 | tf_op jit(solution)/shard_map/all_to_all | solution.py:404
  127.3 66.3 %reduce-scatter.2.cloned.1.call-start = ((), (), s32[]{:S(2)}) async-start(), calls=%async_computation.4 | async-start | bytes 1966080 | tf_op jit(solution)/shard_map/reduce_scatter | solution.py:395
  127.3 2.8 %copy-start.2 = (bf16[3,256,4096]{2,1,0:T(8,128)(2,1)S(1)}, bf16[3,256,4096]{2,1,0:T(8,128)(2,1)}, u32[]{:S(2)}) copy-start(bf16[3,256,4096]{2,1,0:T(8,128)(2,1)} %w_ref.7) | copy-start | bytes 18874372
  133.1 5.2 %copy-start.20 = (bf16[528,256]{1,0:T(8,128)(2,1)}, bf16[528,256]{1,0:T(8,128)(2,1)S(1)}, u32[]{:S(2)}) copy-start(bf16[528,256]{1,0:T(8,128)(2,1)S(1)} %get-tuple-element.90) | copy-start | bytes 811012
  138.2 15.1 %collective-permute-start.27 = (bf16[528,256]{1,0:T(8,128)(2,1)}, bf16[528,256]{1,0:T(8,128)(2,1)S(1)}, u32[]{:S(2)}, u32[]{:S(2)}) collective-permute-start(bf16[528,256]{1,0:T(8,128)(2,1)} %get-tuple-element.88), channel_id=1, source_target_pairs={{0,2},{2,4},{4,6},{6,0},{1,3},{3,5},{5,7},{7,1},{8,10},{10,12},{12... | collective-permute-start | bytes 811016 | tf_op jit(solution)/shard_map/ppermute | solution.py:255
  138.3 15.0 %collective-permute-start.28 = (bf16[528,256]{1,0:T(8,128)(2,1)}, bf16[528,256]{1,0:T(8,128)(2,1)S(1)}, u32[]{:S(2)}, u32[]{:S(2)}) collective-permute-start(bf16[528,256]{1,0:T(8,128)(2,1)} %get-tuple-element.89), channel_id=1, source_target_pairs={{0,4},{2,6},{4,0},{6,2},{1,5},{3,7},{5,1},{7,3},{8,12},{10,14},{12... | collective-permute-start | bytes 811016 | tf_op jit(solution)/shard_map/ppermute | solution.py:255
  139.2 14.2 %collective-permute-start.29 = (bf16[528,256]{1,0:T(8,128)(2,1)}, bf16[528,256]{1,0:T(8,128)(2,1)S(1)}, u32[]{:S(2)}, u32[]{:S(2)}) collective-permute-start(bf16[528,256]{1,0:T(8,128)(2,1)} %copy-done.20), channel_id=1, source_target_pairs={{0,6},{2,0},{4,2},{6,4},{1,7},{3,1},{5,3},{7,5},{8,14},{10,8},{12,... | collective-permute-start | bytes 811016 | tf_op jit(solution)/shard_map/ppermute | solution.py:255
  145.5 3.5 %collective-permute-start.34 = (f32[4,128]{1,0:T(4,128)S(1)}, f32[4,128]{1,0:T(4,128)S(1)}, u32[]{:S(2)}, u32[]{:S(2)}) collective-permute-start(f32[4,128]{1,0:T(4,128)S(1)} %bitcast.51), channel_id=1, source_target_pairs={{0,48},{16,0},{32,16},{48,32},{1,49},{17,1},{33,17},{49,33},{2,50}... | collective-permute-start | bytes 6152 | tf_op jit(solution)/shard_map/ppermute | solution.py:403
  148.3 3.9 %collective-permute-start.32 = (f32[4,128]{1,0:T(4,128)S(1)}, f32[4,128]{1,0:T(4,128)S(1)}, u32[]{:S(2)}, u32[]{:S(2)}) collective-permute-start(f32[4,128]{1,0:T(4,128)S(1)} %bitcast.50), channel_id=1, source_target_pairs={{0,16},{16,32},{32,48},{48,0},{1,17},{17,33},{33,49},{49,1},{2,18}... | collective-permute-start | bytes 6152 | tf_op jit(solution)/shard_map/ppermute | solution.py:403
  149.0 4.3 %collective-permute-start.33 = (f32[4,128]{1,0:T(4,128)S(1)}, f32[4,128]{1,0:T(4,128)S(1)}, u32[]{:S(2)}, u32[]{:S(2)}) collective-permute-start(f32[4,128]{1,0:T(4,128)S(1)} %bitcast.49), channel_id=1, source_target_pairs={{0,32},{16,48},{32,0},{48,16},{1,33},{17,49},{33,1},{49,17},{2,34}... | collective-permute-start | bytes 6152 | tf_op jit(solution)/shard_map/ppermute | solution.py:403
  153.5 39.2 %copy-start.19 = (f32[1,256]{1,0:T(1,128)S(1)}, f32[1,256]{1,0:T(1,128)}, u32[]{:S(2)}) copy-start(f32[1,256]{1,0:T(1,128)} %copy-done.18) | copy-start | bytes 3076
  153.5 6.2 %collective-permute-start.38 = (bf16[4,3,256,256]{3,2,1,0:T(8,128)(2,1)S(1)}, bf16[4,3,256,256]{3,2,1,0:T(8,128)(2,1)S(1)}, u32[]{:S(2)}, u32[]{:S(2)}) collective-permute-start(bf16[4,3,256,256]{3,2,1,0:T(8,128)(2,1)S(1)} %all-to-all-done.1.mine_ref.g_ref), channel_id=1, source_target_pairs={{0,1},{1,0},{2,3},{3,2},{4,5},{5,4},{6,7},{7,6},{8,9},{9,8},{10,11... | collective-permute-start | bytes 4718600 | tf_op jit(solution)/shard_map/ppermute | solution.py:405
  161.9 33.7 %all-to-all-start.2 = ((bf16[4,256,256]{2,1,0:T(8,128)(2,1)}), bf16[4,256,256]{2,1,0:T(8,128)(2,1)S(1)}, u32[]{:S(2)}, u32[]{:S(2)}) async-start(bf16[4,256,256]{2,1,0:T(8,128)(2,1)} %bitcast.30), calls=%async_computation.3 | async-start | bytes 1048576 | tf_op jit(solution)/shard_map/all_to_all | solution.py:407
  166.2 14.4 %collective-permute-start.37 = (f32[1,128]{1,0:T(1,128)S(1)}, f32[1,128]{1,0:T(1,128)S(1)}, u32[]{:S(2)}, u32[]{:S(2)}) collective-permute-start(f32[1,128]{1,0:T(1,128)S(1)} %get-tuple-element.106), channel_id=1, source_target_pairs={{0,192},{64,0},{128,64},{192,128},{1,193},{65,1},{129,65},{193,129... | collective-permute-start | bytes 1544 | tf_op jit(solution)/shard_map/ppermute | solution.py:416
  169.6 15.1 %collective-permute-start.35 = (f32[1,128]{1,0:T(1,128)S(1)}, f32[1,128]{1,0:T(1,128)S(1)}, u32[]{:S(2)}, u32[]{:S(2)}) collective-permute-start(f32[1,128]{1,0:T(1,128)S(1)} %get-tuple-element.107), channel_id=1, source_target_pairs={{0,64},{64,128},{128,192},{192,0},{1,65},{65,129},{129,193},{193,1... | collective-permute-start | bytes 1544 | tf_op jit(solution)/shard_map/ppermute | solution.py:416
  169.6 22.6 %collective-permute-start.36 = (f32[1,128]{1,0:T(1,128)S(1)}, f32[1,128]{1,0:T(1,128)S(1)}, u32[]{:S(2)}, u32[]{:S(2)}) collective-permute-start(f32[1,128]{1,0:T(1,128)S(1)} %get-tuple-element.105), channel_id=1, source_target_pairs={{0,128},{64,192},{128,0},{192,64},{1,129},{65,193},{129,1},{193,65... | collective-permute-start | bytes 1544 | tf_op jit(solution)/shard_map/ppermute | solution.py:416
  171.1 21.7 %collective-permute-start.30 = (bf16[272,256]{1,0:T(8,128)(2,1)S(1)}, bf16[272,256]{1,0:T(8,128)(2,1)S(1)}, u32[]{:S(2)}, u32[]{:S(2)}) collective-permute-start(bf16[272,256]{1,0:T(8,128)(2,1)S(1)} %get-tuple-element.92), channel_id=1, source_target_pairs={{0,8},{8,0},{1,9},{9,1},{2,10},{10,2},{3,11},{11,3},{4,12},{12,4},... | collective-permute-start | bytes 417800 | tf_op jit(solution)/shard_map/ppermute | solution.py:264
  (4 other events, 2.8 us)
Sparse Core Ops, SparseCore 0:
  138.3 40.6 reduce-scatter.1

commit v3 on v2

--- a/solution.py
+++ b/solution.py
@@ -379,10 +379,6 @@
     normed_other = lax.ppermute(normed_x, "core", SWAP)
     pg_x = lax.all_to_all(pg_all, "x", 0, 0, tiled=True)
     swapped = swap_products(ids, in_weight, after(pg, normed_x), "norm_grads")
-    part = part + lax.ppermute(part, "core", SWAP)
-    ng_block, *ng_parts = reduce_scatter_tp(
-        ids, in_weight, pg, swapped, part, "norm_grads"
-    )
     layer_out, m_send = call(
         out_body, [shape(256, 256), shape(4, 3, 256, 256)],
         ids, out_weight, hidden_in, out_grads, *mixed_pieces,
@@ -390,10 +386,14 @@
         flops=2 * 256 * 4096 * 256, moved=4 * 2**20, name="layer_out",
     )
     in_part = weight_grads(
-        ids, normed_x, normed_other, after(pg_x, m_send, ng_block), True, 0, 3, "in_w"
+        ids, normed_x, normed_other, after(pg_x, m_send, swapped), True, 0, 3, "in_w"
     )
     in_weight_grads = lax.psum_scatter(in_part, "zl", scatter_dimension=0, tiled=False).astype(F32)
 
+    part = part + lax.ppermute(part, "core", SWAP)
+    ng_block, *ng_parts = reduce_scatter_tp(
+        ids, in_weight, pg, after(swapped, in_part), part, "norm_grads"
+    )
     taps = call(
         filter_grad_body, shape(16, 128, dtype=F32), mixed_in, halo, after(cg, in_part),
         smem=False, flops=2 * 256 * 256 * 256, name="tap_grads",
@@ -401,7 +401,7 @@
     taps = taps.reshape(4, 4, 128)
     pick = lambda s: lax.dynamic_index_in_dim(taps, lax.rem(x + s, 4), 1, False)
     taps = pick(0) + sum(lax.ppermute(pick(s), "x", ring(4, s)) for s in (1, 2, 3))
-    mixed_x = lax.all_to_all(after(m_send, pg_x), "x", 0, 0, tiled=True)
+    mixed_x = lax.all_to_all(after(m_send, in_part), "x", 0, 0, tiled=True)
     mixed_other = lax.ppermute(after(mixed_x, taps, ng_parts[0]), "core", SWAP)
     out_part = weight_grads(ids, mixed_x, mixed_other, mixed_x, False, 2, 1, "out_w")
     out_recv = lax.all_to_all(out_part[:, 0], "zl", 0, 0, tiled=True)

time: 204 us -> 201 us (0.985)
  waiting for transfers between devices: 52.4 us -> 46.3 us
  starting transfers between devices: 82.3 us -> 87.6 us
    ppermute x3, waiting for transfers between devices: 19.5 us -> 14.4 us  [per_device(): lax.ppermute(row(s), 'zl', ring(4, s))]
    ppermute x1, waiting for transfers between devices: 4.27 us -> 0.82 us  [per_device(): part = part + lax.ppermute(part, 'core', SWAP)]
    ppermute x1, waiting for transfers between devices: 0.01 us -> 3.27 us  [gather_tp(): lax.ppermute(near, 'core', SWAP)]
    ppermute x2, starting transfers between devices: 11.8 us -> 8.57 us  [swap_products(): return lax.ppermute(first, 'core', SWAP)]
    unnamed x50 -> x42, local copies, waits for them, and re-layouts: 15.2 us -> 14.4 us
  transfers between devices with their start and end apart: 43 -> 43, of which waited for: 17 -> 16; matrix products, arithmetic and copies ran while one was open for 4% -> 4% of each run, Pallas kernels for 13% -> 11%
where the time goes in v3:
time: 201 us; the launch traced here: 200 us
  starting transfers between devices  87.6 us (44%)
  waiting for transfers between devices  46.3 us (23%)
  Pallas kernels  28.4 us (14%)
  local copies, waits for them, and re-layouts  15.4 us (8%)
  between operations  14.4 us (7%)
  other arithmetic  7.69 us (4%)
    pallas_call x16, Pallas kernels, call(): pl.pallas_call(body, out_shape=list(outs) if multi else outs, in_specs=sp...  28.4 us
    unnamed x42, local copies, waits for them, and re-layouts  14.4 us
    ppermute x3, waiting for transfers between devices, per_device(): lax.ppermute(row(s), 'zl', ring(4, s))  14.4 us
    ppermute x6, waiting for transfers between devices, reduce_scatter_tp(): lax.ppermute(blocks[s], 'y', ring(4, s))  14 us
    ppermute x2, starting transfers between devices, swap_products(): return lax.ppermute(first, 'core', SWAP)  8.57 us
    ppermute x6, starting transfers between devices, reduce_scatter_tp(): lax.ppermute(blocks[s], 'y', ring(4, s))  8.43 us
    ppermute x2, starting transfers between devices, reduce_scatter_tp(): return (blocks[0], near, lax.ppermute(far, 'zh', SWAP), riders)  8.28 us
    ppermute x1, starting transfers between devices, per_device(): other = lax.ppermute(hidden_in, 'zh', SWAP)  6.91 us
  transfers between devices with their start and end apart: 43, of which 16 were waited for; matrix products, arithmetic and copies ran while one was open for 4% of the time, Pallas kernels for 11%

profile of v3, /device:TPU:1, one launch (start us, length us, event | category | flops | bytes accessed | tf_op | source)
XLA Modules:
  0.0 199.8 jit_solution(8726023185989782206)
XLA Ops:
  7.3 1.6 copy-done.3
  10.8 3.3 %collective-permute-start = (bf16[2,4,256,256]{3,2,1,0:T(8,128)(2,1)S(1)}, bf16[2,4,256,256]{3,2,1,0:T(8,128)(2,1)S(1)}, u32[]{:S(2)}, u32[]{:S(2)}) collective-permute-start(bf16[2,4,256,256]{3,2,1,0:T(8,128)(2,1)S(1)} %mixed_grads_a.1), channel_id=1, source_target_pairs={{0,1},{1,0},{2,3},{3,2},{4,5},{5,4},{6,7},{7,6},{8,9},{9,8},{10,11... | collective-permute-start | bytes 3145736 | tf_op jit(solution)/shard_map/ppermute | solution.py:244
  14.1 1.0 collective-permute-start.4
  15.6 1.2 collective-permute-start.3
  16.8 6.9 %collective-permute-start.1 = (bf16[256,256]{1,0:T(8,128)(2,1)S(1)}, bf16[256,256]{1,0:T(8,128)(2,1)S(1)}, u32[]{:S(2)}, u32[]{:S(2)}) collective-permute-start(bf16[256,256]{1,0:T(8,128)(2,1)S(1)} %copy-done.10), channel_id=1, source_target_pairs={{0,8},{8,0},{1,9},{9,1},{2,10},{10,2},{3,11},{11,3},{4,12},{12,4},... | collective-permute-start | bytes 393224 | tf_op jit(solution)/shard_map/ppermute | solution.py:339
  23.9 2.7 %collective-permute-done.1.rider_ref = bf16[256,256]{1,0:T(8,128)(2,1)S(1)} collective-permute-done((bf16[256,256]{1,0:T(8,128)(2,1)S(1)}, bf16[256,256]{1,0:T(8,128)(2,1)S(1)}, u32[]{:S(2)}, u32[]{:S(2)}) %collective-permute-start.1) | collective-permute-done | bytes 131104 | tf_op jit(solution)/shard_map/ppermute | solution.py:339
  27.7 1.7 collective-permute-start.5
  30.2 1.6 collective-permute-start.7
  31.8 2.2 %collective-permute-start.8 = (bf16[4,256,256]{2,1,0:T(8,128)(2,1)S(1)}, bf16[4,256,256]{2,1,0:T(8,128)(2,1)}, u32[]{:S(2)}, u32[]{:S(2)}) collective-permute-start(bf16[4,256,256]{2,1,0:T(8,128)(2,1)S(1)} %pad_maximum_fusion.1.a_ref), channel_id=1, source_target_pairs={{0,1},{1,0},{2,3},{3,2},{4,5},{5,4},{6,7},{7,6},{8,9},{9,8},{10,11... | collective-permute-start | bytes 1572872 | tf_op jit(solution)/shard_map/ppermute | solution.py:338
  34.0 4.0 %collective-permute-done.5.p1 = bf16[768,256]{1,0:T(8,128)(2,1)S(1)} collective-permute-done((bf16[768,256]{1,0:T(8,128)(2,1)S(1)}, bf16[768,256]{1,0:T(8,128)(2,1)S(1)}, u32[]{:S(2)}, u32[]{:S(2)}) %collective-permute-start.5) | collective-permute-done | bytes 393248 | tf_op jit(solution)/shard_map/ppermute | solution.py:255
  37.9 8.6 %collective-permute-done.6.p2 = bf16[768,256]{1,0:T(8,128)(2,1)S(1)} collective-permute-done((bf16[768,256]{1,0:T(8,128)(2,1)S(1)}, bf16[768,256]{1,0:T(8,128)(2,1)S(1)}, u32[]{:S(2)}, u32[]{:S(2)}) %collective-permute-start.6) | collective-permute-done | bytes 393248 | tf_op jit(solution)/shard_map/ppermute | solution.py:255
  46.5 1.4 collective-permute-done.7.p3
  48.8 1.6 collective-permute-start.9
  50.4 5.0 %collective-permute-start.11 = (bf16[256,256]{1,0:T(8,128)(2,1)S(1)}, bf16[256,256]{1,0:T(8,128)(2,1)S(1)}, u32[]{:S(2)}, u32[]{:S(2)}) collective-permute-start(bf16[256,256]{1,0:T(8,128)(2,1)S(1)} %get-tuple-element.64), channel_id=1, source_target_pairs={{0,8},{8,0},{1,9},{9,1},{2,10},{10,2},{3,11},{11,3},{4,12},{12,4},... | collective-permute-start | bytes 393224 | tf_op jit(solution)/shard_map/ppermute | solution.py:264
  55.4 2.8 %copy-done = bf16[3,256,4096]{2,1,0:T(8,128)(2,1)S(1)} copy-done((bf16[3,256,4096]{2,1,0:T(8,128)(2,1)S(1)}, bf16[3,256,4096]{2,1,0:T(8,128)(2,1)}, u32[]{:S(2)}) %copy-start) | copy-done | bytes 6291480
  58.2 3.9 %project.1 = (bf16[3,256,256]{2,1,0:T(8,128)(2,1)S(1)}, bf16[256,256]{1,0:T(8,128)(2,1)S(1)}, bf16[256,128]{1,0:T(8,128)(2,1)S(1)}, f32[1,256]{1,0:T(1,128)S(1)}...) custom-call(s32[5]{0:T(128)S(1)} %stack.83.ids, ...), custom_call_target="tpu_custom_call" | custom-call | flops 1610612736 | bytes 10485760 | tf_op jit(solution)/shard_map/project/pallas_call | solution.py:26
  62.1 3.1 %collective-permute-start.10 = (bf16[256,128]{1,0:T(8,128)(2,1)S(1)}, bf16[256,128]{1,0:T(8,128)(2,1)S(1)}, u32[]{:S(2)}, u32[]{:S(2)}) collective-permute-start(bf16[256,128]{1,0:T(8,128)(2,1)S(1)} %get-tuple-element.63), channel_id=1, source_target_pairs={{0,16},{16,32},{32,48},{48,64},{64,80},{80,96},{96,112},{112,128},... | collective-permute-start | bytes 196616 | tf_op jit(solution)/shard_map/ppermute | solution.py:359
  65.4 1.3 collective-permute-start.12
  66.7 1.1 taps.1
  68.5 1.9 collective-permute-done.12.halo_ref
  70.4 1.2 conv_back.1
  71.6 1.2 copy-done.9
  72.8 1.8 collective-permute-start.16
  74.6 1.4 collective-permute-start.13
  76.0 2.2 %collective-permute-start.14 = (bf16[256,256]{1,0:T(8,128)(2,1)S(1)}, bf16[256,256]{1,0:T(8,128)(2,1)S(1)}, u32[]{:S(2)}, u32[]{:S(2)}) collective-permute-start(bf16[256,256]{1,0:T(8,128)(2,1)S(1)} %get-tuple-element.76), channel_id=1, source_target_pairs={{0,4},{2,6},{4,0},{6,2},{1,5},{3,7},{5,1},{7,3},{8,12},{10,14},{12... | collective-permute-start | bytes 393224 | tf_op jit(solution)/shard_map/ppermute | solution.py:268
  78.7 1.9 collective-permute-done.16
  80.5 1.4 collective-permute-start.17
  81.9 1.2 collective-permute-start.22
  83.1 4.3 %collective-permute-start.23 = (bf16[2,256,256]{2,1,0:T(8,128)(2,1)}, bf16[2,256,256]{2,1,0:T(8,128)(2,1)}, u32[]{:S(2)}, u32[]{:S(2)}) collective-permute-start(bf16[2,256,256]{2,1,0:T(8,128)(2,1)} %get-tuple-element.83), channel_id=1, source_target_pairs={{0,32},{16,48},{32,0},{48,16},{1,33},{17,49},{33,1},{49,17},{2,34}... | collective-permute-start | bytes 786440 | tf_op jit(solution)/shard_map/ppermute | solution.py:377
  87.4 2.2 %collective-permute-start.18 = (bf16[256,256]{1,0:T(8,128)(2,1)S(1)}, bf16[256,256]{1,0:T(8,128)(2,1)}, u32[]{:S(2)}, u32[]{:S(2)}) collective-permute-start(bf16[256,256]{1,0:T(8,128)(2,1)S(1)} %collective-permute-done.16), channel_id=1, source_target_pairs={{0,4},{2,6},{4,0},{6,2},{1,5},{3,7},{5,1},{7,3},{8,12},{10,14},{12... | collective-permute-start | bytes 393224 | tf_op jit(solution)/shard_map/ppermute | solution.py:270
  90.3 4.4 %all-to-all-start = ((bf16[4,3,256,256]{3,2,1,0:T(8,128)(2,1)}), bf16[4,3,256,256]{3,2,1,0:T(8,128)(2,1)}, u32[]{:S(2)}, u32[]{:S(2)}) async-start(bf16[4,3,256,256]{3,2,1,0:T(8,128)(2,1)} %copy-done.9), calls=%async_computation | async-start | bytes 3145728 | tf_op jit(solution)/shard_map/all_to_all | solution.py:380
  94.7 1.1 pad_maximum_fusion.2.a_ref
  95.9 1.1 pad_maximum_fusion.3.b_ref
  97.0 2.1 %pad_maximum_fusion.mine_ref = bf16[4,2,256,256]{3,2,1,0:T(8,128)(2,1)} fusion(bf16[1,2,256,256]{3,2,1,0:T(8,128)(2,1)} %bitcast.22, bf16[1,2,256,256]{3,2,1,0:T(8,128)(2,1)} %bitcast.21, bf16[1,2,256,256]{3,2,1,0:T(8,128)(2,1)S(1)} %bitcast.41, bf16[1,2,256,256]{3,2,1,0:T(8,128)(2,1)S(1)} %bitcast.38), kind=kLoop, calls=%fused_computation | loop fusion | flops 1572864 | bytes 2097152 | tf_op jit(solution)/shard_map/stack | solution.py:378
  99.2 2.8 %copy-done.1 = bf16[3,256,4096]{2,1,0:T(8,128)(2,1)S(1)} copy-done((bf16[3,256,4096]{2,1,0:T(8,128)(2,1)S(1)}, bf16[3,256,4096]{2,1,0:T(8,128)(2,1)}, u32[]{:S(2)}) %copy-start.1) | copy-done | bytes 6291480
  102.0 2.5 %norm_grads_a.1 = bf16[2,4,256,256]{3,2,1,0:T(8,128)(2,1)} custom-call(s32[5]{0:T(128)S(1)} %stack.83.ids, bf16[3,256,4096]{2,1,0:T(8,128)(2,1)S(1)} %copy-done.1, bf16[3,256,256]{2,1,0:T(8,128)(2,1)S(1)} %get-tuple-element.86.g_ref), custom_call_target="tpu_custom_call" | custom-call | flops 805306368 | bytes 3145728 | tf_op jit(solution)/shard_map/norm_grads_a/pallas_call | solution.py:26
  104.5 5.2 %collective-permute-start.25 = (bf16[2,4,256,256]{3,2,1,0:T(8,128)(2,1)}, bf16[2,4,256,256]{3,2,1,0:T(8,128)(2,1)}, u32[]{:S(2)}, u32[]{:S(2)}) collective-permute-start(bf16[2,4,256,256]{3,2,1,0:T(8,128)(2,1)} %norm_grads_a.1), channel_id=1, source_target_pairs={{0,1},{1,0},{2,3},{3,2},{4,5},{5,4},{6,7},{7,6},{8,9},{9,8},{10,11... | collective-permute-start | bytes 3145736 | tf_op jit(solution)/shard_map/ppermute | solution.py:244
  110.2 3.3 %collective-permute-done.20.c_ref = bf16[4,256,256]{2,1,0:T(8,128)(2,1)S(1)} collective-permute-done((bf16[4,256,256]{2,1,0:T(8,128)(2,1)S(1)}, bf16[4,256,256]{2,1,0:T(8,128)(2,1)S(1)}, u32[]{:S(2)}, u32[]{:S(2)}) %collective-permute-start.20) | collective-permute-done | bytes 524320 | tf_op jit(solution)/shard_map/ppermute | solution.py:273
  113.5 1.5 collective-permute-done.21.d_ref
  115.0 2.1 %layer_out.1 = (bf16[256,256]{1,0:T(8,128)(2,1)}, bf16[4,3,256,256]{3,2,1,0:T(8,128)(2,1)S(1)}) custom-call(s32[5]{0:T(128)S(1)} %stack.83.ids, bf16[256,4096]{1,0:T(8,128)(2,1)S(1)} %copy-done.4, bf16[256,256]{1,0:T(8,128)(2,1)S(1)} %copy-done.10, bf16[256,256]{1,0:T(8,128)(2,1)S(1)} %copy-done.6, bf16[4,256,256]{2,1,0:T(8,128)(2,1)S(1)} %pad_maximum_fusion.2.a_ref, ...), custom_call_target="tpu_custom_call" | custom-call | flops 536870912 | bytes 4194304 | tf_op jit(solution)/shard_map/layer_out/pallas_call | solution.py:26
  117.1 1.2 copy-done.8
  118.3 3.9 %in_w.1 = bf16[4,3,256,256]{3,2,1,0:T(8,128)(2,1)S(1)} custom-call(s32[5]{0:T(128)S(1)} %stack.83.ids, bf16[4,2,256,256]{3,2,1,0:T(8,128)(2,1)} %pad_maximum_fusion.mine_ref, bf16[4,2,256,256]{3,2,1,0:T(8,128)(2,1)} %collective-permute-done.26.other_ref, bf16[4,3,256,256]{3,2,1,0:T(8,128)(2,1)} %all-to-all-done.g_ref), custom_call_target="tpu_custom_call" | custom-call | flops 1610612736 | bytes 3145728 | tf_op jit(solution)/shard_map/in_w/pallas_call | solution.py:26
  122.2 1.2 copy-done.7
  123.4 4.5 %all-to-all-start.1 = ((bf16[4,3,256,256]{3,2,1,0:T(8,128)(2,1)}), bf16[4,3,256,256]{3,2,1,0:T(8,128)(2,1)S(1)}, u32[]{:S(2)}, u32[]{:S(2)}) async-start(bf16[4,3,256,256]{3,2,1,0:T(8,128)(2,1)} %copy-done.8), calls=%async_computation.2 | async-start | bytes 3145728 | tf_op jit(solution)/shard_map/all_to_all | solution.py:404
  130.3 2.8 %copy-done.2 = bf16[3,256,4096]{2,1,0:T(8,128)(2,1)S(1)} copy-done((bf16[3,256,4096]{2,1,0:T(8,128)(2,1)S(1)}, bf16[3,256,4096]{2,1,0:T(8,128)(2,1)}, u32[]{:S(2)}) %copy-start.2) | copy-done | bytes 6291480
  133.1 2.3 %norm_grads_b.1 = (bf16[528,256]{1,0:T(8,128)(2,1)S(1)}, bf16[528,256]{1,0:T(8,128)(2,1)S(1)}, bf16[528,256]{1,0:T(8,128)(2,1)S(1)}, bf16[528,256]{1,0:T(8,128)(2,1)S(1)}) custom-call(s32[5]{0:T(128)S(1)} %stack.83.ids, bf16[3,256,4096]{2,1,0:T(8,128)(2,1)S(1)} %copy-done.2, bf16[3,256,256]{2,1,0:T(8,128)(2,1)S(1)} %get-tuple-element.86.g_ref, ...), custom_call_target="tpu_custom_call" | custom-call | flops 805306368 | bytes 3145728 | tf_op jit(solution)/shard_map/norm_grads_b/pallas_call | solution.py:26
  136.4 1.3 collective-permute-start.29
  137.7 2.0 collective-permute-start.30
  139.7 4.5 %tap_grads.1 = f32[16,128]{1,0:T(8,128)S(1)} custom-call(bf16[256,256]{1,0:T(8,128)(2,1)S(1)} %get-tuple-element.62.x_ref, bf16[256,128]{1,0:T(8,128)(2,1)S(1)} %copy-done.12, bf16[256,256]{1,0:T(8,128)(2,1)S(1)} %get-tuple-element.100.g_ref), custom_call_target="tpu_custom_call" | custom-call | flops 33554432 | tf_op jit(solution)/shard_map/tap_grads/pallas_call | solution.py:26
  144.3 1.8 collective-permute-start.32
  146.0 2.4 %collective-permute-start.33 = (f32[4,128]{1,0:T(4,128)S(1)}, f32[4,128]{1,0:T(4,128)S(1)}, u32[]{:S(2)}, u32[]{:S(2)}) collective-permute-start(f32[4,128]{1,0:T(4,128)S(1)} %bitcast.53), channel_id=1, source_target_pairs={{0,32},{16,48},{32,0},{48,16},{1,33},{17,49},{33,1},{49,17},{2,34}... | collective-permute-start | bytes 6152 | tf_op jit(solution)/shard_map/ppermute | solution.py:403
  148.8 1.3 collective-permute-start.34
  150.3 1.4 collective-permute-done.34
  151.9 2.3 %collective-permute-start.38 = (bf16[4,3,256,256]{3,2,1,0:T(8,128)(2,1)S(1)}, bf16[4,3,256,256]{3,2,1,0:T(8,128)(2,1)S(1)}, u32[]{:S(2)}, u32[]{:S(2)}) collective-permute-start(bf16[4,3,256,256]{3,2,1,0:T(8,128)(2,1)S(1)} %all-to-all-done.1.mine_ref.g_ref), channel_id=1, source_target_pairs={{0,1},{1,0},{2,3},{3,2},{4,5},{5,4},{6,7},{7,6},{8,9},{9,8},{10,11... | collective-permute-start | bytes 4718600 | tf_op jit(solution)/shard_map/ppermute | solution.py:405
  154.2 3.0 %collective-permute-done.38.other_ref = bf16[4,3,256,256]{3,2,1,0:T(8,128)(2,1)S(1)} collective-permute-done((bf16[4,3,256,256]{3,2,1,0:T(8,128)(2,1)S(1)}, bf16[4,3,256,256]{3,2,1,0:T(8,128)(2,1)S(1)}, u32[]{:S(2)}, u32[]{:S(2)}) %collective-permute-start.38) | collective-permute-done | bytes 1572896 | tf_op jit(solution)/shard_map/ppermute | solution.py:405
  157.2 2.1 %out_w.1 = bf16[4,1,256,256]{3,2,1,0:T(8,128)(2,1)} custom-call(s32[5]{0:T(128)S(1)} %stack.83.ids, bf16[4,3,256,256]{3,2,1,0:T(8,128)(2,1)S(1)} %all-to-all-done.1.mine_ref.g_ref, bf16[4,3,256,256]{3,2,1,0:T(8,128)(2,1)S(1)} %collective-permute-done.38.other_ref, bf16[4,3,256,256]{3,2,1,0:T(8,128)(2,1)S(1)} %all-to-all-done.1.mine_ref.g_ref), custom_call_target="tpu_custom_call" | custom-call | flops 536870912 | bytes 1048576 | tf_op jit(solution)/shard_map/out_w/pallas_call | solution.py:26
  159.3 6.2 %all-to-all-start.2 = ((bf16[4,256,256]{2,1,0:T(8,128)(2,1)}), bf16[4,256,256]{2,1,0:T(8,128)(2,1)S(1)}, u32[]{:S(2)}, u32[]{:S(2)}) async-start(bf16[4,256,256]{2,1,0:T(8,128)(2,1)} %bitcast.30), calls=%async_computation.3 | async-start | bytes 1048576 | tf_op jit(solution)/shard_map/all_to_all | solution.py:407
  165.5 1.7 collective-permute-start.35
  167.2 1.9 collective-permute-start.36
  169.1 1.2 collective-permute-start.37
  171.2 3.3 %collective-permute-start.31 = (bf16[272,256]{1,0:T(8,128)(2,1)S(1)}, bf16[272,256]{1,0:T(8,128)(2,1)S(1)}, u32[]{:S(2)}, u32[]{:S(2)}) collective-permute-start(bf16[272,256]{1,0:T(8,128)(2,1)S(1)} %get-tuple-element.97), channel_id=1, source_target_pairs={{0,8},{8,0},{1,9},{9,1},{2,10},{10,2},{3,11},{11,3},{4,12},{12,4},... | collective-permute-start | bytes 417800 | tf_op jit(solution)/shard_map/ppermute | solution.py:264
  174.5 9.1 %collective-permute-done.35 = f32[1,128]{1,0:T(1,128)S(1)} collective-permute-done((f32[1,128]{1,0:T(1,128)S(1)}, f32[1,128]{1,0:T(1,128)S(1)}, u32[]{:S(2)}, u32[]{:S(2)}) %collective-permute-start.35) | collective-permute-done | bytes 544 | tf_op jit(solution)/shard_map/ppermute | solution.py:416
  183.7 5.2 %collective-permute-done.36 = f32[1,128]{1,0:T(1,128)S(1)} collective-permute-done((f32[1,128]{1,0:T(1,128)S(1)}, f32[1,128]{1,0:T(1,128)S(1)}, u32[]{:S(2)}, u32[]{:S(2)}) %collective-permute-start.36) | collective-permute-done | bytes 544 | tf_op jit(solution)/shard_map/ppermute | solution.py:416
  190.3 1.9 bitcast_convert_fusion
  (96 shorter events, 15.5 us)
Async XLA Ops:
  7.3 1.6 copy-start.3
  8.9 0.9 copy-start.5
  9.8 4.3 %copy-start.10 = (bf16[256,256]{1,0:T(8,128)(2,1)S(1)}, bf16[256,256]{1,0:T(8,128)(2,1)}, u32[]{:S(2)}) copy-start(bf16[256,256]{1,0:T(8,128)(2,1)} %hid_ref.3) | copy-start | bytes 393220
  9.8 16.9 %copy-start.4 = (bf16[256,4096]{1,0:T(8,128)(2,1)S(1)}, bf16[256,4096]{1,0:T(8,128)(2,1)}, u32[]{:S(2)}) copy-start(bf16[256,4096]{1,0:T(8,128)(2,1)} %w_ref.5) | copy-start | bytes 6291460
  9.8 16.9 %copy-start.6 = (bf16[256,256]{1,0:T(8,128)(2,1)S(1)}, bf16[256,256]{1,0:T(8,128)(2,1)}, u32[]{:S(2)}) copy-start(bf16[256,256]{1,0:T(8,128)(2,1)} %og_ref.3) | copy-start | bytes 393220
  10.8 15.8 %collective-permute-start = (bf16[2,4,256,256]{3,2,1,0:T(8,128)(2,1)S(1)}, bf16[2,4,256,256]{3,2,1,0:T(8,128)(2,1)S(1)}, u32[]{:S(2)}, u32[]{:S(2)}) collective-permute-start(bf16[2,4,256,256]{3,2,1,0:T(8,128)(2,1)S(1)} %mixed_grads_a.1), channel_id=1, source_target_pairs={{0,1},{1,0},{2,3},{3,2},{4,5},{5,4},{6,7},{7,6},{8,9},{9,8},{10,11... | collective-permute-start | bytes 3145736 | tf_op jit(solution)/shard_map/ppermute | solution.py:244
  14.1 9.6 %collective-permute-start.4 = (bf16[256,256]{1,0:T(8,128)(2,1)S(1)}, bf16[256,256]{1,0:T(8,128)(2,1)S(1)}, u32[]{:S(2)}, u32[]{:S(2)}) collective-permute-start(bf16[256,256]{1,0:T(8,128)(2,1)S(1)} %copy-done.10), channel_id=1, source_target_pairs={{0,6},{2,0},{4,2},{6,4},{1,7},{3,1},{5,3},{7,5},{8,14},{10,8},{12,... | collective-permute-start | bytes 393224 | tf_op jit(solution)/shard_map/ppermute | solution.py:337
  15.1 8.7 %collective-permute-start.2 = (bf16[256,256]{1,0:T(8,128)(2,1)S(1)}, bf16[256,256]{1,0:T(8,128)(2,1)S(1)}, u32[]{:S(2)}, u32[]{:S(2)}) collective-permute-start(bf16[256,256]{1,0:T(8,128)(2,1)S(1)} %copy-done.10), channel_id=1, source_target_pairs={{0,2},{2,4},{4,6},{6,0},{1,3},{3,5},{5,7},{7,1},{8,10},{10,12},{12... | collective-permute-start | bytes 393224 | tf_op jit(solution)/shard_map/ppermute | solution.py:337
  15.6 8.3 %collective-permute-start.3 = (bf16[256,256]{1,0:T(8,128)(2,1)S(1)}, bf16[256,256]{1,0:T(8,128)(2,1)S(1)}, u32[]{:S(2)}, u32[]{:S(2)}) collective-permute-start(bf16[256,256]{1,0:T(8,128)(2,1)S(1)} %copy-done.10), channel_id=1, source_target_pairs={{0,4},{2,6},{4,0},{6,2},{1,5},{3,7},{5,1},{7,3},{8,12},{10,14},{12... | collective-permute-start | bytes 393224 | tf_op jit(solution)/shard_map/ppermute | solution.py:337
  16.8 9.8 %collective-permute-start.1 = (bf16[256,256]{1,0:T(8,128)(2,1)S(1)}, bf16[256,256]{1,0:T(8,128)(2,1)S(1)}, u32[]{:S(2)}, u32[]{:S(2)}) collective-permute-start(bf16[256,256]{1,0:T(8,128)(2,1)S(1)} %copy-done.10), channel_id=1, source_target_pairs={{0,8},{8,0},{1,9},{9,1},{2,10},{10,2},{3,11},{11,3},{4,12},{12,4},... | collective-permute-start | bytes 393224 | tf_op jit(solution)/shard_map/ppermute | solution.py:339
  27.6 22.8 %copy-start.20 = (f32[4096]{0:T(1024)S(1)}, f32[4096]{0:T(1024)}, u32[]{:S(2)}) copy-start(f32[4096]{0:T(1024)} %param.7) | copy-start | bytes 49156
  27.7 10.3 %collective-permute-start.5 = (bf16[768,256]{1,0:T(8,128)(2,1)S(1)}, bf16[768,256]{1,0:T(8,128)(2,1)S(1)}, u32[]{:S(2)}, u32[]{:S(2)}) collective-permute-start(bf16[768,256]{1,0:T(8,128)(2,1)S(1)} %get-tuple-element.56), channel_id=1, source_target_pairs={{0,2},{2,4},{4,6},{6,0},{1,3},{3,5},{5,7},{7,1},{8,10},{10,12},{12... | collective-permute-start | bytes 1179656 | tf_op jit(solution)/shard_map/ppermute | solution.py:255
  29.3 17.2 %collective-permute-start.6 = (bf16[768,256]{1,0:T(8,128)(2,1)S(1)}, bf16[768,256]{1,0:T(8,128)(2,1)S(1)}, u32[]{:S(2)}, u32[]{:S(2)}) collective-permute-start(bf16[768,256]{1,0:T(8,128)(2,1)S(1)} %get-tuple-element.57), channel_id=1, source_target_pairs={{0,4},{2,6},{4,0},{6,2},{1,5},{3,7},{5,1},{7,3},{8,12},{10,14},{12... | collective-permute-start | bytes 1179656 | tf_op jit(solution)/shard_map/ppermute | solution.py:255
  30.2 17.7 %collective-permute-start.7 = (bf16[768,256]{1,0:T(8,128)(2,1)S(1)}, bf16[768,256]{1,0:T(8,128)(2,1)S(1)}, u32[]{:S(2)}, u32[]{:S(2)}) collective-permute-start(bf16[768,256]{1,0:T(8,128)(2,1)S(1)} %get-tuple-element.58), channel_id=1, source_target_pairs={{0,6},{2,0},{4,2},{6,4},{1,7},{3,1},{5,3},{7,5},{8,14},{10,8},{12,... | collective-permute-start | bytes 1179656 | tf_op jit(solution)/shard_map/ppermute | solution.py:255
  31.8 23.6 %collective-permute-start.8 = (bf16[4,256,256]{2,1,0:T(8,128)(2,1)S(1)}, bf16[4,256,256]{2,1,0:T(8,128)(2,1)}, u32[]{:S(2)}, u32[]{:S(2)}) collective-permute-start(bf16[4,256,256]{2,1,0:T(8,128)(2,1)S(1)} %pad_maximum_fusion.1.a_ref), channel_id=1, source_target_pairs={{0,1},{1,0},{2,3},{3,2},{4,5},{5,4},{6,7},{7,6},{8,9},{9,8},{10,11... | collective-permute-start | bytes 1572872 | tf_op jit(solution)/shard_map/ppermute | solution.py:338
  48.8 6.5 %collective-permute-start.9 = (bf16[4,256,256]{2,1,0:T(8,128)(2,1)}, bf16[4,256,256]{2,1,0:T(8,128)(2,1)}, u32[]{:S(2)}, u32[]{:S(2)}) collective-permute-start(bf16[4,256,256]{2,1,0:T(8,128)(2,1)} %get-tuple-element.61.b_ref), channel_id=1, source_target_pairs={{0,1},{1,0},{2,3},{3,2},{4,5},{5,4},{6,7},{7,6},{8,9},{9,8},{10,11... | collective-permute-start | bytes 1572872 | tf_op jit(solution)/shard_map/ppermute | solution.py:348
  50.4 14.8 %collective-permute-start.11 = (bf16[256,256]{1,0:T(8,128)(2,1)S(1)}, bf16[256,256]{1,0:T(8,128)(2,1)S(1)}, u32[]{:S(2)}, u32[]{:S(2)}) collective-permute-start(bf16[256,256]{1,0:T(8,128)(2,1)S(1)} %get-tuple-element.64), channel_id=1, source_target_pairs={{0,8},{8,0},{1,9},{9,1},{2,10},{10,2},{3,11},{11,3},{4,12},{12,4},... | collective-permute-start | bytes 393224 | tf_op jit(solution)/shard_map/ppermute | solution.py:264
  55.4 2.8 %copy-start = (bf16[3,256,4096]{2,1,0:T(8,128)(2,1)S(1)}, bf16[3,256,4096]{2,1,0:T(8,128)(2,1)}, u32[]{:S(2)}) copy-start(bf16[3,256,4096]{2,1,0:T(8,128)(2,1)} %w_ref.7) | copy-start | bytes 18874372
  58.2 8.5 %copy-start.15 = (f32[16,128]{1,0:T(8,128)S(1)}, f32[16,128]{1,0:T(8,128)}, u32[]{:S(2)}) copy-start(f32[16,128]{1,0:T(8,128)} %filt_ref) | copy-start | bytes 24580
  62.1 9.5 %copy-start.13 = (bf16[2,256,256]{2,1,0:T(8,128)(2,1)}, bf16[2,256,256]{2,1,0:T(8,128)(2,1)S(1)}, u32[]{:S(2)}) copy-start(bf16[2,256,256]{2,1,0:T(8,128)(2,1)S(1)} %get-tuple-element.79) | copy-start | bytes 786436
  62.1 5.7 %collective-permute-start.10 = (bf16[256,128]{1,0:T(8,128)(2,1)S(1)}, bf16[256,128]{1,0:T(8,128)(2,1)S(1)}, u32[]{:S(2)}, u32[]{:S(2)}) collective-permute-start(bf16[256,128]{1,0:T(8,128)(2,1)S(1)} %get-tuple-element.63), channel_id=1, source_target_pairs={{0,16},{16,32},{32,48},{48,64},{64,80},{80,96},{96,112},{112,128},... | collective-permute-start | bytes 196616 | tf_op jit(solution)/shard_map/ppermute | solution.py:359
  65.4 5.0 %collective-permute-start.12 = (bf16[256,128]{1,0:T(8,128)(2,1)S(1)}, bf16[256,128]{1,0:T(8,128)(2,1)S(1)}, u32[]{:S(2)}, u32[]{:S(2)}) collective-permute-start(bf16[256,128]{1,0:T(8,128)(2,1)S(1)} %get-tuple-element.71), channel_id=1, source_target_pairs={{16,0},{32,16},{48,32},{64,48},{80,64},{96,80},{112,96},{128,112},... | collective-permute-start | bytes 196616 | tf_op jit(solution)/shard_map/ppermute | solution.py:364
  67.8 2.6 %copy-start.11 = (bf16[256,128]{1,0:T(8,128)(2,1)}, bf16[256,128]{1,0:T(8,128)(2,1)S(1)}, u32[]{:S(2)}) copy-start(bf16[256,128]{1,0:T(8,128)(2,1)S(1)} %collective-permute-done.10.halo_ref) | copy-start | bytes 196612
  71.6 1.2 copy-start.9
  72.8 7.7 %collective-permute-start.16 = (bf16[256,256]{1,0:T(8,128)(2,1)S(1)}, bf16[256,256]{1,0:T(8,128)(2,1)S(1)}, u32[]{:S(2)}, u32[]{:S(2)}) collective-permute-start(bf16[256,256]{1,0:T(8,128)(2,1)S(1)} %get-tuple-element.76), channel_id=1, source_target_pairs={{0,8},{8,0},{1,9},{9,1},{2,10},{10,2},{3,11},{11,3},{4,12},{12,4},... | collective-permute-start | bytes 393224 | tf_op jit(solution)/shard_map/ppermute | solution.py:269
  74.6 8.5 %collective-permute-start.13 = (bf16[256,256]{1,0:T(8,128)(2,1)S(1)}, bf16[256,256]{1,0:T(8,128)(2,1)S(1)}, u32[]{:S(2)}, u32[]{:S(2)}) collective-permute-start(bf16[256,256]{1,0:T(8,128)(2,1)S(1)} %get-tuple-element.76), channel_id=1, source_target_pairs={{0,2},{2,4},{4,6},{6,0},{1,3},{3,5},{5,7},{7,1},{8,10},{10,12},{12... | collective-permute-start | bytes 393224 | tf_op jit(solution)/shard_map/ppermute | solution.py:268
  76.0 11.4 %collective-permute-start.14 = (bf16[256,256]{1,0:T(8,128)(2,1)S(1)}, bf16[256,256]{1,0:T(8,128)(2,1)S(1)}, u32[]{:S(2)}, u32[]{:S(2)}) collective-permute-start(bf16[256,256]{1,0:T(8,128)(2,1)S(1)} %get-tuple-element.76), channel_id=1, source_target_pairs={{0,4},{2,6},{4,0},{6,2},{1,5},{3,7},{5,1},{7,3},{8,12},{10,14},{12... | collective-permute-start | bytes 393224 | tf_op jit(solution)/shard_map/ppermute | solution.py:268
  78.1 9.3 %collective-permute-start.15 = (bf16[256,256]{1,0:T(8,128)(2,1)S(1)}, bf16[256,256]{1,0:T(8,128)(2,1)S(1)}, u32[]{:S(2)}, u32[]{:S(2)}) collective-permute-start(bf16[256,256]{1,0:T(8,128)(2,1)S(1)} %get-tuple-element.76), channel_id=1, source_target_pairs={{0,6},{2,0},{4,2},{6,4},{1,7},{3,1},{5,3},{7,5},{8,14},{10,8},{12,... | collective-permute-start | bytes 393224 | tf_op jit(solution)/shard_map/ppermute | solution.py:268
  80.5 9.1 %collective-permute-start.17 = (bf16[256,256]{1,0:T(8,128)(2,1)S(1)}, bf16[256,256]{1,0:T(8,128)(2,1)S(1)}, u32[]{:S(2)}, u32[]{:S(2)}) collective-permute-start(bf16[256,256]{1,0:T(8,128)(2,1)S(1)} %collective-permute-done.16), channel_id=1, source_target_pairs={{0,2},{2,4},{4,6},{6,0},{1,3},{3,5},{5,7},{7,1},{8,10},{10,12},{12... | collective-permute-start | bytes 393224 | tf_op jit(solution)/shard_map/ppermute | solution.py:270
  81.9 15.1 %collective-permute-start.22 = (bf16[2,256,256]{2,1,0:T(8,128)(2,1)}, bf16[2,256,256]{2,1,0:T(8,128)(2,1)S(1)}, u32[]{:S(2)}, u32[]{:S(2)}) collective-permute-start(bf16[2,256,256]{2,1,0:T(8,128)(2,1)} %get-tuple-element.81), channel_id=1, source_target_pairs={{0,16},{16,32},{32,48},{48,0},{1,17},{17,33},{33,49},{49,1},{2,18}... | collective-permute-start | bytes 786440 | tf_op jit(solution)/shard_map/ppermute | solution.py:377
  83.1 6.5 %copy-start.16 = (bf16[256,256]{1,0:T(8,128)(2,1)}, bf16[256,256]{1,0:T(8,128)(2,1)S(1)}, u32[]{:S(2)}) copy-start(bf16[256,256]{1,0:T(8,128)(2,1)S(1)} %collective-permute-done.13) | copy-start | bytes 393220
  83.1 13.9 %collective-permute-start.23 = (bf16[2,256,256]{2,1,0:T(8,128)(2,1)}, bf16[2,256,256]{2,1,0:T(8,128)(2,1)}, u32[]{:S(2)}, u32[]{:S(2)}) collective-permute-start(bf16[2,256,256]{2,1,0:T(8,128)(2,1)} %get-tuple-element.83), channel_id=1, source_target_pairs={{0,32},{16,48},{32,0},{48,16},{1,33},{17,49},{33,1},{49,17},{2,34}... | collective-permute-start | bytes 786440 | tf_op jit(solution)/shard_map/ppermute | solution.py:377
  87.4 2.9 %copy-start.17 = (bf16[256,256]{1,0:T(8,128)(2,1)}, bf16[256,256]{1,0:T(8,128)(2,1)S(1)}, u32[]{:S(2)}) copy-start(bf16[256,256]{1,0:T(8,128)(2,1)S(1)} %collective-permute-done.14) | copy-start | bytes 393220
  87.4 9.6 %collective-permute-start.24 = (bf16[2,256,256]{2,1,0:T(8,128)(2,1)}, bf16[2,256,256]{2,1,0:T(8,128)(2,1)}, u32[]{:S(2)}, u32[]{:S(2)}) collective-permute-start(bf16[2,256,256]{2,1,0:T(8,128)(2,1)} %get-tuple-element.85), channel_id=1, source_target_pairs={{0,48},{16,0},{32,16},{48,32},{1,49},{17,1},{33,17},{49,33},{2,50}... | collective-permute-start | bytes 786440 | tf_op jit(solution)/shard_map/ppermute | solution.py:377
  87.4 2.9 %copy-start.19 = (bf16[256,256]{1,0:T(8,128)(2,1)}, bf16[256,256]{1,0:T(8,128)(2,1)S(1)}, u32[]{:S(2)}) copy-start(bf16[256,256]{1,0:T(8,128)(2,1)S(1)} %collective-permute-done.15) | copy-start | bytes 393220
  87.4 8.4 %collective-permute-start.18 = (bf16[256,256]{1,0:T(8,128)(2,1)S(1)}, bf16[256,256]{1,0:T(8,128)(2,1)}, u32[]{:S(2)}, u32[]{:S(2)}) collective-permute-start(bf16[256,256]{1,0:T(8,128)(2,1)S(1)} %collective-permute-done.16), channel_id=1, source_target_pairs={{0,4},{2,6},{4,0},{6,2},{1,5},{3,7},{5,1},{7,3},{8,12},{10,14},{12... | collective-permute-start | bytes 393224 | tf_op jit(solution)/shard_map/ppermute | solution.py:270
  89.7 0.7 copy-start.18
  89.7 6.2 %collective-permute-start.19 = (bf16[256,256]{1,0:T(8,128)(2,1)S(1)}, bf16[256,256]{1,0:T(8,128)(2,1)}, u32[]{:S(2)}, u32[]{:S(2)}) collective-permute-start(bf16[256,256]{1,0:T(8,128)(2,1)S(1)} %collective-permute-done.16), channel_id=1, source_target_pairs={{0,6},{2,0},{4,2},{6,4},{1,7},{3,1},{5,3},{7,5},{8,14},{10,8},{12,... | collective-permute-start | bytes 393224 | tf_op jit(solution)/shard_map/ppermute | solution.py:270
  90.3 28.0 %all-to-all-start = ((bf16[4,3,256,256]{3,2,1,0:T(8,128)(2,1)}), bf16[4,3,256,256]{3,2,1,0:T(8,128)(2,1)}, u32[]{:S(2)}, u32[]{:S(2)}) async-start(bf16[4,3,256,256]{3,2,1,0:T(8,128)(2,1)} %copy-done.9), calls=%async_computation | async-start | bytes 3145728 | tf_op jit(solution)/shard_map/all_to_all | solution.py:380
  94.7 2.3 %copy-start.14 = (bf16[2,256,256]{2,1,0:T(8,128)(2,1)S(1)}, bf16[2,256,256]{2,1,0:T(8,128)(2,1)}, u32[]{:S(2)}) copy-start(bf16[2,256,256]{2,1,0:T(8,128)(2,1)} %copy-done.13) | copy-start | bytes 786436
  99.2 2.8 %copy-start.1 = (bf16[3,256,4096]{2,1,0:T(8,128)(2,1)S(1)}, bf16[3,256,4096]{2,1,0:T(8,128)(2,1)}, u32[]{:S(2)}) copy-start(bf16[3,256,4096]{2,1,0:T(8,128)(2,1)} %w_ref.7) | copy-start | bytes 18874372
  104.5 13.8 %collective-permute-start.25 = (bf16[2,4,256,256]{3,2,1,0:T(8,128)(2,1)}, bf16[2,4,256,256]{3,2,1,0:T(8,128)(2,1)}, u32[]{:S(2)}, u32[]{:S(2)}) collective-permute-start(bf16[2,4,256,256]{3,2,1,0:T(8,128)(2,1)} %norm_grads_a.1), channel_id=1, source_target_pairs={{0,1},{1,0},{2,3},{3,2},{4,5},{5,4},{6,7},{7,6},{8,9},{9,8},{10,11... | collective-permute-start | bytes 3145736 | tf_op jit(solution)/shard_map/ppermute | solution.py:244
  109.7 8.6 %collective-permute-start.26 = (bf16[4,2,256,256]{3,2,1,0:T(8,128)(2,1)}, bf16[4,2,256,256]{3,2,1,0:T(8,128)(2,1)}, u32[]{:S(2)}, u32[]{:S(2)}) collective-permute-start(bf16[4,2,256,256]{3,2,1,0:T(8,128)(2,1)} %pad_maximum_fusion.mine_ref), channel_id=1, source_target_pairs={{0,1},{1,0},{2,3},{3,2},{4,5},{5,4},{6,7},{7,6},{8,9},{9,8},{10,11... | collective-permute-start | bytes 3145736 | tf_op jit(solution)/shard_map/ppermute | solution.py:379
  109.7 3.8 %collective-permute-start.20 = (bf16[4,256,256]{2,1,0:T(8,128)(2,1)S(1)}, bf16[4,256,256]{2,1,0:T(8,128)(2,1)S(1)}, u32[]{:S(2)}, u32[]{:S(2)}) collective-permute-start(bf16[4,256,256]{2,1,0:T(8,128)(2,1)S(1)} %pad_maximum_fusion.2.a_ref), channel_id=1, source_target_pairs={{0,1},{1,0},{2,3},{3,2},{4,5},{5,4},{6,7},{7,6},{8,9},{9,8},{10,11... | collective-permute-start | bytes 1572872 | tf_op jit(solution)/shard_map/ppermute | solution.py:273
  110.2 4.8 %collective-permute-start.21 = (bf16[4,256,256]{2,1,0:T(8,128)(2,1)S(1)}, bf16[4,256,256]{2,1,0:T(8,128)(2,1)S(1)}, u32[]{:S(2)}, u32[]{:S(2)}) collective-permute-start(bf16[4,256,256]{2,1,0:T(8,128)(2,1)S(1)} %pad_maximum_fusion.3.b_ref), channel_id=1, source_target_pairs={{0,1},{1,0},{2,3},{3,2},{4,5},{5,4},{6,7},{7,6},{8,9},{9,8},{10,11... | collective-permute-start | bytes 1572872 | tf_op jit(solution)/shard_map/ppermute | solution.py:273
  117.1 1.2 copy-start.8
  122.2 1.2 copy-start.7
  123.4 28.5 %all-to-all-start.1 = ((bf16[4,3,256,256]{3,2,1,0:T(8,128)(2,1)}), bf16[4,3,256,256]{3,2,1,0:T(8,128)(2,1)S(1)}, u32[]{:S(2)}, u32[]{:S(2)}) async-start(bf16[4,3,256,256]{3,2,1,0:T(8,128)(2,1)} %copy-done.8), calls=%async_computation.2 | async-start | bytes 3145728 | tf_op jit(solution)/shard_map/all_to_all | solution.py:404
  127.8 62.4 %reduce-scatter.2.cloned.1.call-start = ((), (), s32[]{:S(2)}) async-start(), calls=%async_computation.4 | async-start | bytes 1966080 | tf_op jit(solution)/shard_map/reduce_scatter | solution.py:391
  128.6 1.8 collective-permute-start.27
  130.3 2.8 %copy-start.2 = (bf16[3,256,4096]{2,1,0:T(8,128)(2,1)S(1)}, bf16[3,256,4096]{2,1,0:T(8,128)(2,1)}, u32[]{:S(2)}) copy-start(bf16[3,256,4096]{2,1,0:T(8,128)(2,1)} %w_ref.7) | copy-start | bytes 18874372
  133.1 6.6 %copy-start.12 = (bf16[256,128]{1,0:T(8,128)(2,1)S(1)}, bf16[256,128]{1,0:T(8,128)(2,1)}, u32[]{:S(2)}) copy-start(bf16[256,128]{1,0:T(8,128)(2,1)} %copy-done.11) | copy-start | bytes 196612
  135.5 16.2 %collective-permute-start.28 = (bf16[528,256]{1,0:T(8,128)(2,1)S(1)}, bf16[528,256]{1,0:T(8,128)(2,1)S(1)}, u32[]{:S(2)}, u32[]{:S(2)}) collective-permute-start(bf16[528,256]{1,0:T(8,128)(2,1)S(1)} %get-tuple-element.93), channel_id=1, source_target_pairs={{0,2},{2,4},{4,6},{6,0},{1,3},{3,5},{5,7},{7,1},{8,10},{10,12},{12... | collective-permute-start | bytes 811016 | tf_op jit(solution)/shard_map/ppermute | solution.py:255
  136.4 15.3 %collective-permute-start.29 = (bf16[528,256]{1,0:T(8,128)(2,1)S(1)}, bf16[528,256]{1,0:T(8,128)(2,1)S(1)}, u32[]{:S(2)}, u32[]{:S(2)}) collective-permute-start(bf16[528,256]{1,0:T(8,128)(2,1)S(1)} %get-tuple-element.94), channel_id=1, source_target_pairs={{0,4},{2,6},{4,0},{6,2},{1,5},{3,7},{5,1},{7,3},{8,12},{10,14},{12... | collective-permute-start | bytes 811016 | tf_op jit(solution)/shard_map/ppermute | solution.py:255
  137.7 14.0 %collective-permute-start.30 = (bf16[528,256]{1,0:T(8,128)(2,1)S(1)}, bf16[528,256]{1,0:T(8,128)(2,1)S(1)}, u32[]{:S(2)}, u32[]{:S(2)}) collective-permute-start(bf16[528,256]{1,0:T(8,128)(2,1)S(1)} %get-tuple-element.95), channel_id=1, source_target_pairs={{0,6},{2,0},{4,2},{6,4},{1,7},{3,1},{5,3},{7,5},{8,14},{10,8},{12,... | collective-permute-start | bytes 811016 | tf_op jit(solution)/shard_map/ppermute | solution.py:255
  144.3 4.6 %collective-permute-start.32 = (f32[4,128]{1,0:T(4,128)S(1)}, f32[4,128]{1,0:T(4,128)S(1)}, u32[]{:S(2)}, u32[]{:S(2)}) collective-permute-start(f32[4,128]{1,0:T(4,128)S(1)} %bitcast.54), channel_id=1, source_target_pairs={{0,16},{16,32},{32,48},{48,0},{1,17},{17,33},{33,49},{49,1},{2,18}... | collective-permute-start | bytes 6152 | tf_op jit(solution)/shard_map/ppermute | solution.py:403
  146.0 4.3 %collective-permute-start.33 = (f32[4,128]{1,0:T(4,128)S(1)}, f32[4,128]{1,0:T(4,128)S(1)}, u32[]{:S(2)}, u32[]{:S(2)}) collective-permute-start(f32[4,128]{1,0:T(4,128)S(1)} %bitcast.53), channel_id=1, source_target_pairs={{0,32},{16,48},{32,0},{48,16},{1,33},{17,49},{33,1},{49,17},{2,34}... | collective-permute-start | bytes 6152 | tf_op jit(solution)/shard_map/ppermute | solution.py:403
  148.8 2.8 %collective-permute-start.34 = (f32[4,128]{1,0:T(4,128)S(1)}, f32[4,128]{1,0:T(4,128)S(1)}, u32[]{:S(2)}, u32[]{:S(2)}) collective-permute-start(f32[4,128]{1,0:T(4,128)S(1)} %bitcast.52), channel_id=1, source_target_pairs={{0,48},{16,0},{32,16},{48,32},{1,49},{17,1},{33,17},{49,33},{2,50}... | collective-permute-start | bytes 6152 | tf_op jit(solution)/shard_map/ppermute | solution.py:403
  151.9 5.3 %collective-permute-start.38 = (bf16[4,3,256,256]{3,2,1,0:T(8,128)(2,1)S(1)}, bf16[4,3,256,256]{3,2,1,0:T(8,128)(2,1)S(1)}, u32[]{:S(2)}, u32[]{:S(2)}) collective-permute-start(bf16[4,3,256,256]{3,2,1,0:T(8,128)(2,1)S(1)} %all-to-all-done.1.mine_ref.g_ref), channel_id=1, source_target_pairs={{0,1},{1,0},{2,3},{3,2},{4,5},{5,4},{6,7},{7,6},{8,9},{9,8},{10,11... | collective-permute-start | bytes 4718600 | tf_op jit(solution)/shard_map/ppermute | solution.py:405
  159.3 32.9 %all-to-all-start.2 = ((bf16[4,256,256]{2,1,0:T(8,128)(2,1)}), bf16[4,256,256]{2,1,0:T(8,128)(2,1)S(1)}, u32[]{:S(2)}, u32[]{:S(2)}) async-start(bf16[4,256,256]{2,1,0:T(8,128)(2,1)} %bitcast.30), calls=%async_computation.3 | async-start | bytes 1048576 | tf_op jit(solution)/shard_map/all_to_all | solution.py:407
  165.5 18.2 %collective-permute-start.35 = (f32[1,128]{1,0:T(1,128)S(1)}, f32[1,128]{1,0:T(1,128)S(1)}, u32[]{:S(2)}, u32[]{:S(2)}) collective-permute-start(f32[1,128]{1,0:T(1,128)S(1)} %get-tuple-element.109), channel_id=1, source_target_pairs={{0,64},{64,128},{128,192},{192,0},{1,65},{65,129},{129,193},{193,1... | collective-permute-start | bytes 1544 | tf_op jit(solution)/shard_map/ppermute | solution.py:416
  167.2 21.6 %collective-permute-start.36 = (f32[1,128]{1,0:T(1,128)S(1)}, f32[1,128]{1,0:T(1,128)S(1)}, u32[]{:S(2)}, u32[]{:S(2)}) collective-permute-start(f32[1,128]{1,0:T(1,128)S(1)} %get-tuple-element.107), channel_id=1, source_target_pairs={{0,128},{64,192},{128,0},{192,64},{1,129},{65,193},{129,1},{193,65... | collective-permute-start | bytes 1544 | tf_op jit(solution)/shard_map/ppermute | solution.py:416
  169.1 19.7 %collective-permute-start.37 = (f32[1,128]{1,0:T(1,128)S(1)}, f32[1,128]{1,0:T(1,128)S(1)}, u32[]{:S(2)}, u32[]{:S(2)}) collective-permute-start(f32[1,128]{1,0:T(1,128)S(1)} %get-tuple-element.108), channel_id=1, source_target_pairs={{0,192},{64,0},{128,64},{192,128},{1,193},{65,1},{129,65},{193,129... | collective-permute-start | bytes 1544 | tf_op jit(solution)/shard_map/ppermute | solution.py:416
  171.2 18.2 %collective-permute-start.31 = (bf16[272,256]{1,0:T(8,128)(2,1)S(1)}, bf16[272,256]{1,0:T(8,128)(2,1)S(1)}, u32[]{:S(2)}, u32[]{:S(2)}) collective-permute-start(bf16[272,256]{1,0:T(8,128)(2,1)S(1)} %get-tuple-element.97), channel_id=1, source_target_pairs={{0,8},{8,0},{1,9},{9,1},{2,10},{10,2},{3,11},{11,3},{4,12},{12,4},... | collective-permute-start | bytes 417800 | tf_op jit(solution)/shard_map/ppermute | solution.py:264
Sparse Core Ops, SparseCore 0:
  131.2 42.0 reduce-scatter.1
